TPU v7x, 128 devices: a whole 4x4x4 slice. The times are simulated.
128 devices in a mesh: seq: 32 (over y_lo, x, z), row: 4 (over y_hi, core).
Axes of the slice: x: 4, y: 4 (y_hi: 2, y_lo: 2; y = y_hi * 2 + y_lo), z: 4, core: 2. Of those that a mesh axis runs over, the one named last changes fastest.
Arguments:
- frames: bfloat16 [4, 6144, 1024], P('row', 'seq'), may hold values from -6 to 6
- segment_ids: int32 [4, 6144], P('row', 'seq'), may hold values from 0 to 4, as said below
- norm1_gain: float32 [1024], replicated, may hold values from 0.1 to 1.9
- w_qkv: bfloat16 [1024, 3072], replicated, may hold values from -0.1875 to 0.1875
- w_out: bfloat16 [1024, 1024], replicated, may hold values from -1.5 to 1.5
- norm2_gain: float32 [1024], replicated, may hold values from 0.1 to 1.9
- w_up: bfloat16 [1024, 4096], replicated, may hold values from -0.1875 to 0.1875
- w_down: bfloat16 [4096, 1024], replicated, may hold values from -0.09375 to 0.09375
- out_grad: bfloat16 [4, 6144, 1024], P('row', 'seq'), may hold values from -6 to 6
Outputs:
- block_out: bfloat16 [4, 6144, 1024], P('row', 'seq')
- frames_grad: bfloat16 [4, 6144, 1024], P('row', 'seq')
- norm1_grad: float32 [1024], P(('seq', 'row'))
- qkv_grad: float32 [1024, 3072], P(('seq', 'row'))
- out_w_grad: float32 [1024, 1024], P(('seq', 'row'))
- norm2_grad: float32 [1024], P(('seq', 'row'))
- up_grad: float32 [1024, 4096], P(('seq', 'row'))
- down_grad: float32 [4096, 1024], P(('seq', 'row'))
Inputs may be any that keep to these rules, and one draw needn't show every extreme that they name: `segment_ids`: along each row the numbers never fall; each row holds five documents, and one of them begins within the row's first 192 frames and ends within its last 192.
All inputs are finite; a program needn't handle non-finite values.
Results may differ from a plain program's by a relative error of at most 0.025.
Values may be sent and summed in bfloat16 or wider, within the bound.
A program may use at most 192 MiB of HBM per device.

v0:
```python
import jax
import jax.numpy as jnp
from jax import lax
from jax.sharding import PartitionSpec as P

H = 16
HD = 64


epsilon = 1e-05


def from_behind(block, axis, distance):
    devices = range(lax.axis_size(axis))
    route = [((i - distance) % len(devices), i) for i in devices]
    return lax.ppermute(block, axis, route)


def shifted(value, axis, steps):
    count = lax.axis_size(axis)
    leading, last = (max(0, -steps), min(count, count - steps))
    return lax.ppermute(value, axis, [(source, source + steps) for source in range(leading, last)])


def rms_scale(value, gain):
    return value * lax.rsqrt(jnp.mean(value * value, axis=-1, keepdims=True) + epsilon) * gain


def pass_grads(key_acc, value_acc):
    return (
        from_behind(key_acc.astype(jnp.bfloat16), "seq", 1).astype(key_acc.dtype),
        from_behind(value_acc.astype(jnp.bfloat16), "seq", 1).astype(value_acc.dtype),
    )


def shards(frames, segment_ids, norm1_gain, w_qkv, w_out, norm2_gain, w_up, w_down, out_grad):
    f32 = jnp.float32
    bf16 = jnp.bfloat16
    count = frames.shape[1]
    width = frames.shape[2]
    cycle = lax.axis_size("seq")
    me = lax.axis_index("seq")
    scale = HD ** (-0.5)
    xf = frames[0].astype(f32)
    seg_own = segment_ids[0].astype(bf16)
    h1, norm1_pull = jax.vjp(rms_scale, xf, norm1_gain)
    act_in = h1.astype(bf16)
    qkv = jnp.dot(act_in, w_qkv, preferred_element_type=f32).astype(bf16)
    queries = qkv[:, :width].reshape(count, H, HD)
    keys_own = qkv[:, width : 2 * width]
    values_own = qkv[:, 2 * width :]
    pos_q = me * count + jnp.arange(count, dtype=jnp.int32)

    def block_scores(key_block, key_seg, source):
        heads_k = key_block.reshape(count, H, HD)
        scores = jnp.einsum("qhd,khd->hqk", queries, heads_k, preferred_element_type=f32) * scale
        pos_k = source * count + jnp.arange(count, dtype=jnp.int32)
        allowed = (seg_own[:, None] == key_seg[None, :]) & (pos_k[None, :] <= pos_q[:, None])
        return (scores, allowed[None])

    def absorb(state, key_block, value_block, key_seg, source):
        running, total, accum = state
        scores, allowed = block_scores(key_block, key_seg, source)
        top = jnp.maximum(running, jnp.max(jnp.where(allowed, scores, -1e30), axis=-1))
        weights = jnp.where(allowed, jnp.exp(scores - top[..., None]), 0.0)
        fade = jnp.exp(running - top)
        total = total * fade + jnp.sum(weights, axis=-1)
        heads_v = value_block.reshape(count, H, HD)
        accum = accum * fade[..., None] + jnp.einsum(
            "hqk,khd->hqd", weights.astype(bf16), heads_v, preferred_element_type=f32
        )
        return (top, total, accum)

    start_state = (
        jnp.full((H, count), -1e30, f32),
        jnp.zeros((H, count), f32),
        jnp.zeros((H, count, HD), f32),
    )
    state = absorb(start_state, keys_own, values_own, seg_own, me)
    stored = ()

    def forward_step(step, carry):
        state, key_block, value_block, key_seg, stored = carry
        key_block, value_block, key_seg = shifted((key_block, value_block, key_seg), "seq", 1)
        source = (me - step) % cycle
        state = absorb(state, key_block, value_block, key_seg, source)
        return (state, key_block, value_block, key_seg, stored)

    state, _, _, _, stored = lax.fori_loop(
        1, cycle, forward_step, (state, keys_own, values_own, seg_own, stored)
    )
    running, total, accum = state
    lse = running + jnp.log(total)
    attn_heads = accum / total[..., None]
    attn = jnp.transpose(attn_heads, (1, 0, 2)).reshape(count, width)
    attn_low = attn.astype(bf16)
    x1 = xf + jnp.dot(attn_low, w_out, preferred_element_type=f32)
    h2, norm2_pull = jax.vjp(rms_scale, x1, norm2_gain)
    act_mid = h2.astype(bf16)
    hidden = jnp.dot(act_mid, w_up, preferred_element_type=f32)
    gelu_out, gelu_pull = jax.vjp(jax.nn.gelu, hidden)
    gelu_low = gelu_out.astype(bf16)
    result = x1 + jnp.dot(gelu_low, w_down, preferred_element_type=f32)
    grad_y = out_grad[0].astype(f32)
    grad_m = grad_y.astype(bf16)
    down_part = jnp.einsum("fk,fd->kd", gelu_low, grad_m, preferred_element_type=f32)
    grad_g = jnp.einsum("fd,kd->fk", grad_m, w_down, preferred_element_type=f32)
    grad_z = gelu_pull(grad_g)[0].astype(bf16)
    up_part = jnp.einsum("fd,fk->dk", act_mid, grad_z, preferred_element_type=f32)
    grad_h2 = jnp.einsum("fk,dk->fd", grad_z, w_up, preferred_element_type=f32)
    grad_x1_part, gain2_part = norm2_pull(grad_h2)
    grad_x1 = grad_y + grad_x1_part
    grad_a = grad_x1.astype(bf16)
    out_part = jnp.einsum("fa,fd->ad", attn_low, grad_a, preferred_element_type=f32)
    grad_attn = jnp.einsum("fd,ad->fa", grad_a, w_out, preferred_element_type=f32).astype(bf16)
    grad_heads = grad_attn.reshape(count, H, HD)
    delta = jnp.einsum("qhd,hqd->hq", grad_heads.astype(f32), attn_heads)

    def release(grads, key_block, value_block, key_seg, source):
        grad_q, key_acc, value_acc = grads
        scores, allowed = block_scores(key_block, key_seg, source)
        probs = jnp.where(allowed, jnp.exp(scores - lse[..., None]), 0.0)
        heads_k = key_block.reshape(count, H, HD)
        heads_v = value_block.reshape(count, H, HD)
        grad_p = jnp.einsum("qhd,khd->hqk", grad_heads, heads_v, preferred_element_type=f32)
        grad_s = (probs * (grad_p - delta[..., None])).astype(bf16)
        grad_q = (
            grad_q + jnp.einsum("hqk,khd->qhd", grad_s, heads_k, preferred_element_type=f32) * scale
        )
        key_acc = (
            key_acc
            + jnp.einsum("hqk,qhd->khd", grad_s, queries, preferred_element_type=f32) * scale
        )
        value_acc = value_acc + jnp.einsum(
            "hqk,qhd->khd", probs.astype(bf16), grad_heads, preferred_element_type=f32
        )
        return (grad_q, key_acc, value_acc)

    def fetch(key_block, value_block, key_seg):
        return (key_block, value_block, key_seg)

    def backward_step(step, carry):
        grad_q, key_block, value_block, key_seg, key_acc, value_acc = carry
        source = (me - step) % cycle
        used = fetch(key_block, value_block, key_seg)
        grad_q, key_acc, value_acc = release(
            (grad_q, key_acc, value_acc), used[0], used[1], used[2], source
        )
        key_acc, value_acc = pass_grads(key_acc, value_acc)
        key_block, value_block, key_seg = shifted((key_block, value_block, key_seg), "seq", 1)
        return (grad_q, key_block, value_block, key_seg, key_acc, value_acc)

    zeros_heads = jnp.zeros((count, H, HD), f32)
    carry = lax.fori_loop(
        0,
        cycle - 1,
        backward_step,
        (zeros_heads, keys_own, values_own, seg_own, zeros_heads, zeros_heads),
    )
    grad_q, key_block, value_block, key_seg, key_acc, value_acc = carry
    last = cycle - 1
    used = fetch(key_block, value_block, key_seg)
    grad_q, key_acc, value_acc = release(
        (grad_q, key_acc, value_acc), used[0], used[1], used[2], (me - last) % cycle
    )
    key_acc, value_acc = pass_grads(key_acc, value_acc)
    grad_qkv = jnp.concatenate(
        [
            grad_q.reshape(count, width).astype(bf16),
            key_acc.reshape(count, width).astype(bf16),
            value_acc.reshape(count, width).astype(bf16),
        ],
        axis=-1,
    )
    qkv_part = jnp.einsum("fd,fe->de", act_in, grad_qkv, preferred_element_type=f32)
    grad_h1 = jnp.einsum("fe,de->fd", grad_qkv, w_qkv, preferred_element_type=f32)
    grad_x_part, gain1_part = norm1_pull(grad_h1)
    grad_x = grad_x1 + grad_x_part
    summed = (
        lax.psum_scatter(gain1_part, ("seq", "row"), scatter_dimension=0, tiled=True),
        lax.psum_scatter(qkv_part, ("seq", "row"), scatter_dimension=0, tiled=True),
        lax.psum_scatter(out_part, ("seq", "row"), scatter_dimension=0, tiled=True),
        lax.psum_scatter(gain2_part, ("seq", "row"), scatter_dimension=0, tiled=True),
        lax.psum_scatter(up_part, ("seq", "row"), scatter_dimension=0, tiled=True),
        lax.psum_scatter(down_part, ("seq", "row"), scatter_dimension=0, tiled=True),
    )
    gain1_sum, qkv_sum, out_sum, gain2_sum, up_sum, down_sum = summed
    return (
        result[None].astype(bf16),
        grad_x[None].astype(bf16),
        gain1_sum,
        qkv_sum,
        out_sum,
        gain2_sum,
        up_sum,
        down_sum,
    )


def solution(mesh):
    return jax.shard_map(
        shards,
        mesh=mesh,
        in_specs=(
            P("row", "seq", None),
            P("row", "seq"),
            P(),
            P(),
            P(),
            P(),
            P(),
            P(),
            P("row", "seq", None),
        ),
        out_specs=(
            P("row", "seq", None),
            P("row", "seq", None),
            P(("seq", "row")),
            P(("seq", "row"), None),
            P(("seq", "row"), None),
            P(("seq", "row")),
            P(("seq", "row"), None),
            P(("seq", "row"), None),
        ),
        check_vma=False,
    )
```

profile of v0, /device:TPU:1, one launch (start us, length us, event | category | flops | bytes accessed | tf_op | source)
XLA Modules:
  0.0 4671.1 jit_solution(18069443172983879203)
XLA Ops:
  26.1 859.4 %while.52 = (s32[]{:T(128)}, f32[16,192]{1,0:T(8,128)S(1)}, f32[16,192]{1,0:T(8,128)}, f32[16,192,64]{1,2,0:T(8,128)}, bf16[192,1024]{0,1:T(8,128)(2,1)}, /*inde...) while((s32[]{:T(128)}, f32[16,192]{1,0:T(8,128)S(1)}, ...), condition=%wide.region_6.7_spmd.clone, body=%wide.region_3.6_spmd.clone.sunk | while | flops 158067088 | bytes 21289480 | solution.py:89
  893.2 8.9 fusion.46
  918.8 1667.9 %while.53 = (s32[]{:T(128)}, f32[192,16,64]{0,2,1:T(8,128)}, bf16[192,1024]{0,1:T(8,128)(2,1)S(1)}, bf16[192,1024]{0,1:T(8,128)(2,1)}, bf16[192]{0:T(256)(128)(2...) while((s32[]{:T(128)}, f32[192,16,64]{0,2,1:T(8,128)}, ...), condition=%wide.region_10.11_spmd.clone, body=%wide.region_9.10_spmd.clone.sunk | while | flops 385929600 | bytes 34072244 | solution.py:154
  999.0 11.0 collective-permute-done.5
  1051.6 12.7 collective-permute-done.5
  1084.0 10.0 collective-permute-start.4
  1106.0 12.9 collective-permute-done.5
  1162.4 12.1 collective-permute-done.5
  1199.0 8.4 collective-permute-start.4
  1220.4 12.0 collective-permute-done.5
  1250.0 8.4 collective-permute-start.3
  1280.0 8.8 collective-permute-done.5
  1317.3 8.8 collective-permute-start.4
  1376.7 8.4 collective-permute-start.4
  1398.7 8.4 collective-permute-done.5
  1433.9 8.3 collective-permute-start.4
  1454.8 8.6 collective-permute-done.5
  1509.8 9.0 collective-permute-done.5
  1564.3 9.2 collective-permute-done.5
  1618.4 9.7 collective-permute-done.5
  1671.6 10.8 collective-permute-done.5
  1724.8 11.3 collective-permute-done.5
  1765.9 8.6 collective-permute-start.5
  1806.9 9.2 collective-permute-start.3
  1816.0 10.2 collective-permute-start.4
  1826.2 8.2 collective-permute-start.5
  1866.9 8.8 collective-permute-start.3
  1875.7 9.4 collective-permute-start.4
  1908.4 8.5 collective-permute-start.6
  1933.7 9.1 collective-permute-start.4
  1991.3 8.8 collective-permute-start.4
  2120.9 11.0 collective-permute-done.5
  2155.8 8.2 collective-permute-start.4
  2176.6 9.0 collective-permute-done.5
  2229.2 10.5 collective-permute-done.5
  2281.3 12.7 collective-permute-done.5
  2331.7 15.2 collective-permute-done.5
  2382.4 15.8 collective-permute-done.5
  2431.9 15.1 collective-permute-done.5
  2480.3 14.1 collective-permute-done.5
  2531.3 9.4 collective-permute-done.5
  2599.0 15.3 collective-permute-done.8
  2628.5 10.1 fusion.96
  2640.2 8.2 fusion.116
  2662.0 108.7 %all-reduce.2 = (f32[1024]{0:T(1024)S(1)}, f32[1024]{0:T(1024)S(1)}) all-reduce(f32[1024]{0:T(1024)S(1)} %get-tuple-element.770, f32[1024]{0:T(1024)S(1)} %copy-done.49), channel_id=2, replica_groups=mesh['seq'=32,'row'=4] {'seq','row'}, use_global_device_ids=true, to_apply=%region_13.14.clone | all-reduce | flops 2048 | bytes 16384
  2774.0 560.3 %reduce-scatter.5.cloned.1.call-done = f32[8,3072]{1,0:T(8,128)} async-done(((f32[1024,3072]{1,0:T(8,128)}), f32[8,3072]{1,0:T(8,128)}) %reduce-scatter.5.cloned.1.call-update) | async-done | bytes 98320 | tf_op jit(solution)/shard_map/reduce_scatter | solution.py:181
  3334.3 665.7 %reduce-scatter.11.cloned.1.call-done = f32[32,1024]{1,0:T(8,128)} async-done(((f32[4096,1024]{1,0:T(8,128)}), f32[32,1024]{1,0:T(8,128)}) %reduce-scatter.11.cloned.1.call-update) | async-done | bytes 131088 | tf_op jit(solution)/shard_map/reduce_scatter | solution.py:185
  4000.0 664.2 %reduce-scatter.9.cloned.1.call-done = f32[8,4096]{1,0:T(8,128)} async-done(((f32[1024,4096]{1,0:T(8,128)}), f32[8,4096]{1,0:T(8,128)}) %reduce-scatter.9.cloned.1.call-update) | async-done | bytes 131088 | tf_op jit(solution)/shard_map/reduce_scatter | solution.py:184
  (1968 shorter events, 2216.4 us)
Async XLA Ops:
  7.2 2766.8 %reduce-scatter.7.cloned.1.call-start = ((), (), s32[]{:S(2)}) async-start(), calls=%async_computation.5 | async-start | bytes 4227072 | tf_op jit(solution)/shard_map/reduce_scatter | solution.py:182
  909.8 2424.5 %reduce-scatter.5.cloned.1.call-start = ((), (), s32[]{:S(2)}) async-start(), calls=%async_computation.4 | async-start | bytes 12681216 | tf_op jit(solution)/shard_map/reduce_scatter | solution.py:181
  973.5 36.5 collective-permute-start.3
  1024.6 39.6 collective-permute-start.3
  1030.2 34.1 collective-permute-start.4
  1077.4 41.5 collective-permute-start.3
  1084.0 34.8 collective-permute-start.4
  1135.1 39.3 collective-permute-start.3
  1182.4 33.7 collective-permute-start.6
  1192.7 39.7 collective-permute-start.3
  1240.4 35.3 collective-permute-start.6
  1250.0 38.8 collective-permute-start.3
  1296.8 39.7 collective-permute-start.6
  1303.8 34.8 collective-permute-start.7
  1311.1 35.9 collective-permute-start.3
  1355.0 39.5 collective-permute-start.6
  1369.3 37.8 collective-permute-start.3
  1415.0 35.5 collective-permute-start.6
  1427.5 35.9 collective-permute-start.3
  1471.4 34.1 collective-permute-start.6
  1483.7 35.1 collective-permute-start.3
  1538.4 35.0 collective-permute-start.3
  1592.8 35.3 collective-permute-start.3
  1647.2 35.2 collective-permute-start.3
  1700.8 35.3 collective-permute-start.3
  1753.9 35.1 collective-permute-start.3
  1797.0 40.3 collective-permute-start.6
  1802.8 36.6 collective-permute-start.7
  1806.9 34.9 collective-permute-start.3
  1849.8 45.3 collective-permute-start.6
  1859.0 38.1 collective-permute-start.7
  1908.4 44.2 collective-permute-start.6
  1919.5 35.2 collective-permute-start.7
  1925.7 35.1 collective-permute-start.3
  1968.7 41.0 collective-permute-start.6
  1977.0 34.8 collective-permute-start.7
  1983.4 34.9 collective-permute-start.3
  2026.3 37.6 collective-permute-start.6
  2041.1 34.9 collective-permute-start.3
  2097.2 34.6 collective-permute-start.3
  2151.0 34.6 collective-permute-start.3
  2205.1 34.7 collective-permute-start.3
  2259.1 34.9 collective-permute-start.3
  2312.3 34.7 collective-permute-start.3
  2363.8 34.4 collective-permute-start.3
  2413.4 33.6 collective-permute-start.3
  2627.5 1372.5 %reduce-scatter.11.cloned.1.call-start = ((), (), s32[]{:S(2)}) async-start(), calls=%async_computation.7 | async-start | bytes 16908288 | tf_op jit(solution)/shard_map/reduce_scatter | solution.py:185
  2638.6 2025.6 %reduce-scatter.9.cloned.1.call-start = ((), (), s32[]{:S(2)}) async-start(), calls=%async_computation.6 | async-start | bytes 16908288 | tf_op jit(solution)/shard_map/reduce_scatter | solution.py:184
  (559 other events, 12875.4 us)
Sparse Core Ops, SparseCore 0:
  909.9 1746.8 reduce-scatter.6
  2659.8 674.4 reduce-scatter.4
  3337.3 662.6 reduce-scatter.10
  4002.8 661.3 reduce-scatter.8
where the time goes:
time: 4700 us; the launch traced here: 4670 us
  waiting for transfers between devices  2400 us (51%)
  starting transfers between devices  1240 us (26%)
  matrix products  474 us (10%)
  local copies, waits for them, and re-layouts  234 us (5%)
  other arithmetic  196 us (4%)
  blocking collectives  109 us (2%)
    ppermute x186, starting transfers between devices, shifted(): lax.ppermute(value, axis, [(source, source + steps) for source in range(l...  981 us
    reduce_scatter x1, waiting for transfers between devices, shards(): lax.psum_scatter(down_part, ('seq', 'row'), scatter_dimension=0, tiled=True)  666 us
    reduce_scatter x1, waiting for transfers between devices, shards(): lax.psum_scatter(up_part, ('seq', 'row'), scatter_dimension=0, tiled=True)  664 us
    reduce_scatter x1, waiting for transfers between devices, shards(): lax.psum_scatter(qkv_part, ('seq', 'row'), scatter_dimension=0, tiled=True)  560 us
    ppermute x186, waiting for transfers between devices, shifted(): lax.ppermute(value, axis, [(source, source + steps) for source in range(l...  476 us
    ppermute x64, starting transfers between devices, from_behind(): return lax.ppermute(block, axis, route)  256 us
    while x837, local copies, waits for them, and re-layouts  221 us
    unnamed x1, blocking collectives  109 us
  transfers between devices with their start and end apart: 254, of which 78 were waited for; matrix products, arithmetic and copies ran while one was open for 16% of the time, Pallas kernels for 0%

commit v1 on v0

v1 whole, which is shorter than its diff:
```python
import functools
import math

import jax
import jax.numpy as jnp
from jax import lax
from jax.experimental import pallas as pl
from jax.experimental.pallas import tpu as pltpu
from jax.sharding import PartitionSpec as P

MESH = pl.DeviceIdType.MESH
f32 = jnp.float32
bf16 = jnp.bfloat16

D = 1024
H = 16
HD = 64
FF = 4096
T = 192
HT = T // 2
BLOCKS = 32
TILE = 768
TILES = 8
PACK = 304
GRAD = 288
EPS = 1e-05
NEG = -1e30
LOG2E = math.log2(math.e)
LN2 = math.log(2.0)
SCALE = HD**-0.5
VMEM_LIMIT = 60 * 1024 * 1024

ANY = pl.BlockSpec(memory_space=pl.ANY)
VM = pl.BlockSpec(memory_space=pltpu.VMEM)


def dot(a, b):
    return jnp.dot(a, b, preferred_element_type=f32)


def dot_nt(a, b):
    return lax.dot_general(a, b, (((1,), (1,)), ((), ())), preferred_element_type=f32)


def transposed(v):
    return v.astype(f32).T.astype(bf16)


def swap_halves(first, second):
    lane = lax.broadcasted_iota(jnp.int32, first.shape, 1)
    low = lane < HD
    first, second = first.astype(f32), second.astype(f32)
    return (
        jnp.where(low, first, pltpu.roll(second, HD, 1)).astype(bf16),
        jnp.where(low, pltpu.roll(first, HD, 1), second).astype(bf16),
    )


class Place:
    def __init__(self):
        self.s = lax.axis_index("seq")
        self.r = lax.axis_index("row")
        self.y_lo = lax.div(self.s, 16)
        self.head = lax.rem(self.s, 16)
        self.y_hi = lax.div(self.r, 2)
        self.core = lax.rem(self.r, 2)
        tile = lax.div(self.s, 4)
        self.block_core = lax.rem(lax.div(tile + 1, 2), 2)
        self.slot = lax.div(self.s, 8) * 4 + lax.rem(self.s, 4)
        self.partner = (self.s, self.r + 1 - 2 * self.core)
        self.self_served = jnp.logical_and(self.y_lo == self.core, self.block_core == self.core)
        self.self_count = jnp.where(self.self_served, 1, 0)

    def head_device(self, h):
        return (self.core * 16 + h, self.y_hi * 2 + self.block_core)

    def own_tile(self, j, core=None):
        core = self.core if core is None else core
        return 2 * j + lax.rem(j + core, 2)

    def own_block(self, n):
        return self.own_tile(lax.div(n, 4)) * 4 + lax.rem(n, 4)

    def block_device(self, n):
        return (self.own_block(n), self.y_hi * 2 + self.y_lo)

    def is_self(self, device):
        return jnp.logical_and(device[0] == self.s, device[1] == self.r)


def remote(src, dst, send, recv, device):
    return pltpu.make_async_remote_copy(
        src_ref=src, dst_ref=dst, send_sem=send, recv_sem=recv, device_id=device, device_id_type=MESH
    )


def send_to(place, src, dst, send, recv, device):
    own = place.is_self(device)

    @pl.when(own)
    def _():
        pltpu.make_async_copy(src, dst, recv).start()

    @pl.when(jnp.logical_not(own))
    def _():
        remote(src, dst, send, recv, device).start()


def sent_to(place, src, dst, send, recv, device):
    @pl.when(jnp.logical_not(place.is_self(device)))
    def _():
        remote(src, dst, send, recv, device).wait_send()


def arrived(dst, recv):
    pltpu.make_async_copy(dst, dst, recv).wait()


def greet(barrier, device):
    pl.semaphore_signal(barrier, inc=1, device_id=device, device_id_type=MESH)


def greet_all(place, barrier, device_of):
    def one(n, carry):
        device = device_of(n)

        @pl.when(jnp.logical_not(place.is_self(device)))
        def _():
            greet(barrier, device)

        return carry

    lax.fori_loop(0, 16, one, 0)


def loop(count, body):
    def one(n, carry):
        body(n)
        return carry

    lax.fori_loop(0, count, one, 0)


def params(collective_id):
    return pltpu.CompilerParams(
        collective_id=collective_id, has_side_effects=True, vmem_limit_bytes=VMEM_LIMIT
    )


def qkv_kernel(x_ref, seg_ref, gain_ref, w_ref, pk_ref, w_scr, stage, w_sem, send, recv, fsend, frecv):
    place = Place()

    def weight(g, part):
        return pltpu.make_async_copy(
            w_ref.at[:, pl.ds(part * D + g * 256, 256)], w_scr.at[g, part], w_sem.at[g, part]
        )

    for g in range(4):
        for part in range(3):
            weight(g, part).start()
    barrier = pltpu.get_barrier_semaphore()
    greet_all(place, barrier, place.block_device)
    greet(barrier, place.partner)

    x = x_ref[0].astype(f32)
    a = (x * lax.rsqrt(jnp.mean(x * x, axis=-1, keepdims=True) + EPS) * gain_ref[...]).astype(bf16)
    seg = seg_ref[...].astype(f32)
    row = lax.broadcasted_iota(jnp.int32, (16, 128), 0)
    rest = jnp.concatenate([seg[:, 128:T], jnp.zeros((1, 256 - T), f32)], axis=1)
    seg_tile = jnp.where(row == 0, seg[:, :128], jnp.where(row == 1, rest, 0.0)).astype(bf16)
    pl.semaphore_wait(barrier, 17 - place.self_count)

    for g in range(4):
        for part in range(3):
            weight(g, part).wait()
        q = dot(a, w_scr[g, 0]) * (SCALE * LOG2E)
        k = dot(a, w_scr[g, 1])
        v = dot(a, w_scr[g, 2])
        for m in range(2):
            lanes = slice(128 * m, 128 * m + 128)
            h = 4 * g + 2 * m
            kv = swap_halves(k[:, lanes].astype(bf16), v[:, lanes].astype(bf16))
            qq = q[:, lanes].astype(bf16)
            qp = swap_halves(qq[:HT], qq[HT:])
            for e in range(2):
                stage[h + e, 0:T] = kv[e]
                stage[h + e, T : T + HT] = qp[e]
                stage[h + e, T + HT : PACK] = seg_tile
                send_to(
                    place, stage.at[h + e], pk_ref.at[place.s], send.at[h + e], recv.at[place.slot],
                    place.head_device(h + e),
                )

    def forward(n):
        i = place.own_block(n)
        return remote(pk_ref.at[i], pk_ref.at[i], fsend.at[n], frecv.at[n], place.partner)

    def pass_on(n):
        arrived(pk_ref.at[place.own_block(n)], recv.at[n])
        forward(n).start()

    loop(16, pass_on)

    def finish(n):
        sent_to(
            place, stage.at[n], pk_ref.at[place.s], send.at[n], recv.at[place.slot], place.head_device(n)
        )
        forward(n).wait_send()
        forward(n).wait_recv()

    loop(16, finish)


def qkv_call(frames, segment_ids, gain, w_qkv):
    return pl.pallas_call(
        qkv_kernel,
        name="qkv_to_heads",
        out_shape=jax.ShapeDtypeStruct((BLOCKS, PACK, 128), bf16),
        in_specs=[VM, VM, VM, ANY],
        out_specs=ANY,
        scratch_shapes=[
            pltpu.VMEM((4, 3, D, 256), bf16),
            pltpu.VMEM((16, PACK, 128), bf16),
            pltpu.SemaphoreType.DMA((4, 3)),
            pltpu.SemaphoreType.DMA((16,)),
            pltpu.SemaphoreType.DMA((16,)),
            pltpu.SemaphoreType.DMA((16,)),
            pltpu.SemaphoreType.DMA((16,)),
        ],
        compiler_params=params(0),
    )(frames, segment_ids, gain, w_qkv)


def seg_parts(pk_ref, block):
    tile = pk_ref[block, T + HT : PACK].astype(f32)
    first, second = tile[0:1], tile[1:2]
    row = jnp.concatenate([first, second[:, : T - 128]], axis=1)
    column = jnp.concatenate(
        [
            jnp.broadcast_to(first, (128, 128)).T,
            jnp.broadcast_to(second, (128, 128)).T[: T - 128],
        ],
        axis=0,
    )
    return row, column


def fill_segments(pk_ref, seg_row, seg_col):
    row0, col0 = seg_parts(pk_ref, 0)
    row7, col7 = seg_parts(pk_ref, BLOCKS - 1)
    common = row0[:, T - 1 : T]
    common_row = jnp.broadcast_to(common, (1, TILE - T))
    common_col = jnp.broadcast_to(common, (TILE - T, 128))
    seg_row[0, 0:1] = jnp.concatenate([row0, common_row], axis=1)
    seg_row[1, 0:1] = jnp.broadcast_to(common, (1, TILE))
    seg_row[2, 0:1] = jnp.concatenate([common_row, row7], axis=1)
    seg_col[0] = jnp.concatenate([col0, common_col], axis=0)
    seg_col[1] = jnp.broadcast_to(common, (TILE, 128))
    seg_col[2] = jnp.concatenate([common_col, col7], axis=0)


def seg_kind(tile):
    return jnp.where(tile == 0, 0, jnp.where(tile == TILES - 1, 2, 1))


def allowed_pairs(seg_row, seg_col, q_tile, k_tile):
    rows = seg_row[pl.ds(seg_kind(q_tile), 1), 0:1][0]
    columns = seg_col[pl.ds(seg_kind(k_tile), 1)][0][:, 0:1]
    pos_k = k_tile * TILE + lax.broadcasted_iota(jnp.int32, (TILE, TILE), 0)
    pos_q = q_tile * TILE + lax.broadcasted_iota(jnp.int32, (TILE, TILE), 1)
    return jnp.logical_and(columns == rows, pos_k <= pos_q)


def load_queries(pk_ref, tile, qp):
    lane = lax.broadcasted_iota(jnp.int32, (HT, 128), 1)
    for b in range(4):
        packed = pk_ref[tile * 4 + b, T : T + HT].astype(f32)
        qp[b * T : b * T + HT] = jnp.where(lane < HD, packed, 0.0).astype(bf16)
        qp[b * T + HT : b * T + T] = jnp.where(lane < HD, pltpu.roll(packed, HD, 1), 0.0).astype(bf16)


def load_keys(pk_ref, tile):
    return pk_ref[pl.ds(tile * 4, 4), 0:T].reshape(TILE, 128)


def packed_rows(value_t, b):
    twice = jnp.concatenate([value_t, value_t], axis=0)[:, b * T : (b + 1) * T]
    return twice


def pack_transposed(value_t):
    both = jnp.concatenate([value_t, value_t], axis=0).T
    lane = lax.broadcasted_iota(jnp.int32, (HT, 128), 1)
    return [
        jnp.where(lane < HD, both[b * T : b * T + HT], both[b * T + HT : b * T + T]).astype(bf16)
        for b in range(4)
    ]


def forward_kernel(pk_ref, o_in, lse_ref, ot_ref, vt, qp, top, acc, seg_row, seg_col, stage, send, recv):
    place = Place()
    barrier = pltpu.get_barrier_semaphore()
    greet_all(place, barrier, place.head_device)
    fill_segments(pk_ref, seg_row, seg_col)
    one = jnp.where(lax.broadcasted_iota(jnp.int32, (16, TILE), 0) == 0, 1.0, 0.0).astype(bf16)

    def prepare(t):
        vt[t, 0:HD] = transposed(load_keys(pk_ref, t))[HD:]
        vt[t, HD : HD + 16] = one

    loop(TILES, prepare)
    pl.semaphore_wait(barrier, 16 - place.self_count)

    def step(q_tile, k_tile, masked):
        scores = dot_nt(load_keys(pk_ref, k_tile), qp[...])
        if masked:
            scores = jnp.where(allowed_pairs(seg_row, seg_col, q_tile, k_tile), scores, NEG)
        peak = jnp.maximum(top[...], jnp.max(scores, axis=0, keepdims=True))
        fade = jnp.exp2(top[...] - peak)
        top[...] = peak
        weights = jnp.exp2(scores - peak).astype(bf16)
        acc[...] = acc[...] * fade + dot(vt[k_tile], weights)

    def q_loop(n):
        j = 3 - n
        q_tile = place.own_tile(j)
        load_queries(pk_ref, q_tile, qp)
        top[...] = jnp.full((1, TILE), NEG, f32)
        acc[...] = jnp.zeros((HD + 16, TILE), f32)
        step(q_tile, q_tile, True)

        def k_loop(k_tile, carry):
            plain = jnp.logical_and(k_tile > 0, q_tile < TILES - 1)

            @pl.when(plain)
            def _():
                step(q_tile, k_tile, False)

            @pl.when(jnp.logical_not(plain))
            def _():
                step(q_tile, k_tile, True)

            return carry

        lax.fori_loop(0, q_tile, k_loop, 0)
        total = acc[HD : HD + 1]
        out_t = acc[0:HD] / total
        lse_ref[j, 0:1] = top[...] + jnp.log2(total)
        ot_ref[j] = out_t
        packed = pack_transposed(out_t)
        for b in range(4):
            m = j * 4 + b
            stage[m] = packed[b]
            send_to(
                place, stage.at[m], o_in.at[place.head], send.at[m], recv.at[place.head],
                place.block_device(m),
            )

    loop(4, q_loop)

    def finish(n):
        sent_to(
            place, stage.at[n], o_in.at[place.head], send.at[n], recv.at[place.head], place.block_device(n)
        )
        arrived(o_in.at[n], recv.at[n])

    loop(16, finish)


def forward_call(pk):
    return pl.pallas_call(
        forward_kernel,
        name="attention",
        out_shape=(
            jax.ShapeDtypeStruct((16, HT, 128), bf16),
            jax.ShapeDtypeStruct((4, 1, TILE), f32),
            jax.ShapeDtypeStruct((4, HD, TILE), f32),
        ),
        in_specs=[VM],
        out_specs=(ANY, VM, VM),
        scratch_shapes=[
            pltpu.VMEM((TILES, HD + 16, TILE), bf16),
            pltpu.VMEM((TILE, 128), bf16),
            pltpu.VMEM((1, TILE), f32),
            pltpu.VMEM((HD + 16, TILE), f32),
            pltpu.VMEM((3, 1, TILE), f32),
            pltpu.VMEM((3, TILE, 128), f32),
            pltpu.VMEM((16, HT, 128), bf16),
            pltpu.SemaphoreType.DMA((16,)),
            pltpu.SemaphoreType.DMA((16,)),
        ],
        compiler_params=params(1),
    )(pk)


FIRST = lambda c: ((c + 1) // 2) % 2
SECOND = lambda c: c // 2


def chip_bits(x, y, z):
    return [FIRST(x), FIRST(y), FIRST(z), SECOND(x), SECOND(y), SECOND(z)]


def position(part, y_lo, x, z, y_hi):
    bits = chip_bits(x, y_hi * 2 + y_lo, z)
    at = 0
    for k in range(6):
        at = at * 2 + bits[(part + k) % 6]
    return at


class Halving:
    START = [0, 32, 48, 56, 60, 62]

    def __init__(self, place, grads, each, acc, land, keep_sem, send, recv):
        self.place, self.grads, self.each = place, grads, each
        self.acc, self.land, self.keep_sem, self.send, self.recv = acc, land, keep_sem, send, recv
        x, z = lax.div(place.head, 4), lax.rem(place.head, 4)
        y = place.y_hi * 2 + place.y_lo
        self.bits = [
            lax.rem(lax.div(x + 1, 2), 2), lax.rem(lax.div(y + 1, 2), 2), lax.rem(lax.div(z + 1, 2), 2),
            lax.div(x, 2), lax.div(y, 2), lax.div(z, 2),
        ]

        def device(x, y, z):
            return (lax.rem(y, 2) * 16 + x * 4 + z, lax.div(y, 2) * 2 + place.core)

        flip = lambda c: c + 1 - 2 * lax.rem(c, 2)
        self.neighbours = [
            device(flip(x), y, z), device(x, flip(y), z), device(x, y, flip(z)),
            device(3 - x, y, z), device(x, 3 - y, z), device(x, y, 3 - z),
        ]

    def greet(self, barrier):
        for device in self.neighbours:
            greet(barrier, device)

    def bit(self, part, stage):
        return self.bits[(part + stage) % 6]

    def units(self, part):
        return pl.ds(part * self.each, self.each)

    def kept(self, part):
        return pltpu.make_async_copy(
            self.grads.at[self.units(part), pl.ds(self.bit(part, 0) * 32, 32)],
            self.acc.at[self.units(part)],
            self.keep_sem.at[part],
        )

    def hop(self, part, stage):
        half = 32 >> stage
        if stage == 0:
            source = self.grads.at[self.units(part), pl.ds((1 - self.bit(part, 0)) * 32, 32)]
        else:
            base = self.base(part, stage - 1) + (1 - self.bit(part, stage)) * half
            source = self.acc.at[self.units(part), pl.ds(base, half)]
        return remote(
            source,
            self.land.at[self.units(part), pl.ds(self.START[stage], half)],
            self.send.at[part, stage],
            self.recv.at[part, stage],
            self.neighbours[(part + stage) % 6],
        )

    def base(self, part, stage):
        at = 0
        for k in range(1, stage + 1):
            at = at + self.bit(part, k) * (32 >> k)
        return at

    def start(self, part):
        self.hop(part, 0).start()
        self.kept(part).start()

    def add(self, part, base, landed, count):
        group = min(count, 4)

        def body(i):
            here = pl.ds(base + i * group, group)
            there = pl.ds(landed + i * group, group)
            total = self.acc[self.units(part), here].astype(f32) + self.land[self.units(part), there].astype(f32)
            self.acc[self.units(part), here] = total.astype(bf16)

        loop(count // group, body)

    def advance(self, part, stage):
        self.hop(part, stage).wait_recv()
        if stage == 0:
            self.kept(part).wait()
        half = 16 >> stage
        base = self.base(part, stage)
        bit = self.bit(part, stage + 1)
        self.add(part, base + (1 - bit) * half, self.START[stage] + (1 - bit) * half, half)
        self.hop(part, stage + 1).start()
        self.add(part, base + bit * half, self.START[stage] + bit * half, half)

    def last(self, part):
        self.hop(part, 5).wait_recv()
        base = self.base(part, 5)
        return (
            self.acc[self.units(part), pl.ds(base, 1)].astype(f32)
            + self.land[self.units(part), pl.ds(62, 1)].astype(f32)
        )[:, 0]

    def finish(self):
        for part in range(6):
            for stage in range(6):
                self.hop(part, stage).wait_send()


def halving_scratch(units, width):
    return [
        pltpu.VMEM((units, 32, 16, width), bf16),
        pltpu.VMEM((units, 64, 16, width), bf16),
        pltpu.SemaphoreType.DMA((6,)),
        pltpu.SemaphoreType.DMA((6, 6)),
        pltpu.SemaphoreType.DMA((6, 6)),
    ]


class MidSums:
    def __init__(self, place, fin, side, down, sem, up_out, out_out, down_out):
        self.place, self.fin, self.side, self.down, self.sem = place, fin, side, down, sem
        self.up_out, self.out_out, self.down_out = up_out, out_out, down_out

    def targets(self):
        return [(self.place.core * 16 + self.place.head, self.place.y_hi * 2 + k) for k in range(2)]

    def sources(self):
        return [(m * 16 + self.place.head, self.place.y_hi * 2 + self.place.y_lo) for m in range(2)]

    def self_count(self):
        return jnp.where(self.place.y_lo == self.place.core, 1, 0)

    def greet(self, barrier):
        greet(barrier, self.place.partner)
        for device in self.sources():

            @pl.when(jnp.logical_not(self.place.is_self(device)))
            def _(device=device):
                greet(barrier, device)

    def greetings(self):
        return 3 - self.self_count()

    def store(self, part, value):
        for u in range(3):
            self.fin[part * 3 + u] = value[u].reshape(2, 8, 256)

    def aside(self):
        return remote(
            self.fin.at[0:10, 1 - self.place.core], self.side, self.sem.at[0], self.sem.at[1], self.place.partner
        )

    def down_hop(self, k):
        return (
            self.fin.at[10 + 4 * k : 14 + 4 * k],
            self.down.at[self.place.y_lo],
            self.sem.at[2 + k],
            self.sem.at[4 + self.place.y_lo],
            self.targets()[k],
        )

    def run(self):
        place = self.place
        self.aside().start()
        for k in range(2):
            send_to(place, *self.down_hop(k))
        self.aside().wait_recv()
        mine, other = place.core, 1 - place.core
        for u in range(8):
            self.up_out[:, pl.ds(mine * 2048 + u * 256, 256)] = self.fin[u, mine]
            self.up_out[:, pl.ds(other * 2048 + u * 256, 256)] = self.side[u]
        for u in range(2):
            self.out_out[:, pl.ds(mine * 512 + u * 256, 256)] = self.fin[8 + u, mine]
            self.out_out[:, pl.ds(other * 512 + u * 256, 256)] = self.side[8 + u]
        for m in range(2):
            arrived(self.down.at[m], self.sem.at[4 + m])
            for v in range(4):
                group, half = v // 2, v % 2
                self.down_out[group * 16 : group * 16 + 16, m * 512 + half * 256 : m * 512 + half * 256 + 256] = (
                    self.down[m, v].reshape(16, 256)
                )
        self.aside().wait_send()
        for k in range(2):
            sent_to(place, *self.down_hop(k))


def mid_scratch():
    return halving_scratch(18, 256) + [
        pltpu.VMEM((18, 2, 8, 256), f32),
        pltpu.VMEM((10, 8, 256), f32),
        pltpu.VMEM((2, 4, 2, 8, 256), f32),
        pltpu.SemaphoreType.DMA((6,)),
    ]


MID_OUT = (
    jax.ShapeDtypeStruct((8, FF), f32),
    jax.ShapeDtypeStruct((8, D), f32),
    jax.ShapeDtypeStruct((32, D), f32),
)


def mid_sums_kernel(grads, up_out, out_out, down_out, acc, land, keep_sem, hsend, hrecv, fin, side, down, sem):
    place = Place()
    halving = Halving(place, grads, 3, acc, land, keep_sem, hsend, hrecv)
    mid = MidSums(place, fin, side, down, sem, up_out, out_out, down_out)
    barrier = pltpu.get_barrier_semaphore()
    halving.greet(barrier)
    mid.greet(barrier)
    pl.semaphore_wait(barrier, 6 + mid.greetings())
    for part in range(6):
        halving.start(part)
    for stage in range(5):
        for part in range(6):
            halving.advance(part, stage)
    for part in range(6):
        mid.store(part, halving.last(part))
    mid.run()
    halving.finish()


def mid_sums_call(grads):
    return pl.pallas_call(
        mid_sums_kernel,
        name="sum_mid_grads",
        out_shape=MID_OUT,
        in_specs=[ANY],
        out_specs=(VM, VM, VM),
        scratch_shapes=mid_scratch(),
        compiler_params=params(5),
    )(grads)


ROOT = math.sqrt(2.0 / math.pi)
CUBE = 0.044715


def middle_kernel(
    o_in, x_ref, dy_ref, gain_ref, w_out, w_up, w_down,
    y_ref, grads, dx1_ref, gain_grad, da_in,
    wo, wu, wd, o2, b2, dm2, b2t, x1s, ysum, hsum, yside, hside, da_side, outg, gs, stage,
    w_sem, p_send, p_recv, g_sem, send, recv,
):
    place = Place()
    core = place.core

    def up_copy(j):
        at = pl.multiple_of(core * 2048 + j * 512, 512)
        return pltpu.make_async_copy(w_up.at[:, pl.ds(at, 512)], wu.at[j], w_sem.at[1 + j])

    def down_copy(j):
        at = pl.multiple_of(core * 2048 + j * 512, 512)
        return pltpu.make_async_copy(w_down.at[pl.ds(at, 512)], wd.at[j], w_sem.at[5 + j])

    out_copy = pltpu.make_async_copy(w_out, wo, w_sem.at[0])
    out_copy.start()
    for j in range(4):
        up_copy(j).start()
        down_copy(j).start()
    barrier = pltpu.get_barrier_semaphore()
    greet_all(place, barrier, place.block_device)
    greet(barrier, place.partner)

    def across(k, src, dst):
        return remote(src, dst, p_send.at[k], p_recv.at[k], place.partner)

    dm2[0:T] = dy_ref[0]
    for m in range(8):
        lo, hi = swap_halves(o_in[2 * m], o_in[2 * m + 1])
        o2[0:HT, 128 * m : 128 * m + 128] = lo
        o2[HT:T, 128 * m : 128 * m + 128] = hi
    pl.semaphore_wait(barrier, 17 - place.self_count)
    dm_hop = across(0, dm2.at[0:T], dm2.at[T : 2 * T])
    o_hop = across(1, o2.at[0:T], o2.at[T : 2 * T])
    dm_hop.start()
    o_hop.start()
    out_copy.wait()
    x1 = x_ref[0].astype(f32) + dot(o2[0:T], wo[...])
    x1s[...] = x1
    scale1 = lax.rsqrt(jnp.mean(x1 * x1, axis=-1, keepdims=True) + EPS)
    b2[0:T] = (x1 * scale1 * gain_ref[...]).astype(bf16)
    b_hop = across(2, b2.at[0:T], b2.at[T : 2 * T])
    b_hop.start()
    dm_hop.wait_recv()
    b_hop.wait_recv()
    b2t[...] = transposed(b2[...])

    for j in range(4):
        up_copy(j).wait()
        down_copy(j).wait()
        z = dot(b2[...], wu[j])
        zz = z * z
        th = jnp.tanh(ROOT * z * (1.0 + CUBE * zz))
        half = 0.5 * (1.0 + th)
        gz = (z * half).astype(bf16)
        slope = half + 0.5 * z * (1.0 - th * th) * (ROOT * (1.0 + 3.0 * CUBE * zz))
        dz = (dot_nt(dm2[...], wd[j]) * slope).astype(bf16)
        yj = dot(gz, wd[j])
        hj = dot_nt(dz, wu[j])
        if j == 0:
            ysum[...] = yj
            hsum[...] = hj
        else:
            ysum[...] += yj
            hsum[...] += hj
        up = dot(b2t[...], dz).astype(bf16)
        for u in range(2):
            unit = 2 * j + u
            for chip in range(64):
                y_lo, x, z_, y_hi = chip // 32, chip // 8 % 4, chip // 2 % 4, chip % 2
                gs[unit, position(unit // 3, y_lo, x, z_, y_hi)] = up[
                    chip * 16 : chip * 16 + 16, u * 256 : u * 256 + 256
                ]
            pltpu.make_async_copy(gs.at[unit], grads.at[unit], g_sem.at[unit]).start()
        down = dot(transposed(gz), dm2[...]).astype(bf16)
        for chip in range(8):
            for group in range(4):
                rows = slice(chip * 64 + group * 16, chip * 64 + group * 16 + 16)
                for y_lo in range(2):
                    for u in range(2):
                        unit = 10 + group * 2 + u
                        at = y_lo * 512 + u * 256
                        gs[unit, position(unit // 3, y_lo, j, chip // 2, chip % 2)] = down[rows, at : at + 256]
    for unit in range(10, 18):
        pltpu.make_async_copy(gs.at[unit], grads.at[unit], g_sem.at[unit]).start()

    y_hop = across(3, ysum.at[T : 2 * T], yside)
    h_hop = across(4, hsum.at[T : 2 * T], hside)
    h_hop.start()
    y_hop.start()
    h_hop.wait_recv()
    x1 = x1s[...]
    scale1 = lax.rsqrt(jnp.mean(x1 * x1, axis=-1, keepdims=True) + EPS)
    dh2 = hsum[0:T] + hside[...]
    gain_grad[...] = jnp.sum(dh2 * x1 * scale1, axis=0, keepdims=True)
    dn = dh2 * gain_ref[...]
    back = scale1 * dn - x1 * (scale1 * scale1 * scale1) * jnp.mean(dn * x1, axis=-1, keepdims=True)
    dx1 = dy_ref[0].astype(f32) + back
    dx1_ref[...] = dx1
    da = dx1.astype(bf16)
    da_side[0, 0:T] = da[:, 0:512]
    da_side[1, 0:T] = da[:, 512:1024]
    da_hop = across(5, da_side.at[1 - core, 0:T], da_side.at[1 - core, T : 2 * T])
    da_hop.start()
    for g in range(4):
        dattn = dot_nt(da, wo[256 * g : 256 * g + 256]).astype(bf16)
        for m in range(2):
            tile = dattn[:, 128 * m : 128 * m + 128]
            packed = swap_halves(tile[:HT], tile[HT:])
            for e in range(2):
                h = 4 * g + 2 * m + e
                stage[h] = packed[e]
                send_to(
                    place, stage.at[h], da_in.at[place.slot], send.at[h], recv.at[place.slot],
                    place.head_device(h),
                )
    y_hop.wait_recv()
    y_ref[0] = (x1 + ysum[0:T] + yside[...]).astype(bf16)
    o_hop.wait_recv()
    da_hop.wait_recv()
    out = dot(transposed(o2[...]), da_side[core]).astype(bf16)
    for u in range(2):
        unit = 8 + u
        for chip in range(64):
            y_lo, x, z_, y_hi = chip // 32, chip // 8 % 4, chip // 2 % 4, chip % 2
            gs[unit, position(unit // 3, y_lo, x, z_, y_hi)] = out[
                chip * 16 : chip * 16 + 16, u * 256 : u * 256 + 256
            ]
        pltpu.make_async_copy(gs.at[unit], grads.at[unit], g_sem.at[unit]).start()

    def finish(n):
        sent_to(
            place, stage.at[n], da_in.at[place.slot], send.at[n], recv.at[place.slot], place.head_device(n)
        )
        arrived(da_in.at[n], recv.at[n])

    loop(16, finish)
    for unit in range(18):
        pltpu.make_async_copy(gs.at[unit], grads.at[unit], g_sem.at[unit]).wait()
    for hop in (dm_hop, o_hop, b_hop, y_hop, h_hop, da_hop):
        hop.wait_send()


def middle_call(o_in, frames, out_grad, gain, w_out, w_up, w_down):
    return pl.pallas_call(
        middle_kernel,
        name="feed_forward",
        out_shape=(
            jax.ShapeDtypeStruct((1, T, D), bf16),
            jax.ShapeDtypeStruct((18, 64, 16, 256), bf16),
            jax.ShapeDtypeStruct((T, D), f32),
            jax.ShapeDtypeStruct((1, D), f32),
            jax.ShapeDtypeStruct((16, HT, 128), bf16),
        ),
        in_specs=[VM, VM, VM, VM, ANY, ANY, ANY],
        out_specs=(VM, ANY, VM, VM, ANY),
        scratch_shapes=[
            pltpu.VMEM((D, D), bf16),
            pltpu.VMEM((4, D, 512), bf16),
            pltpu.VMEM((4, 512, D), bf16),
            pltpu.VMEM((2 * T, D), bf16),
            pltpu.VMEM((2 * T, D), bf16),
            pltpu.VMEM((2 * T, D), bf16),
            pltpu.VMEM((D, 2 * T), bf16),
            pltpu.VMEM((T, D), f32),
            pltpu.VMEM((2 * T, D), f32),
            pltpu.VMEM((2 * T, D), f32),
            pltpu.VMEM((T, D), f32),
            pltpu.VMEM((T, D), f32),
            pltpu.VMEM((2, 2 * T, 512), bf16),
            pltpu.VMEM((8, 128), f32),
            pltpu.VMEM((18, 64, 16, 256), bf16),
            pltpu.VMEM((16, HT, 128), bf16),
            pltpu.SemaphoreType.DMA((9,)),
            pltpu.SemaphoreType.DMA((6,)),
            pltpu.SemaphoreType.DMA((6,)),
            pltpu.SemaphoreType.DMA((18,)),
            pltpu.SemaphoreType.DMA((16,)),
            pltpu.SemaphoreType.DMA((16,)),
        ],
        compiler_params=params(2),
    )(o_in, frames, out_grad, gain, w_out, w_up, w_down)


def backward_kernel(
    pk_ref, da_ref, lse_ref, ot_ref, dqkv_in,
    kt, qp, gp, delta, lse, dq, dkv, seg_row, seg_col, part, landed, stage,
    p_send, p_recv, send, recv,
):
    place = Place()
    barrier = pltpu.get_barrier_semaphore()
    greet_all(place, barrier, place.head_device)
    greet(barrier, place.partner)
    fill_segments(pk_ref, seg_row, seg_col)

    def prepare(t):
        kt[t] = transposed(load_keys(pk_ref, t))[:HD]
        dkv[t] = jnp.zeros((TILE, 128), f32)

    loop(TILES, prepare)

    def step(q_tile, k_tile, masked):
        keys = load_keys(pk_ref, k_tile)
        scores = dot_nt(keys, qp[...])
        if masked:
            scores = jnp.where(allowed_pairs(seg_row, seg_col, q_tile, k_tile), scores, NEG)
        weights = jnp.exp2(scores - lse[...])
        slopes = (weights * (dot_nt(keys, gp[...]) - delta[...])).astype(bf16)
        weights = weights.astype(bf16)
        dkv[k_tile] += dot(weights, gp[...]) + dot(slopes, qp[...])
        dq[...] += dot(kt[k_tile], slopes)

    def q_loop(n):
        j = 3 - n
        q_tile = place.own_tile(j)
        load_queries(pk_ref, q_tile, qp)
        lane = lax.broadcasted_iota(jnp.int32, (HT, 128), 1)
        for b in range(4):
            packed = da_ref[j * 4 + b].astype(f32)
            gp[b * T : b * T + HT] = jnp.where(lane < HD, 0.0, pltpu.roll(packed, HD, 1)).astype(bf16)
            gp[b * T + HT : b * T + T] = jnp.where(lane < HD, 0.0, packed).astype(bf16)
        delta[...] = jnp.sum(gp[...].astype(f32).T[HD:] * ot_ref[j], axis=0, keepdims=True)
        lse[...] = lse_ref[j, 0:1]
        dq[...] = jnp.zeros((HD, TILE), f32)
        step(q_tile, q_tile, True)

        def k_loop(k_tile, carry):
            plain = jnp.logical_and(k_tile > 0, q_tile < TILES - 1)

            @pl.when(plain)
            def _():
                step(q_tile, k_tile, False)

            @pl.when(jnp.logical_not(plain))
            def _():
                step(q_tile, k_tile, True)

            return carry

        lax.fori_loop(0, q_tile, k_loop, 0)
        packed = pack_transposed(dq[...] * SCALE)
        for b in range(4):
            stage[j * 4 + b, T:GRAD] = packed[b]

    loop(4, q_loop)

    factor = jnp.where(lax.broadcasted_iota(jnp.int32, (1, 128), 1) < HD, LN2, 1.0)
    pl.semaphore_wait(barrier, 17 - place.self_count)

    def part_hop(j):
        return remote(part.at[j], landed.at[j], p_send.at[j], p_recv.at[j], place.partner)

    def give(j):
        part[j] = (dkv[place.own_tile(j, 1 - place.core)] * factor).astype(bf16)
        part_hop(j).start()

    loop(4, give)

    def take(j):
        part_hop(j).wait_recv()
        total = dkv[place.own_tile(j)] * factor + landed[j].astype(f32)
        total = total.astype(bf16)
        for b in range(4):
            m = j * 4 + b
            stage[m, 0:T] = total[b * T : (b + 1) * T]
            send_to(
                place, stage.at[m], dqkv_in.at[place.head], send.at[m], recv.at[place.head],
                place.block_device(m),
            )

    loop(4, take)

    def finish(n):
        sent_to(
            place, stage.at[n], dqkv_in.at[place.head], send.at[n], recv.at[place.head],
            place.block_device(n),
        )
        arrived(dqkv_in.at[n], recv.at[n])

    loop(16, finish)
    loop(4, lambda j: part_hop(j).wait_send())


def backward_call(pk, da_in, lse, ot):
    return pl.pallas_call(
        backward_kernel,
        name="attention_grad",
        out_shape=jax.ShapeDtypeStruct((16, GRAD, 128), bf16),
        in_specs=[VM, VM, VM, VM],
        out_specs=ANY,
        scratch_shapes=[
            pltpu.VMEM((TILES, HD, TILE), bf16),
            pltpu.VMEM((TILE, 128), bf16),
            pltpu.VMEM((TILE, 128), bf16),
            pltpu.VMEM((1, TILE), f32),
            pltpu.VMEM((1, TILE), f32),
            pltpu.VMEM((HD, TILE), f32),
            pltpu.VMEM((TILES, TILE, 128), f32),
            pltpu.VMEM((3, 1, TILE), f32),
            pltpu.VMEM((3, TILE, 128), f32),
            pltpu.VMEM((4, TILE, 128), bf16),
            pltpu.VMEM((4, TILE, 128), bf16),
            pltpu.VMEM((16, GRAD, 128), bf16),
            pltpu.SemaphoreType.DMA((4,)),
            pltpu.SemaphoreType.DMA((4,)),
            pltpu.SemaphoreType.DMA((16,)),
            pltpu.SemaphoreType.DMA((16,)),
        ],
        compiler_params=params(3),
    )(pk, da_in, lse, ot)


def last_kernel(
    dqkv_in, x_ref, dx1_ref, gain_ref, gain2_ref, w_ref,
    dx_ref, qkv_out, gain_out, gain2_out, grads,
    w_scr, a2, dn, dhalf, a2t, fin, side, gstage, gacc, gland,
    acc, land, keep_sem, hsend, hrecv,
    w_sem, p_send, p_recv, g_sem, gs_send, gs_recv,
):
    place = Place()
    core = place.core
    halving = Halving(place, grads, 1, acc, land, keep_sem, hsend, hrecv)
    weight = pltpu.make_async_copy(w_ref, w_scr, w_sem.at[0])
    weight.start()
    barrier = pltpu.get_barrier_semaphore()
    halving.greet(barrier)
    greet(barrier, place.partner)

    def across(k, src, dst):
        return remote(src, dst, p_send.at[k], p_recv.at[k], place.partner)

    x = x_ref[0].astype(f32)
    scale = lax.rsqrt(jnp.mean(x * x, axis=-1, keepdims=True) + EPS)
    a2[0:T] = (x * scale * gain_ref[...]).astype(bf16)
    for m in range(8):
        lo, hi = swap_halves(dqkv_in[2 * m, T:GRAD], dqkv_in[2 * m + 1, T:GRAD])
        dk, dv = swap_halves(dqkv_in[2 * m, 0:T], dqkv_in[2 * m + 1, 0:T])
        dn[0:HT, 128 * m : 128 * m + 128] = lo
        dn[HT:T, 128 * m : 128 * m + 128] = hi
        dn[:, D + 128 * m : D + 128 * m + 128] = dk
        dn[:, 2 * D + 128 * m : 2 * D + 128 * m + 128] = dv
        at = 128 * (m % 4)
        dhalf[m // 4, 0:HT, at : at + 128] = lo
        dhalf[m // 4, HT:T, at : at + 128] = hi
        dhalf[m // 4, 0:T, 512 + at : 512 + at + 128] = dk
        dhalf[m // 4, 0:T, 1024 + at : 1024 + at + 128] = dv
    pl.semaphore_wait(barrier, 7)
    a_hop = across(0, a2.at[0:T], a2.at[T : 2 * T])
    d_hop = across(1, dhalf.at[1 - core, 0:T], dhalf.at[1 - core, T : 2 * T])
    a_hop.start()
    d_hop.start()
    a_hop.wait_recv()
    a2t[...] = transposed(a2[...])
    d_hop.wait_recv()
    for u in range(6):
        block = dot(a2t[...], dhalf[core, :, u * 256 : u * 256 + 256]).astype(bf16)
        for chip in range(64):
            y_lo, cx, z_, y_hi = chip // 32, chip // 8 % 4, chip // 2 % 4, chip % 2
            gstage[u, position(u, y_lo, cx, z_, y_hi)] = block[chip * 16 : chip * 16 + 16]
        pltpu.make_async_copy(gstage.at[u], grads.at[u], g_sem.at[u]).start()
    weight.wait()
    dh1 = dot_nt(dn[...], w_scr[...])
    gain1_grad = jnp.sum(dh1 * x * scale, axis=0, keepdims=True)
    dxn = dh1 * gain_ref[...]
    back = scale * dxn - x * (scale * scale * scale) * jnp.mean(dxn * x, axis=-1, keepdims=True)
    dx_ref[0] = (dx1_ref[...] + back).astype(bf16)

    row = lax.broadcasted_iota(jnp.int32, (128, D), 0)
    both = jnp.where(row == 0, gain1_grad, jnp.where(row == 1, gain2_ref[...], 0.0))
    columns = both.T.astype(bf16)
    for chip in range(64):
        y_lo, cx, z_, y_hi = chip // 32, chip // 8 % 4, chip // 2 % 4, chip % 2
        gacc[position(0, y_lo, cx, z_, y_hi)] = columns[chip * 16 : chip * 16 + 16]

    for u in range(6):
        pltpu.make_async_copy(gstage.at[u], grads.at[u], g_sem.at[u]).wait()
    for p in range(6):
        halving.start(p)

    def gain_hop(stage):
        half = 32 >> stage
        base = 0
        for k in range(stage):
            base = base + halving.bit(0, k) * (32 >> k)
        return base, remote(
            gacc.at[pl.ds(base + (1 - halving.bit(0, stage)) * half, half)],
            gland.at[pl.ds(Halving.START[stage], half)],
            gs_send.at[stage],
            gs_recv.at[stage],
            halving.neighbours[stage],
        )

    def gain_stage(stage):
        base, hop = gain_hop(stage)
        half = 32 >> stage
        hop.wait_recv()
        here = pl.ds(base + halving.bit(0, stage) * half, half)
        there = pl.ds(Halving.START[stage], half)
        gacc[here] = (gacc[here].astype(f32) + gland[there].astype(f32)).astype(bf16)
        if stage < 5:
            gain_hop(stage + 1)[1].start()

    gain_hop(0)[1].start()
    for stage in range(5):
        for p in range(6):
            halving.advance(p, stage)
        gain_stage(stage)
    gain_stage(5)
    for p in range(6):
        fin[p] = halving.last(p)[0].reshape(2, 8, 256)
    base = 0
    for k in range(6):
        base = base + halving.bit(0, k) * (32 >> k)
    gain_rows = gacc[pl.ds(base, 1)][0].astype(f32)
    pair = jnp.concatenate([gain_rows[0:8], gain_rows[8:16]], axis=1)
    fin[6] = jnp.concatenate([gain_rows, jnp.zeros((16, 128), f32)], axis=1).reshape(2, 8, 256)
    del pair
    aside = across(2, fin.at[:, 1 - core], side)
    aside.start()
    aside.wait_recv()
    mine, other = core, 1 - core
    for u in range(6):
        at = (u // 2) * D + (u % 2) * 256
        qkv_out[:, pl.ds(at + mine * 512, 256)] = fin[u, mine]
        qkv_out[:, pl.ds(at + other * 512, 256)] = side[u]
    sums = fin[6, mine][:, 0:128] + side[6][:, 0:128]
    wide = jnp.concatenate([sums] + [jnp.zeros((8, 128), f32)] * 15, axis=0).T
    gain_out[...] = wide[0:1]
    gain2_out[...] = wide[1:2]
    for hop in (a_hop, d_hop, aside):
        hop.wait_send()
    halving.finish()
    for stage in range(6):
        gain_hop(stage)[1].wait_send()


def last_call(dqkv_in, frames, dx1, gain, gain2_grad, w_qkv):
    return pl.pallas_call(
        last_kernel,
        name="input_grad",
        out_shape=(
            jax.ShapeDtypeStruct((1, T, D), bf16),
            jax.ShapeDtypeStruct((8, 3 * D), f32),
            jax.ShapeDtypeStruct((1, 128), f32),
            jax.ShapeDtypeStruct((1, 128), f32),
            jax.ShapeDtypeStruct((6, 64, 16, 256), bf16),
        ),
        in_specs=[VM, VM, VM, VM, VM, ANY],
        out_specs=(VM, VM, VM, VM, ANY),
        scratch_shapes=[
            pltpu.VMEM((D, 3 * D), bf16),
            pltpu.VMEM((2 * T, D), bf16),
            pltpu.VMEM((T, 3 * D), bf16),
            pltpu.VMEM((2, 2 * T, 1536), bf16),
            pltpu.VMEM((D, 2 * T), bf16),
            pltpu.VMEM((7, 2, 8, 256), f32),
            pltpu.VMEM((7, 8, 256), f32),
            pltpu.VMEM((6, 64, 16, 256), bf16),
            pltpu.VMEM((64, 16, 128), bf16),
            pltpu.VMEM((64, 16, 128), bf16),
        ]
        + halving_scratch(6, 256)
        + [
            pltpu.SemaphoreType.DMA((1,)),
            pltpu.SemaphoreType.DMA((3,)),
            pltpu.SemaphoreType.DMA((3,)),
            pltpu.SemaphoreType.DMA((6,)),
            pltpu.SemaphoreType.DMA((6,)),
            pltpu.SemaphoreType.DMA((6,)),
        ],
        compiler_params=params(4),
    )(dqkv_in, frames, dx1, gain, gain2_grad, w_qkv)


def shards(frames, segment_ids, norm1_gain, w_qkv, w_out, norm2_gain, w_up, w_down, out_grad):
    gain1, gain2 = norm1_gain[None], norm2_gain[None]
    pk = qkv_call(frames, segment_ids, gain1, w_qkv)
    o_in, lse, ot = forward_call(pk)
    y, grads, dx1, gain2_grad, da_in = middle_call(o_in, frames, out_grad, gain2, w_out, w_up, w_down)
    dqkv_in = backward_call(pk, da_in, lse, ot)
    up_sum, out_sum, down_sum = mid_sums_call(grads)
    dx, qkv_sum, gain1_sum, gain2_sum, _ = last_call(dqkv_in, frames, dx1, gain1, gain2_grad, w_qkv)
    return (y, dx, gain1_sum[0, 0:8], qkv_sum, out_sum, gain2_sum[0, 0:8], up_sum, down_sum)


def solution(mesh):
    return jax.shard_map(
        shards,
        mesh=mesh,
        in_specs=(
            P("row", "seq", None),
            P("row", "seq"),
            P(),
            P(),
            P(),
            P(),
            P(),
            P(),
            P("row", "seq", None),
        ),
        out_specs=(
            P("row", "seq", None),
            P("row", "seq", None),
            P(("seq", "row")),
            P(("seq", "row"), None),
            P(("seq", "row"), None),
            P(("seq", "row")),
            P(("seq", "row"), None),
            P(("seq", "row"), None),
        ),
        check_vma=False,
    )
```

time: 4700 us -> 273 us (0.06)
  waiting for transfers between devices: 2400 us -> 0 us
  starting transfers between devices: 1240 us -> 0 us
  matrix products: 474 us -> 0 us
  Pallas kernels: 0 us -> 265 us
  local copies, waits for them, and re-layouts: 234 us -> 7.19 us
  other arithmetic: 196 us -> 0 us
  blocking collectives: 109 us -> 0 us
    reduce_scatter x4 -> x0, waiting for transfers between devices: 1890 us -> none  [the longest x1 666 us: shards(): lax.psum_scatter(down_part, ('seq', 'row'), scatter_dimension=0, tiled=True)]
    ppermute x250 -> x0, starting transfers between devices: 1240 us -> none  [the longest x186 981 us: shifted(): lax.ppermute(value, axis, [(source, source + steps) for source in range(l...]
    ppermute x250 -> x0, waiting for transfers between devices: 508 us -> none  [the longest x186 476 us: shifted(): lax.ppermute(value, axis, [(source, source + steps) for source in range(l...]
    dot_general x236 -> x0, matrix products: 474 us -> none  [the longest x32 88.7 us: release(): jnp.einsum('hqk,khd->qhd', grad_s, heads_k, preferred_element_type=f32)]
    pallas_call x0 -> x6, Pallas kernels: none -> 265 us  [the longest x1 65.4 us: mid_sums_call(): pl.pallas_call(mid_sums_kernel, name='sum_mid_grads', out_shape=MID_OUT,...]
    while x837 -> x0, local copies, waits for them, and re-layouts: 221 us -> none
    convert_element_type x65 -> x0, other arithmetic: 137 us -> none  [the longest x31 66.2 us: pass_grads(): from_behind(value_acc.astype(jnp.bfloat16), 'seq', 1)]
    unnamed x1 -> x0, blocking collectives: 109 us -> none
  transfers between devices with their start and end apart: 254 -> 0, of which waited for: 78 -> 0; matrix products, arithmetic and copies ran while one was open for 16% -> 0% of each run, Pallas kernels for 0% -> 0%
where the time goes in v1:
time: 273 us
  Pallas kernels  265 us (97%)
  local copies, waits for them, and re-layouts  7.19 us (3%)
    pallas_call x1, Pallas kernels, mid_sums_call(): pl.pallas_call(mid_sums_kernel, name='sum_mid_grads', out_shape=MID_OUT,...  65.4 us
    pallas_call x1, Pallas kernels, backward_call(): pl.pallas_call(backward_kernel, name='attention_grad', out_shape=jax.Shap...  54.9 us
    pallas_call x1, Pallas kernels, last_call(): pl.pallas_call(last_kernel, name='input_grad', out_shape=(jax.ShapeDtypeS...  41.8 us
    pallas_call x1, Pallas kernels, forward_call(): pl.pallas_call(forward_kernel, name='attention', out_shape=(jax.ShapeDtyp...  41.6 us
    pallas_call x1, Pallas kernels, middle_call(): pl.pallas_call(middle_kernel, name='feed_forward', out_shape=(jax.ShapeDt...  31.1 us
    pallas_call x1, Pallas kernels, qkv_call(): pl.pallas_call(qkv_kernel, name='qkv_to_heads', out_shape=jax.ShapeDtypeS...  30.1 us
    unnamed x14, local copies, waits for them, and re-layouts  5.99 us

profile of v1, /device:TPU:1, one launch (start us, length us, event | category | flops | bytes accessed | tf_op | source)
XLA Modules:
  0.0 272.8 jit_solution(549254210617404837)
XLA Ops:
  0.6 30.1 %qkv_to_heads.1.pk_ref = bf16[32,304,128]{2,1,0:T(8,128)(2,1)} custom-call(bf16[1,192,1024]{2,1,0:T(8,128)(2,1)} %x_ref.5, s32[1,192]{1,0:T(1,128)} %seg_ref.1, f32[1,1024]{1,0:T(1,128)} %bitcast.6, bf16[1024,3072]{1,0:T(8,128)(2,1)} %w_ref.3), custom_call_target="tpu_custom_call" | custom-call | tf_op jit(solution)/shard_map/qkv_to_heads/pallas_call | solution.py:215
  30.7 41.6 %attention.1 = (bf16[16,96,128]{2,1,0:T(8,128)(2,1)}, f32[4,1,768]{2,1,0:T(1,128)}, f32[4,64,768]{2,1,0:T(8,128)}) custom-call(bf16[32,304,128]{2,1,0:T(8,128)(2,1)} %qkv_to_heads.1.pk_ref), custom_call_target="tpu_custom_call" | custom-call | tf_op jit(solution)/shard_map/attention/pallas_call | solution.py:371
  72.4 31.1 %feed_forward.1 = (bf16[1,192,1024]{2,1,0:T(8,128)(2,1)}, bf16[18,64,16,256]{3,2,1,0:T(8,128)(2,1)}, f32[192,1024]{1,0:T(8,128)}, f32[1,1024]{1,0:T(1,128)}, bf16[16,96,128]{2,1,0:T(8,128)(2,1)}) custom-call(bf16[16,96,128]{2,1,0:T(8,128)(2,1)} %get-tuple-element.23.o_in, bf16[1,192,1024]{2,1,0:T(8,128)(2,1)} %x_ref.5, bf16[1,192,1024]{2,1,0:T(8,128)(2,1)} %dy_ref.1, ...), custom_call_target="tpu_custom_call" | custom-call | tf_op jit(solution)/shard_map/feed_forward/pallas_call | solution.py:788
  103.5 54.9 %attention_grad.1.dqkv_in = bf16[16,288,128]{2,1,0:T(8,128)(2,1)} custom-call(bf16[32,304,128]{2,1,0:T(8,128)(2,1)} %qkv_to_heads.1.pk_ref, bf16[16,96,128]{2,1,0:T(8,128)(2,1)} %get-tuple-element.25.da_ref, f32[4,1,768]{2,1,0:T(1,128)} %get-tuple-element.26.lse_ref, f32[4,64,768]{2,1,0:T(8,128)} %get-tuple-element.27.ot_ref), custom_call_target="tpu_custom_call" | custom-call | tf_op jit(solution)/shard_map/attention_grad/pallas_call | solution.py:928
  158.4 65.4 %sum_mid_grads.1 = (f32[8,4096]{1,0:T(8,128)}, f32[8,1024]{1,0:T(8,128)}, f32[32,1024]{1,0:T(8,128)}) custom-call(bf16[18,64,16,256]{3,2,1,0:T(8,128)(2,1)} %get-tuple-element.33.grads), custom_call_target="tpu_custom_call" | custom-call | tf_op jit(solution)/shard_map/sum_mid_grads/pallas_call | solution.py:626
  223.8 0.0 copy-start
  223.8 0.0 copy-start.3
  223.8 0.0 copy-start.2
  223.8 0.0 copy-start.1
  223.8 41.8 %input_grad.1 = (bf16[1,192,1024]{2,1,0:T(8,128)(2,1)}, f32[8,3072]{1,0:T(8,128)}, f32[1,128]{1,0:T(1,128)}, f32[1,128]{1,0:T(1,128)}, bf16[6,64,16,256]{3,2,1,0:T(8,128)(2,1)}) custom-call(bf16[16,288,128]{2,1,0:T(8,128)(2,1)} %attention_grad.1.dqkv_in, bf16[1,192,1024]{2,1,0:T(8,128)(2,1)} %x_ref.5, f32[192,1024]{1,0:T(8,128)} %get-tuple-element.28.dx1_ref, ...), custom_call_target="tpu_custom_call" | custom-call | tf_op jit(solution)/shard_map/input_grad/pallas_call | solution.py:1081
  265.6 1.2 slice_bitcast_fusion
  266.8 0.0 copy-done
  266.8 0.7 copy.23
  267.6 1.8 copy.24
  269.4 1.5 copy.25
  270.9 0.0 copy-done.3
  270.9 0.6 copy.26
  271.5 0.0 copy-done.2
  271.5 0.7 copy.27
  272.2 0.0 copy-done.1
  272.2 0.7 copy.28
Async XLA Ops:
  223.8 43.0 %copy-start = (bf16[1,192,1024]{2,1,0:T(8,128)(2,1)S(1)}, bf16[1,192,1024]{2,1,0:T(8,128)(2,1)}, u32[]{:S(2)}) copy-start(bf16[1,192,1024]{2,1,0:T(8,128)(2,1)} %get-tuple-element.48) | copy-start | bytes 1179652
  223.8 47.1 %copy-start.3 = (f32[8,1024]{1,0:T(8,128)S(1)}, f32[8,1024]{1,0:T(8,128)}, u32[]{:S(2)}) copy-start(f32[8,1024]{1,0:T(8,128)} %get-tuple-element.52) | copy-start | bytes 98308
  223.8 47.7 %copy-start.2 = (f32[8,4096]{1,0:T(8,128)S(1)}, f32[8,4096]{1,0:T(8,128)}, u32[]{:S(2)}) copy-start(f32[8,4096]{1,0:T(8,128)} %get-tuple-element.54) | copy-start | bytes 393220
  223.8 48.3 %copy-start.1 = (f32[32,1024]{1,0:T(8,128)S(1)}, f32[32,1024]{1,0:T(8,128)}, u32[]{:S(2)}) copy-start(f32[32,1024]{1,0:T(8,128)} %get-tuple-element.55) | copy-start | bytes 393220

commit v2 on v1

v2 whole, which is shorter than its diff:
```python
import functools
import math

import jax
import jax.numpy as jnp
from jax import lax
from jax.experimental import pallas as pl
from jax.experimental.pallas import tpu as pltpu
from jax.sharding import PartitionSpec as P

MESH = pl.DeviceIdType.MESH
f32 = jnp.float32
bf16 = jnp.bfloat16

D = 1024
H = 16
HD = 64
FF = 4096
T = 192
HT = T // 2
BLOCKS = 32
TILE = 768
TILES = 8
PACK = 304
GRAD = 288
EPS = 1e-05
NEG = -1e30
LOG2E = math.log2(math.e)
LN2 = math.log(2.0)
SCALE = HD**-0.5
VMEM_LIMIT = 60 * 1024 * 1024

ANY = pl.BlockSpec(memory_space=pl.ANY)
VM = pl.BlockSpec(memory_space=pltpu.VMEM)


def dot(a, b):
    return jnp.dot(a, b, preferred_element_type=f32)


def dot_nt(a, b):
    return lax.dot_general(a, b, (((1,), (1,)), ((), ())), preferred_element_type=f32)


def transposed(v):
    return v.astype(f32).T.astype(bf16)


def swap_halves(first, second):
    lane = lax.broadcasted_iota(jnp.int32, first.shape, 1)
    low = lane < HD
    first, second = first.astype(f32), second.astype(f32)
    return (
        jnp.where(low, first, pltpu.roll(second, HD, 1)).astype(bf16),
        jnp.where(low, pltpu.roll(first, HD, 1), second).astype(bf16),
    )


class Place:
    def __init__(self):
        self.s = lax.axis_index("seq")
        self.r = lax.axis_index("row")
        self.y_lo = lax.div(self.s, 16)
        self.head = lax.rem(self.s, 16)
        self.y_hi = lax.div(self.r, 2)
        self.core = lax.rem(self.r, 2)
        tile = lax.div(self.s, 4)
        self.block_core = lax.rem(lax.div(tile + 1, 2), 2)
        self.slot = lax.div(self.s, 8) * 4 + lax.rem(self.s, 4)
        self.partner = (self.s, self.r + 1 - 2 * self.core)
        self.self_served = jnp.logical_and(self.y_lo == self.core, self.block_core == self.core)
        self.self_count = jnp.where(self.self_served, 1, 0)

    def head_device(self, h):
        return (self.core * 16 + h, self.y_hi * 2 + self.block_core)

    def own_tile(self, j, core=None):
        core = self.core if core is None else core
        return 2 * j + lax.rem(j + core, 2)

    def own_block(self, n):
        return self.own_tile(lax.div(n, 4)) * 4 + lax.rem(n, 4)

    def block_device(self, n):
        return (self.own_block(n), self.y_hi * 2 + self.y_lo)

    def is_self(self, device):
        return jnp.logical_and(device[0] == self.s, device[1] == self.r)


def remote(src, dst, send, recv, device):
    return pltpu.make_async_remote_copy(
        src_ref=src, dst_ref=dst, send_sem=send, recv_sem=recv, device_id=device, device_id_type=MESH
    )


def send_to(place, src, dst, send, recv, device):
    own = place.is_self(device)

    @pl.when(own)
    def _():
        pltpu.make_async_copy(src, dst, recv).start()

    @pl.when(jnp.logical_not(own))
    def _():
        remote(src, dst, send, recv, device).start()


def sent_to(place, src, dst, send, recv, device):
    @pl.when(jnp.logical_not(place.is_self(device)))
    def _():
        remote(src, dst, send, recv, device).wait_send()


def arrived(dst, recv):
    pltpu.make_async_copy(dst, dst, recv).wait()


def greet(barrier, device):
    pl.semaphore_signal(barrier, inc=1, device_id=device, device_id_type=MESH)


def greet_all(place, barrier, device_of):
    def one(n, carry):
        device = device_of(n)

        @pl.when(jnp.logical_not(place.is_self(device)))
        def _():
            greet(barrier, device)

        return carry

    lax.fori_loop(0, 16, one, 0)


def loop(count, body):
    def one(n, carry):
        body(n)
        return carry

    lax.fori_loop(0, count, one, 0)


def params(collective_id):
    return pltpu.CompilerParams(
        collective_id=collective_id, has_side_effects=True, vmem_limit_bytes=VMEM_LIMIT
    )


def qkv_kernel(x_ref, seg_ref, gain_ref, w_ref, pk_ref, w_scr, stage, w_sem, send, recv, fsend, frecv):
    place = Place()

    def weight(g, part):
        return pltpu.make_async_copy(
            w_ref.at[:, pl.ds(part * D + g * 256, 256)], w_scr.at[g, part], w_sem.at[g, part]
        )

    for g in range(4):
        for part in range(3):
            weight(g, part).start()
    barrier = pltpu.get_barrier_semaphore()
    greet_all(place, barrier, place.block_device)
    greet(barrier, place.partner)

    x = x_ref[0].astype(f32)
    a = (x * lax.rsqrt(jnp.mean(x * x, axis=-1, keepdims=True) + EPS) * gain_ref[...]).astype(bf16)
    seg = seg_ref[...].astype(f32)
    row = lax.broadcasted_iota(jnp.int32, (16, 128), 0)
    rest = jnp.concatenate([seg[:, 128:T], jnp.zeros((1, 256 - T), f32)], axis=1)
    seg_tile = jnp.where(row == 0, seg[:, :128], jnp.where(row == 1, rest, 0.0)).astype(bf16)
    pl.semaphore_wait(barrier, 17 - place.self_count)

    for g in range(4):
        for part in range(3):
            weight(g, part).wait()
        q = dot(a, w_scr[g, 0]) * (SCALE * LOG2E)
        k = dot(a, w_scr[g, 1])
        v = dot(a, w_scr[g, 2])
        for m in range(2):
            lanes = slice(128 * m, 128 * m + 128)
            h = 4 * g + 2 * m
            kv = swap_halves(k[:, lanes].astype(bf16), v[:, lanes].astype(bf16))
            qq = q[:, lanes].astype(bf16)
            qp = swap_halves(qq[:HT], qq[HT:])
            for e in range(2):
                stage[h + e, 0:T] = kv[e]
                stage[h + e, T : T + HT] = qp[e]
                stage[h + e, T + HT : PACK] = seg_tile
                send_to(
                    place, stage.at[h + e], pk_ref.at[place.s], send.at[h + e], recv.at[place.slot],
                    place.head_device(h + e),
                )

    def forward(n):
        i = place.own_block(n)
        return remote(pk_ref.at[i], pk_ref.at[i], fsend.at[n], frecv.at[n], place.partner)

    def pass_on(n):
        arrived(pk_ref.at[place.own_block(n)], recv.at[n])
        forward(n).start()

    loop(16, pass_on)

    def finish(n):
        sent_to(
            place, stage.at[n], pk_ref.at[place.s], send.at[n], recv.at[place.slot], place.head_device(n)
        )
        forward(n).wait_send()
        forward(n).wait_recv()

    loop(16, finish)


def qkv_call(frames, segment_ids, gain, w_qkv):
    return pl.pallas_call(
        qkv_kernel,
        name="qkv_to_heads",
        out_shape=jax.ShapeDtypeStruct((BLOCKS, PACK, 128), bf16),
        in_specs=[VM, VM, VM, ANY],
        out_specs=ANY,
        scratch_shapes=[
            pltpu.VMEM((4, 3, D, 256), bf16),
            pltpu.VMEM((16, PACK, 128), bf16),
            pltpu.SemaphoreType.DMA((4, 3)),
            pltpu.SemaphoreType.DMA((16,)),
            pltpu.SemaphoreType.DMA((16,)),
            pltpu.SemaphoreType.DMA((16,)),
            pltpu.SemaphoreType.DMA((16,)),
        ],
        compiler_params=params(0),
    )(frames, segment_ids, gain, w_qkv)


def seg_column(pk_ref, block):
    tile = pk_ref[block, T + HT : PACK].astype(f32)
    return jnp.concatenate(
        [
            jnp.broadcast_to(tile[0:1], (128, 128)).T,
            jnp.broadcast_to(tile[1:2], (128, 128)).T[: T - 128],
        ],
        axis=0,
    )


def fill_segments(pk_ref, seg):
    first = seg_column(pk_ref, 0)
    last = seg_column(pk_ref, BLOCKS - 1)
    common = jnp.broadcast_to(first[T - 1 : T], (TILE, 128))
    seg[0] = common
    seg[1] = common
    seg[2] = common
    seg[0, 0:T] = first
    seg[2, TILE - T : TILE] = last


def seg_kind(tile):
    return jnp.where(tile == 0, 0, jnp.where(tile == TILES - 1, 2, 1))


def fill_operands(place, pk_ref, seg, keys, queries):
    fill_segments(pk_ref, seg)
    lane = lax.broadcasted_iota(jnp.int32, (TILE, 128), 1)
    number = lane.astype(f32)

    def key_tile(t):
        keys[t, :, 0:128] = load_keys(pk_ref, t)
        keys[t, :, 128:256] = jnp.where(seg[seg_kind(t)] == number, 1.0, 0.0).astype(bf16)

    loop(TILES, key_tile)
    low = lax.broadcasted_iota(jnp.int32, (HT, 128), 1) < HD

    def query_tile(j):
        tile = place.own_tile(j)
        for b in range(4):
            packed = pk_ref[tile * 4 + b, T : T + HT].astype(f32)
            queries[j, b * T : b * T + HT, 0:128] = jnp.where(low, packed, 0.0).astype(bf16)
            queries[j, b * T + HT : b * T + T, 0:128] = jnp.where(low, pltpu.roll(packed, HD, 1), 0.0).astype(bf16)
        other = jnp.logical_and(lane < 8, seg[seg_kind(tile)] != number)
        queries[j, :, 128:256] = jnp.where(other, NEG, 0.0).astype(bf16)

    loop(4, query_tile)


STEPS = 18
HOOKS = (6, 8, 10, 12, 14, 16, 17)


def walk(place, n):
    turn = lax.div(place.head, 4)
    j, start, end = lax.rem(turn, 4), 0, 0
    end = place.own_tile(j) + 1
    for k in range(1, 4):
        past = n >= end
        following = lax.rem(turn + k, 4)
        j = jnp.where(past, following, j)
        start = jnp.where(past, end, start)
        end = jnp.where(past, end + place.own_tile(following) + 1, end)
    at = n - start
    k_tile = jnp.where(at == 0, place.own_tile(j), at - 1)
    return j, k_tile, at == 0, n + 1 == end


def key_order(place, i):
    turn = lax.div(place.head, 4)
    return jnp.where(i == 7, 0, 7 - lax.rem(i + 2 * turn, 7))


def causal(scores):
    k = lax.broadcasted_iota(jnp.int32, scores.shape, 0)
    q = lax.broadcasted_iota(jnp.int32, scores.shape, 1)
    return jnp.where(k <= q, scores, NEG)


def load_keys(pk_ref, tile):
    return pk_ref[pl.ds(tile * 4, 4), 0:T].reshape(TILE, 128)


def pack_transposed(value_t):
    both = jnp.concatenate([value_t, value_t], axis=0).T
    lane = lax.broadcasted_iota(jnp.int32, (HT, 128), 1)
    return [
        jnp.where(lane < HD, both[b * T : b * T + HT], both[b * T + HT : b * T + T]).astype(bf16)
        for b in range(4)
    ]


def forward_kernel(
    pk_ref, o_in, lse_ref, ot_ref, seg, keys, queries, vt, top, acc, even, odd, stage, send, recv
):
    place = Place()
    barrier = pltpu.get_barrier_semaphore()
    greet_all(place, barrier, place.head_device)
    fill_operands(place, pk_ref, seg, keys, queries)
    one = jnp.where(lax.broadcasted_iota(jnp.int32, (16, TILE), 0) == 0, 1.0, 0.0).astype(bf16)

    def prepare(t):
        vt[t, 0:HD] = transposed(keys[t, :, 0:128])[HD:]
        vt[t, HD : HD + 16] = one

    loop(TILES, prepare)
    pl.semaphore_wait(barrier, 16 - place.self_count)

    def score(n, scores):
        j, k_tile, _, _ = walk(place, jnp.minimum(n, STEPS - 1))
        scores[...] = dot_nt(keys[k_tile], queries[j])

    def body(n, now, later):
        j, k_tile, first, last = walk(place, n)

        @pl.when(first)
        def _():
            score(n + 1, later)
            scores = causal(now[...])
            peak = jnp.max(scores, axis=0, keepdims=True)
            top[...] = peak
            acc[...] = dot(vt[k_tile], jnp.exp2(scores - peak).astype(bf16))

        @pl.when(jnp.logical_not(first))
        def _():
            score(n + 1, later)
            scores = now[...]
            peak = jnp.maximum(top[...], jnp.max(scores, axis=0, keepdims=True))
            fade = jnp.exp2(top[...] - peak)
            top[...] = peak
            acc[...] = acc[...] * fade + dot(vt[k_tile], jnp.exp2(scores - peak).astype(bf16))

        @pl.when(last)
        def _():
            total = acc[HD : HD + 1]
            out_t = acc[0:HD] / total
            lse_ref[j] = top[...] + jnp.log2(total)
            ot_ref[j] = out_t
            packed = pack_transposed(out_t)
            for b in range(4):
                m = j * 4 + b
                stage[m] = packed[b]
                send_to(
                    place, stage.at[m], o_in.at[place.head], send.at[m], recv.at[place.head],
                    place.block_device(m),
                )

    score(0, even)

    def pair(i):
        body(2 * i, even, odd)
        body(2 * i + 1, odd, even)

    loop(STEPS // 2, pair)

    def finish(n):
        sent_to(
            place, stage.at[n], o_in.at[place.head], send.at[n], recv.at[place.head], place.block_device(n)
        )
        arrived(o_in.at[n], recv.at[n])

    loop(16, finish)


def forward_call(pk):
    return pl.pallas_call(
        forward_kernel,
        name="attention",
        out_shape=(
            jax.ShapeDtypeStruct((16, HT, 128), bf16),
            jax.ShapeDtypeStruct((4, 1, TILE), f32),
            jax.ShapeDtypeStruct((4, HD, TILE), f32),
        ),
        in_specs=[VM],
        out_specs=(ANY, VM, VM),
        scratch_shapes=[
            pltpu.VMEM((3, TILE, 128), f32),
            pltpu.VMEM((TILES, TILE, 256), bf16),
            pltpu.VMEM((4, TILE, 256), bf16),
            pltpu.VMEM((TILES, HD + 16, TILE), bf16),
            pltpu.VMEM((1, TILE), f32),
            pltpu.VMEM((HD + 16, TILE), f32),
            pltpu.VMEM((TILE, TILE), f32),
            pltpu.VMEM((TILE, TILE), f32),
            pltpu.VMEM((16, HT, 128), bf16),
            pltpu.SemaphoreType.DMA((16,)),
            pltpu.SemaphoreType.DMA((16,)),
        ],
        compiler_params=params(1),
    )(pk)


FIRST = lambda c: ((c + 1) // 2) % 2
SECOND = lambda c: c // 2


def chip_bits(x, y, z):
    return [FIRST(x), FIRST(y), FIRST(z), SECOND(x), SECOND(y), SECOND(z)]


def position(part, y_lo, x, z, y_hi):
    bits = chip_bits(x, y_hi * 2 + y_lo, z)
    at = 0
    for k in range(6):
        at = at * 2 + bits[(part + k) % 6]
    return at


class Part:
    def __init__(self, net, acc, land, at, count, turn, first, send, recv):
        self.net, self.acc, self.land, self.turn, self.first = net, acc, land, turn, first
        self.units = pl.ds(at, count)
        self.count, self.send, self.recv = count, send, recv

    def bit(self, stage):
        return self.net.bits[(self.turn + stage) % 6]

    def base(self, stage):
        at = 0
        for k in range(self.first, stage + 1):
            at = at + self.bit(k) * (32 >> k)
        return at

    def landing(self, stage):
        return sum(32 >> k for k in range(self.first, stage))

    def hop(self, stage):
        half = 32 >> stage
        base = self.base(stage - 1) + (1 - self.bit(stage)) * half
        return remote(
            self.acc.at[self.units, pl.ds(base, half)],
            self.land.at[self.units, pl.ds(self.landing(stage), half)],
            self.send[0].at[self.send[1], stage],
            self.recv[0].at[self.recv[1], stage],
            self.net.neighbours[(self.turn + stage) % 6],
        )

    def start(self):
        self.hop(self.first).start()

    def add(self, base, landed, count):
        group = min(count, 4)

        def body(i):
            here = pl.ds(base + i * group, group)
            there = pl.ds(landed + i * group, group)
            total = self.acc[self.units, here].astype(f32) + self.land[self.units, there].astype(f32)
            self.acc[self.units, here] = total.astype(bf16)

        loop(count // group, body)

    def advance(self, stage):
        self.hop(stage).wait_recv()
        half = 16 >> stage
        base, landed = self.base(stage), self.landing(stage)
        bit = self.bit(stage + 1)
        self.add(base + (1 - bit) * half, landed + (1 - bit) * half, half)
        self.hop(stage + 1).start()
        self.add(base + bit * half, landed + bit * half, half)

    def last(self):
        self.hop(5).wait_recv()
        return (
            self.acc[self.units, pl.ds(self.base(5), 1)].astype(f32)
            + self.land[self.units, pl.ds(self.landing(5), 1)].astype(f32)
        )[:, 0]

    def finish(self):
        for stage in range(self.first, 6):
            self.hop(stage).wait_send()


class Net:
    def __init__(self, place):
        x, z = lax.div(place.head, 4), lax.rem(place.head, 4)
        y = place.y_hi * 2 + place.y_lo
        self.bits = [
            lax.rem(lax.div(x + 1, 2), 2), lax.rem(lax.div(y + 1, 2), 2), lax.rem(lax.div(z + 1, 2), 2),
            lax.div(x, 2), lax.div(y, 2), lax.div(z, 2),
        ]

        def device(x, y, z):
            return (lax.rem(y, 2) * 16 + x * 4 + z, lax.div(y, 2) * 2 + place.core)

        flip = lambda c: c + 1 - 2 * lax.rem(c, 2)
        self.neighbours = [
            device(flip(x), y, z), device(x, flip(y), z), device(x, y, flip(z)),
            device(3 - x, y, z), device(x, 3 - y, z), device(x, y, 3 - z),
        ]

    def greet(self, barrier):
        for device in self.neighbours:
            greet(barrier, device)


TURN = [u % 6 for u in range(18)]
COUNTS = [3, 3, 3, 3, 2, 2]
STARTS = [0, 3, 6, 9, 12, 14]
SLOT = [STARTS[u % 6] + u // 6 for u in range(16)]
FINAL = list(range(8)) + [10 + (v % 4) * 2 + v // 4 for v in range(8)] + [8, 9]


class MidSums:
    def __init__(self, place, fin, side, down, sem, up_out, out_out, down_out):
        self.place, self.fin, self.side, self.down, self.sem = place, fin, side, down, sem
        self.up_out, self.out_out, self.down_out = up_out, out_out, down_out

    def targets(self):
        return [(self.place.core * 16 + self.place.head, self.place.y_hi * 2 + k) for k in range(2)]

    def sources(self):
        return [(m * 16 + self.place.head, self.place.y_hi * 2 + self.place.y_lo) for m in range(2)]

    def self_count(self):
        return jnp.where(self.place.y_lo == self.place.core, 1, 0)

    def greet(self, barrier):
        greet(barrier, self.place.partner)
        for device in self.sources():

            @pl.when(jnp.logical_not(self.place.is_self(device)))
            def _(device=device):
                greet(barrier, device)

    def greetings(self):
        return 3 - self.self_count()

    def store(self, unit, value):
        self.fin[FINAL[unit]] = value.reshape(2, 8, 256)

    def aside(self):
        return remote(
            self.fin.at[0:10, 1 - self.place.core], self.side, self.sem.at[0], self.sem.at[1], self.place.partner
        )

    def down_hop(self, k):
        return (
            self.fin.at[10 + 4 * k : 14 + 4 * k],
            self.down.at[self.place.y_lo],
            self.sem.at[2 + k],
            self.sem.at[4 + self.place.y_lo],
            self.targets()[k],
        )

    def start(self):
        self.aside().start()
        for k in range(2):
            send_to(self.place, *self.down_hop(k))

    def finish(self):
        place = self.place
        self.aside().wait_recv()
        mine, other = place.core, 1 - place.core
        for u in range(8):
            self.up_out[:, pl.ds(mine * 2048 + u * 256, 256)] = self.fin[u, mine]
            self.up_out[:, pl.ds(other * 2048 + u * 256, 256)] = self.side[u]
        for u in range(2):
            self.out_out[:, pl.ds(mine * 512 + u * 256, 256)] = self.fin[8 + u, mine]
            self.out_out[:, pl.ds(other * 512 + u * 256, 256)] = self.side[8 + u]
        for m in range(2):
            arrived(self.down.at[m], self.sem.at[4 + m])
            for v in range(4):
                group, half = v // 2, v % 2
                self.down_out[group * 16 : group * 16 + 16, m * 512 + half * 256 : m * 512 + half * 256 + 256] = (
                    self.down[m, v].reshape(16, 256)
                )
        self.aside().wait_send()
        for k in range(2):
            sent_to(place, *self.down_hop(k))


MID_OUT = (
    jax.ShapeDtypeStruct((8, FF), f32),
    jax.ShapeDtypeStruct((8, D), f32),
    jax.ShapeDtypeStruct((32, D), f32),
)
MID_SCRATCH = [
    pltpu.VMEM((18, 2, 8, 256), f32),
    pltpu.VMEM((10, 8, 256), f32),
    pltpu.VMEM((2, 4, 2, 8, 256), f32),
    pltpu.SemaphoreType.DMA((6,)),
]


def spread(target, unit_slot, turn, block):
    for chip in range(64):
        y_lo, x, z, y_hi = chip // 32, chip // 8 % 4, chip // 2 % 4, chip % 2
        target[unit_slot, position(turn, y_lo, x, z, y_hi)] = block[chip * 16 : chip * 16 + 16]


ROOT = math.sqrt(2.0 / math.pi)
CUBE = 0.044715


def middle_kernel(
    o_in, x_ref, dy_ref, gain_ref, w_out, w_up, w_down,
    y_ref, grads, out_grads, dx1_ref, gain_grad, da_in,
    wo, wu, wd, o2, b2, dm2, b2t, gzt, x1s, ysum, hsum, yside, hside, da_side, gs, land, outg, stage,
    w_sem, p_send, p_recv, g_sem, h_send, h_recv, send, recv,
):
    place = Place()
    core = place.core
    net = Net(place)

    def up_copy(j):
        at = pl.multiple_of(core * 2048 + j * 512, 512)
        return pltpu.make_async_copy(w_up.at[:, pl.ds(at, 512)], wu.at[j], w_sem.at[1 + j])

    def down_copy(j):
        at = pl.multiple_of(core * 2048 + j * 512, 512)
        return pltpu.make_async_copy(w_down.at[pl.ds(at, 512)], wd.at[j], w_sem.at[5 + j])

    out_copy = pltpu.make_async_copy(w_out, wo, w_sem.at[0])
    out_copy.start()
    for j in range(4):
        up_copy(j).start()
        down_copy(j).start()
    barrier = pltpu.get_barrier_semaphore()
    greet_all(place, barrier, place.block_device)
    greet(barrier, place.partner)
    net.greet(barrier)

    def across(k, src, dst):
        return remote(src, dst, p_send.at[k], p_recv.at[k], place.partner)

    def first_hop(unit):
        bit = net.bits[TURN[unit]]
        return remote(
            gs.at[SLOT[unit], pl.ds((1 - bit) * 32, 32)], land.at[SLOT[unit]],
            h_send.at[unit], h_recv.at[unit], net.neighbours[TURN[unit]],
        )

    dm2[0:T] = dy_ref[0]
    for m in range(8):
        lo, hi = swap_halves(o_in[2 * m], o_in[2 * m + 1])
        o2[0:HT, 128 * m : 128 * m + 128] = lo
        o2[HT:T, 128 * m : 128 * m + 128] = hi
    pl.semaphore_wait(barrier, 23 - place.self_count)
    dm_hop = across(0, dm2.at[0:T], dm2.at[T : 2 * T])
    o_hop = across(1, o2.at[0:T], o2.at[T : 2 * T])
    dm_hop.start()
    o_hop.start()
    out_copy.wait()
    x1 = x_ref[0].astype(f32) + dot(o2[0:T], wo[...])
    x1s[...] = x1
    scale1 = lax.rsqrt(jnp.mean(x1 * x1, axis=-1, keepdims=True) + EPS)
    b2[0:T] = (x1 * scale1 * gain_ref[...]).astype(bf16)
    b_hop = across(2, b2.at[0:T], b2.at[T : 2 * T])
    b_hop.start()
    dm_hop.wait_recv()
    b_hop.wait_recv()
    b2t[...] = transposed(b2[...])

    for j in range(4):
        up_copy(j).wait()
        down_copy(j).wait()
        z = dot(b2[...], wu[j])
        zz = z * z
        th = jnp.tanh(ROOT * z * (1.0 + CUBE * zz))
        half = 0.5 * (1.0 + th)
        gz = (z * half).astype(bf16)
        slope = half + 0.5 * z * (1.0 - th * th) * (ROOT * (1.0 + 3.0 * CUBE * zz))
        dz = (dot_nt(dm2[...], wd[j]) * slope).astype(bf16)
        gzt[j * 512 : (j + 1) * 512] = transposed(gz)
        yj = dot(gz, wd[j])
        hj = dot_nt(dz, wu[j])
        if j == 0:
            ysum[...] = yj
            hsum[...] = hj
        else:
            ysum[...] += yj
            hsum[...] += hj
        up = dot(b2t[...], dz).astype(bf16)
        for u in range(2):
            unit = 2 * j + u
            spread(gs, SLOT[unit], TURN[unit], up[:, u * 256 : u * 256 + 256])
            first_hop(unit).start()

    y_hop = across(3, ysum.at[T : 2 * T], yside)
    h_hop = across(4, hsum.at[T : 2 * T], hside)
    h_hop.start()
    y_hop.start()

    def down_units(u):
        for y_lo in range(2):
            at = y_lo * 512 + u * 256
            down = dot(gzt[...], dm2[:, at : at + 256]).astype(bf16)
            for owner in range(32):
                for group in range(4):
                    unit = 8 + u * 4 + group
                    place_at = position(TURN[unit], y_lo, owner // 8, owner // 2 % 4, owner % 2)
                    gs[SLOT[unit], place_at] = down[owner * 64 + group * 16 : owner * 64 + group * 16 + 16]
        for group in range(4):
            first_hop(8 + u * 4 + group).start()

    down_units(0)
    h_hop.wait_recv()
    x1 = x1s[...]
    scale1 = lax.rsqrt(jnp.mean(x1 * x1, axis=-1, keepdims=True) + EPS)
    dh2 = hsum[0:T] + hside[...]
    gain_grad[...] = jnp.sum(dh2 * x1 * scale1, axis=0, keepdims=True)
    dn = dh2 * gain_ref[...]
    back = scale1 * dn - x1 * (scale1 * scale1 * scale1) * jnp.mean(dn * x1, axis=-1, keepdims=True)
    dx1 = dy_ref[0].astype(f32) + back
    dx1_ref[...] = dx1
    da = dx1.astype(bf16)
    da_side[0, 0:T] = da[:, 0:512]
    da_side[1, 0:T] = da[:, 512:1024]
    da_hop = across(5, da_side.at[1 - core, 0:T], da_side.at[1 - core, T : 2 * T])
    da_hop.start()
    for g in range(4):
        dattn = dot_nt(da, wo[256 * g : 256 * g + 256]).astype(bf16)
        for m in range(2):
            tile = dattn[:, 128 * m : 128 * m + 128]
            packed = swap_halves(tile[:HT], tile[HT:])
            for e in range(2):
                h = 4 * g + 2 * m + e
                stage[h] = packed[e]
                send_to(
                    place, stage.at[h], da_in.at[place.slot], send.at[h], recv.at[place.slot],
                    place.head_device(h),
                )
    down_units(1)
    y_hop.wait_recv()
    y_ref[0] = (x1 + ysum[0:T] + yside[...]).astype(bf16)
    o_hop.wait_recv()
    da_hop.wait_recv()
    out = dot(transposed(o2[...]), da_side[core]).astype(bf16)
    for u in range(2):
        spread(outg, u, TURN[16 + u], out[:, u * 256 : u * 256 + 256])
    out_move = pltpu.make_async_copy(outg, out_grads, g_sem.at[16])
    out_move.start()

    def kept(unit):
        return pltpu.make_async_copy(land.at[SLOT[unit]], grads.at[SLOT[unit]], g_sem.at[unit])

    for unit in range(16):
        first_hop(unit).wait_recv()
        bit = net.bits[TURN[unit]]

        def add(i, unit=unit, bit=bit):
            here = pl.ds(i * 4, 4)
            mine = gs[SLOT[unit], pl.ds(bit * 32 + i * 4, 4)].astype(f32)
            land[SLOT[unit], here] = (land[SLOT[unit], here].astype(f32) + mine).astype(bf16)

        loop(8, add)
        kept(unit).start()

    def finish(n):
        sent_to(
            place, stage.at[n], da_in.at[place.slot], send.at[n], recv.at[place.slot], place.head_device(n)
        )
        arrived(da_in.at[n], recv.at[n])

    loop(16, finish)
    out_move.wait()
    for unit in range(16):
        kept(unit).wait()
        first_hop(unit).wait_send()
    for hop in (dm_hop, o_hop, b_hop, y_hop, h_hop, da_hop):
        hop.wait_send()


def middle_call(o_in, frames, out_grad, gain, w_out, w_up, w_down):
    return pl.pallas_call(
        middle_kernel,
        name="feed_forward",
        out_shape=(
            jax.ShapeDtypeStruct((1, T, D), bf16),
            jax.ShapeDtypeStruct((16, 32, 16, 256), bf16),
            jax.ShapeDtypeStruct((2, 64, 16, 256), bf16),
            jax.ShapeDtypeStruct((T, D), f32),
            jax.ShapeDtypeStruct((1, D), f32),
            jax.ShapeDtypeStruct((16, HT, 128), bf16),
        ),
        in_specs=[VM, VM, VM, VM, ANY, ANY, ANY],
        out_specs=(VM, ANY, ANY, VM, VM, ANY),
        scratch_shapes=[
            pltpu.VMEM((D, D), bf16),
            pltpu.VMEM((4, D, 512), bf16),
            pltpu.VMEM((4, 512, D), bf16),
            pltpu.VMEM((2 * T, D), bf16),
            pltpu.VMEM((2 * T, D), bf16),
            pltpu.VMEM((2 * T, D), bf16),
            pltpu.VMEM((D, 2 * T), bf16),
            pltpu.VMEM((2048, 2 * T), bf16),
            pltpu.VMEM((T, D), f32),
            pltpu.VMEM((2 * T, D), f32),
            pltpu.VMEM((2 * T, D), f32),
            pltpu.VMEM((T, D), f32),
            pltpu.VMEM((T, D), f32),
            pltpu.VMEM((2, 2 * T, 512), bf16),
            pltpu.VMEM((16, 64, 16, 256), bf16),
            pltpu.VMEM((16, 32, 16, 256), bf16),
            pltpu.VMEM((2, 64, 16, 256), bf16),
            pltpu.VMEM((16, HT, 128), bf16),
            pltpu.SemaphoreType.DMA((9,)),
            pltpu.SemaphoreType.DMA((6,)),
            pltpu.SemaphoreType.DMA((6,)),
            pltpu.SemaphoreType.DMA((17,)),
            pltpu.SemaphoreType.DMA((16,)),
            pltpu.SemaphoreType.DMA((16,)),
            pltpu.SemaphoreType.DMA((16,)),
            pltpu.SemaphoreType.DMA((16,)),
        ],
        compiler_params=params(2),
    )(o_in, frames, out_grad, gain, w_out, w_up, w_down)


def backward_kernel(
    pk_ref, da_ref, lse_ref, ot_ref, grads, out_grads,
    dqkv_in, up_out, out_out, down_out,
    seg, keys, queries, kt, gp, delta, dq, dkv, part, landed, stage,
    acc, land, acc2, land2, fin, side, down,
    p_send, p_recv, send, recv, l_sem, h_send, h_recv, m_sem,
):
    place = Place()
    core = place.core
    net = Net(place)
    main = [
        Part(net, acc, land, STARTS[p], COUNTS[p], p, 1, (h_send, p), (h_recv, p)) for p in range(6)
    ]
    outs = [Part(net, acc2, land2, u, 1, TURN[16 + u], 0, (h_send, 6 + u), (h_recv, 6 + u)) for u in range(2)]
    mid = MidSums(place, fin, side, down, m_sem, up_out, out_out, down_out)

    def load(p):
        if p < 6:
            return pltpu.make_async_copy(grads.at[main[p].units], acc.at[main[p].units], l_sem.at[p])
        return pltpu.make_async_copy(out_grads.at[p - 6], acc2.at[p - 6], l_sem.at[p])

    for p in range(8):
        load(p).start()
    barrier = pltpu.get_barrier_semaphore()
    greet_all(place, barrier, place.head_device)
    net.greet(barrier)
    mid.greet(barrier)
    pl.semaphore_wait(barrier, 16 - place.self_count + 6 + mid.greetings())
    for p, sums in enumerate(main + outs):
        load(p).wait()
        sums.start()

    fill_operands(place, pk_ref, seg, keys, queries)

    low = lax.broadcasted_iota(jnp.int32, (HT, 128), 1) < HD

    def prepare(t):
        kt[t] = transposed(keys[t, :, 0:128])[:HD]
        dkv[t] = jnp.zeros((TILE, 128), f32)

    loop(TILES, prepare)

    def prepare_query(j):
        for b in range(4):
            packed = da_ref[j * 4 + b].astype(f32)
            gp[j, b * T : b * T + HT] = jnp.where(low, 0.0, pltpu.roll(packed, HD, 1)).astype(bf16)
            gp[j, b * T + HT : b * T + T] = jnp.where(low, 0.0, packed).astype(bf16)
        delta[j] = jnp.sum(gp[j].astype(f32).T[HD:] * ot_ref[j], axis=0, keepdims=True)
        dq[j] = jnp.zeros((HD, TILE), f32)

    loop(4, prepare_query)
    factor = jnp.where(lax.broadcasted_iota(jnp.int32, (1, 128), 1) < HD, LN2, 1.0)

    def part_hop(j):
        return remote(part.at[j], landed.at[j], p_send.at[j], p_recv.at[j], place.partner)

    def give(j):
        part[j] = (dkv[place.own_tile(j, 1 - core)] * factor).astype(bf16)
        part_hop(j).start()

    def key_hop(m):
        return (
            stage.at[m, 0:T], dqkv_in.at[place.head, 0:T], send.at[0, m], recv.at[0, place.head],
            place.block_device(m),
        )

    def query_hop(m):
        return (
            stage.at[m, T:GRAD], dqkv_in.at[place.head, T:GRAD], send.at[1, m], recv.at[1, place.head],
            place.block_device(m),
        )

    def take(j):
        alone = jnp.logical_and(core == 0, j == 3)

        @pl.when(jnp.logical_not(alone))
        def _():
            part_hop(j).wait_recv()

        total = dkv[place.own_tile(j)] * factor
        total = (total + jnp.where(alone, 0.0, landed[j].astype(f32))).astype(bf16)
        for b in range(4):
            m = j * 4 + b
            stage[m, 0:T] = total[b * T : (b + 1) * T]
            send_to(place, *key_hop(m))

    def step(j, k_tile, diagonal):
        rows = keys[k_tile]
        scores = dot_nt(rows, queries[j])
        if diagonal:
            scores = causal(scores)
        weights = jnp.exp2(scores - lse_ref[j])
        slopes = (weights * (dot_nt(rows[:, 0:128], gp[j]) - delta[j])).astype(bf16)
        weights = weights.astype(bf16)
        dkv[k_tile] += dot(weights, gp[j]) + dot(slopes, queries[j, :, 0:128])
        dq[j] += dot(kt[k_tile], slopes)

    def hooks(n):
        @pl.when(n == HOOKS[0])
        def _():
            for sums in main:
                sums.advance(1)
            for sums in outs:
                sums.advance(0)

        @pl.when(n == HOOKS[1])
        def _():
            for sums in main:
                sums.advance(2)
            for sums in outs:
                sums.advance(1)

        @pl.when(n == HOOKS[2])
        def _():
            for sums in main:
                sums.advance(3)
            for sums in outs:
                sums.advance(2)

        @pl.when(n == HOOKS[3])
        def _():
            for sums in main:
                sums.advance(4)
            for sums in outs:
                sums.advance(3)

        @pl.when(n == HOOKS[4])
        def _():
            for p, sums in enumerate(main):
                total = sums.last()
                for k in range(COUNTS[p]):
                    mid.store(p + 6 * k, total[k])
            for sums in outs:
                sums.advance(4)

        @pl.when(n == HOOKS[5])
        def _():
            for u, sums in enumerate(outs):
                mid.store(16 + u, sums.last()[0])
            mid.start()

        @pl.when(n == HOOKS[6])
        def _():
            mid.finish()

    turn = lax.div(place.head, 4)

    def owned(k_tile):
        return lax.rem(lax.div(k_tile + 1, 2), 2) == core

    def key_tile(i, n):
        k_tile = key_order(place, i)
        skip = 0
        for j in range(4):
            skip = skip + jnp.where(place.own_tile(j) < k_tile, 1, 0)

        def query_tile(at, n):
            hooks(n)
            j = jnp.where(k_tile == 0, lax.rem(at + turn, 4), at)
            diagonal = place.own_tile(j) == k_tile

            @pl.when(diagonal)
            def _():
                step(j, k_tile, True)

            @pl.when(jnp.logical_not(diagonal))
            def _():
                step(j, k_tile, False)

            @pl.when(k_tile == 0)
            def _():
                packed = pack_transposed(dq[j] * SCALE)
                for b in range(4):
                    m = j * 4 + b
                    stage[m, T:GRAD] = packed[b]
                    send_to(place, *query_hop(m))

            return n + 1

        n = lax.fori_loop(skip, 4, query_tile, n)
        mine = owned(k_tile)
        before = key_order(place, jnp.maximum(i - 1, 0))

        @pl.when(jnp.logical_and(jnp.logical_not(mine), jnp.logical_not(jnp.logical_and(core == 1, k_tile == 7))))
        def _():
            give(lax.div(k_tile, 2))

        @pl.when(jnp.logical_and(i > 0, owned(before)))
        def _():
            take(lax.div(before, 2))

        return n

    lax.fori_loop(0, TILES, key_tile, 0)

    @pl.when(core == 0)
    def _():
        take(0)

    def finish(n):
        sent_to(place, *key_hop(n))
        sent_to(place, *query_hop(n))
        arrived(dqkv_in.at[n, 0:T], recv.at[0, n])
        arrived(dqkv_in.at[n, T:GRAD], recv.at[1, n])

    loop(16, finish)

    def given(j, carry):
        part_hop(j).wait_send()
        return carry

    lax.fori_loop(0, 4 - core, given, 0)
    for sums in main + outs:
        sums.finish()


def backward_call(pk, da_in, lse, ot, grads, out_grads):
    return pl.pallas_call(
        backward_kernel,
        name="attention_grad",
        out_shape=(jax.ShapeDtypeStruct((16, GRAD, 128), bf16),) + MID_OUT,
        in_specs=[VM, VM, VM, VM, ANY, ANY],
        out_specs=(ANY, VM, VM, VM),
        scratch_shapes=[
            pltpu.VMEM((3, TILE, 128), f32),
            pltpu.VMEM((TILES, TILE, 256), bf16),
            pltpu.VMEM((4, TILE, 256), bf16),
            pltpu.VMEM((TILES, HD, TILE), bf16),
            pltpu.VMEM((4, TILE, 128), bf16),
            pltpu.VMEM((4, 1, TILE), f32),
            pltpu.VMEM((4, HD, TILE), f32),
            pltpu.VMEM((TILES, TILE, 128), f32),
            pltpu.VMEM((4, TILE, 128), bf16),
            pltpu.VMEM((4, TILE, 128), bf16),
            pltpu.VMEM((16, GRAD, 128), bf16),
            pltpu.VMEM((16, 32, 16, 256), bf16),
            pltpu.VMEM((16, 32, 16, 256), bf16),
            pltpu.VMEM((2, 64, 16, 256), bf16),
            pltpu.VMEM((2, 64, 16, 256), bf16),
        ]
        + MID_SCRATCH[:3]
        + [
            pltpu.SemaphoreType.DMA((4,)),
            pltpu.SemaphoreType.DMA((4,)),
            pltpu.SemaphoreType.DMA((2, 16)),
            pltpu.SemaphoreType.DMA((2, 16)),
            pltpu.SemaphoreType.DMA((8,)),
            pltpu.SemaphoreType.DMA((8, 6)),
            pltpu.SemaphoreType.DMA((8, 6)),
        ]
        + MID_SCRATCH[3:],
        compiler_params=params(3),
    )(pk, da_in, lse, ot, grads, out_grads)


def last_kernel(
    dqkv_in, x_ref, dx1_ref, gain_ref, gain2_ref, w_ref,
    dx_ref, qkv_out, gain_out,
    w_scr, a2, dn, dhalf, a2t, fin, side, gs, land, gain_acc, gain_land,
    w_sem, p_send, p_recv, h_send, h_recv,
):
    place = Place()
    core = place.core
    net = Net(place)
    sums = [Part(net, gs, land, u, 1, u, 0, (h_send, u), (h_recv, u)) for u in range(6)]
    gains = Part(net, gain_acc, gain_land, 0, 1, 0, 0, (h_send, 6), (h_recv, 6))
    weight = pltpu.make_async_copy(w_ref, w_scr, w_sem.at[0])
    weight.start()
    barrier = pltpu.get_barrier_semaphore()
    net.greet(barrier)
    greet(barrier, place.partner)

    def across(k, src, dst):
        return remote(src, dst, p_send.at[k], p_recv.at[k], place.partner)

    x = x_ref[0].astype(f32)
    scale = lax.rsqrt(jnp.mean(x * x, axis=-1, keepdims=True) + EPS)
    a2[0:T] = (x * scale * gain_ref[...]).astype(bf16)
    pl.semaphore_wait(barrier, 7)
    a_hop = across(0, a2.at[0:T], a2.at[T : 2 * T])
    a_hop.start()
    for m in range(8):
        lo, hi = swap_halves(dqkv_in[2 * m, T:GRAD], dqkv_in[2 * m + 1, T:GRAD])
        dk, dv = swap_halves(dqkv_in[2 * m, 0:T], dqkv_in[2 * m + 1, 0:T])
        dn[0:HT, 128 * m : 128 * m + 128] = lo
        dn[HT:T, 128 * m : 128 * m + 128] = hi
        dn[:, D + 128 * m : D + 128 * m + 128] = dk
        dn[:, 2 * D + 128 * m : 2 * D + 128 * m + 128] = dv
        at = 128 * (m % 4)
        dhalf[m // 4, 0:HT, at : at + 128] = lo
        dhalf[m // 4, HT:T, at : at + 128] = hi
        dhalf[m // 4, 0:T, 512 + at : 512 + at + 128] = dk
        dhalf[m // 4, 0:T, 1024 + at : 1024 + at + 128] = dv
    d_hop = across(1, dhalf.at[1 - core, 0:T], dhalf.at[1 - core, T : 2 * T])
    d_hop.start()
    a_hop.wait_recv()
    a2t[...] = transposed(a2[...])
    d_hop.wait_recv()
    for u in range(6):
        spread(gs, u, u, dot(a2t[...], dhalf[core, :, u * 256 : u * 256 + 256]).astype(bf16))
        sums[u].start()
    weight.wait()
    dh1 = dot_nt(dn[...], w_scr[...])
    gain1_grad = jnp.sum(dh1 * x * scale, axis=0, keepdims=True)
    row = lax.broadcasted_iota(jnp.int32, (128, D), 0)
    both = jnp.where(row == 0, gain1_grad, jnp.where(row == 1, gain2_ref[...], 0.0))
    columns = both.T.astype(bf16)
    for chip in range(64):
        y_lo, cx, z, y_hi = chip // 32, chip // 8 % 4, chip // 2 % 4, chip % 2
        gain_acc[0, position(0, y_lo, cx, z, y_hi)] = columns[chip * 16 : chip * 16 + 16]
    gains.start()
    dxn = dh1 * gain_ref[...]
    back = scale * dxn - x * (scale * scale * scale) * jnp.mean(dxn * x, axis=-1, keepdims=True)
    dx_ref[0] = (dx1_ref[...] + back).astype(bf16)

    for stage in range(5):
        for part in sums + [gains]:
            part.advance(stage)
    for u in range(6):
        fin[u] = sums[u].last()[0].reshape(2, 8, 256)
    gain_rows = gains.last()[0]
    fin[6] = jnp.concatenate([gain_rows, jnp.zeros((16, 128), f32)], axis=1).reshape(2, 8, 256)
    aside = across(2, fin.at[:, 1 - core], side)
    aside.start()
    aside.wait_recv()
    mine, other = core, 1 - core
    for u in range(6):
        at = (u // 2) * D + (u % 2) * 256
        qkv_out[:, pl.ds(at + mine * 512, 256)] = fin[u, mine]
        qkv_out[:, pl.ds(at + other * 512, 256)] = side[u]
    both = fin[6, mine][:, 0:128] + side[6][:, 0:128]
    wide = jnp.concatenate([both] + [jnp.zeros((8, 128), f32)] * 15, axis=0).T
    gain_out[...] = wide[0:8]
    for hop in (a_hop, d_hop, aside):
        hop.wait_send()
    for part in sums + [gains]:
        part.finish()


def last_call(dqkv_in, frames, dx1, gain, gain2_grad, w_qkv):
    return pl.pallas_call(
        last_kernel,
        name="input_grad",
        out_shape=(
            jax.ShapeDtypeStruct((1, T, D), bf16),
            jax.ShapeDtypeStruct((8, 3 * D), f32),
            jax.ShapeDtypeStruct((8, 128), f32),
        ),
        in_specs=[VM, VM, VM, VM, VM, ANY],
        out_specs=(VM, VM, VM),
        scratch_shapes=[
            pltpu.VMEM((D, 3 * D), bf16),
            pltpu.VMEM((2 * T, D), bf16),
            pltpu.VMEM((T, 3 * D), bf16),
            pltpu.VMEM((2, 2 * T, 1536), bf16),
            pltpu.VMEM((D, 2 * T), bf16),
            pltpu.VMEM((7, 2, 8, 256), f32),
            pltpu.VMEM((7, 8, 256), f32),
            pltpu.VMEM((6, 64, 16, 256), bf16),
            pltpu.VMEM((6, 64, 16, 256), bf16),
            pltpu.VMEM((1, 64, 16, 128), bf16),
            pltpu.VMEM((1, 64, 16, 128), bf16),
            pltpu.SemaphoreType.DMA((1,)),
            pltpu.SemaphoreType.DMA((3,)),
            pltpu.SemaphoreType.DMA((3,)),
            pltpu.SemaphoreType.DMA((7, 6)),
            pltpu.SemaphoreType.DMA((7, 6)),
        ],
        compiler_params=params(4),
    )(dqkv_in, frames, dx1, gain, gain2_grad, w_qkv)


def deliver_kernel(*refs):
    count = len(refs) // 2 - 2
    sources, gains, targets = refs[:count], refs[count], refs[count + 1 : 2 * count + 1]
    gain1, gain2, sem = refs[2 * count + 1 :]
    del sem
    for k in range(count):
        targets[k][...] = sources[k][...]
    gain1[...] = gains[0, 0:8]
    gain2[...] = gains[1, 0:8]


def deliver(arrays, gains):
    count = len(arrays)
    small = jax.ShapeDtypeStruct((8,), f32)
    return pl.pallas_call(
        deliver_kernel,
        name="deliver",
        out_shape=tuple(jax.ShapeDtypeStruct(v.shape, v.dtype) for v in arrays) + (small, small),
        in_specs=[VM] * (count + 1),
        out_specs=(VM,) * (count + 2),
        scratch_shapes=[pltpu.SemaphoreType.DMA((count,))],
    )(*arrays, gains)


def shards(frames, segment_ids, norm1_gain, w_qkv, w_out, norm2_gain, w_up, w_down, out_grad):
    gain1, gain2 = norm1_gain[None], norm2_gain[None]
    pk = qkv_call(frames, segment_ids, gain1, w_qkv)
    o_in, lse, ot = forward_call(pk)
    y, grads, out_grads, dx1, gain2_grad, da_in = middle_call(
        o_in, frames, out_grad, gain2, w_out, w_up, w_down
    )
    dqkv_in, up_sum, out_sum, down_sum = backward_call(pk, da_in, lse, ot, grads, out_grads)
    dx, qkv_sum, gain_sums = last_call(dqkv_in, frames, dx1, gain1, gain2_grad, w_qkv)
    y, dx, qkv_sum, out_sum, up_sum, down_sum, gain1_sum, gain2_sum = deliver(
        (y, dx, qkv_sum, out_sum, up_sum, down_sum), gain_sums
    )
    return (y, dx, gain1_sum, qkv_sum, out_sum, gain2_sum, up_sum, down_sum)


def solution(mesh):
    return jax.shard_map(
        shards,
        mesh=mesh,
        in_specs=(
            P("row", "seq", None),
            P("row", "seq"),
            P(),
            P(),
            P(),
            P(),
            P(),
            P(),
            P("row", "seq", None),
        ),
        out_specs=(
            P("row", "seq", None),
            P("row", "seq", None),
            P(("seq", "row")),
            P(("seq", "row"), None),
            P(("seq", "row"), None),
            P(("seq", "row")),
            P(("seq", "row"), None),
            P(("seq", "row"), None),
        ),
        check_vma=False,
    )
```

time: 273 us -> 216 us (0.79)
  Pallas kernels: 265 us -> 215 us
  local copies, waits for them, and re-layouts: 7.19 us -> 0 us
    pallas_call x2, Pallas kernels: 120 us -> 71.2 us  [the longest x1 68.8 us: backward_call(): pl.pallas_call(backward_kernel, name='attention_grad', out_shape=(jax.Sha...]
    pallas_call x1, Pallas kernels: 41.6 us -> 31.6 us  [forward_call(): pl.pallas_call(forward_kernel, name='attention', out_shape=(jax.ShapeDtyp...]
    pallas_call x1, Pallas kernels: 31.1 us -> 40.8 us  [middle_call(): pl.pallas_call(middle_kernel, name='feed_forward', out_shape=(jax.ShapeDt...]
    unnamed x14 -> x0, local copies, waits for them, and re-layouts: 5.99 us -> none
where the time goes in v2:
time: 216 us
  Pallas kernels  215 us (100%)
    pallas_call x1, Pallas kernels, backward_call(): pl.pallas_call(backward_kernel, name='attention_grad', out_shape=(jax.Sha...  68.8 us
    pallas_call x1, Pallas kernels, last_call(): pl.pallas_call(last_kernel, name='input_grad', out_shape=(jax.ShapeDtypeS...  41.3 us
    pallas_call x1, Pallas kernels, middle_call(): pl.pallas_call(middle_kernel, name='feed_forward', out_shape=(jax.ShapeDt...  40.8 us
    pallas_call x1, Pallas kernels, forward_call(): pl.pallas_call(forward_kernel, name='attention', out_shape=(jax.ShapeDtyp...  31.6 us
    pallas_call x1, Pallas kernels, qkv_call(): pl.pallas_call(qkv_kernel, name='qkv_to_heads', out_shape=jax.ShapeDtypeS...  30.1 us

profile of v2, /device:TPU:1, one launch (start us, length us, event | category | flops | bytes accessed | tf_op | source)
XLA Modules:
  0.0 215.8 jit_solution(17755743598684684762)
XLA Ops:
  0.6 30.1 %qkv_to_heads.1.pk_ref = bf16[32,304,128]{2,1,0:T(8,128)(2,1)} custom-call(bf16[1,192,1024]{2,1,0:T(8,128)(2,1)} %x_ref.5, s32[1,192]{1,0:T(1,128)} %seg_ref.1, f32[1,1024]{1,0:T(1,128)} %bitcast.2, bf16[1024,3072]{1,0:T(8,128)(2,1)} %w_ref.3), custom_call_target="tpu_custom_call" | custom-call | tf_op jit(solution)/shard_map/qkv_to_heads/pallas_call | solution.py:215
  30.7 31.6 %attention.1 = (bf16[16,96,128]{2,1,0:T(8,128)(2,1)}, f32[4,1,768]{2,1,0:T(1,128)}, f32[4,64,768]{2,1,0:T(8,128)}) custom-call(bf16[32,304,128]{2,1,0:T(8,128)(2,1)} %qkv_to_heads.1.pk_ref), custom_call_target="tpu_custom_call" | custom-call | tf_op jit(solution)/shard_map/attention/pallas_call | solution.py:400
  62.3 40.8 %feed_forward.1 = (bf16[1,192,1024]{2,1,0:T(8,128)(2,1)}, bf16[16,32,16,256]{3,2,1,0:T(8,128)(2,1)}, bf16[2,64,16,256]{3,2,1,0:T(8,128)(2,1)}, f32[192,1024]{1,0...) custom-call(bf16[16,96,128]{2,1,0:T(8,128)(2,1)} %get-tuple-element.32.o_in, bf16[1,192,1024]{2,1,0:T(8,128)(2,1)} %x_ref.5, ...), custom_call_target="tpu_custom_call" | custom-call | tf_op jit(solution)/shard_map/feed_forward/pallas_call | solution.py:799
  103.1 68.8 %attention_grad.1 = (bf16[16,288,128]{2,1,0:T(8,128)(2,1)}, f32[8,4096]{1,0:T(8,128)}, f32[8,1024]{1,0:T(8,128)}, f32[32,1024]{1,0:T(8,128)}) custom-call(bf16[32,304,128]{2,1,0:T(8,128)(2,1)} %qkv_to_heads.1.pk_ref, bf16[16,96,128]{2,1,0:T(8,128)(2,1)} %get-tuple-element.34.da_ref, f32[4,1,768]{2,1,0:T(1,128)} %get-tuple-element.35.lse_ref, ...), custom_call_target="tpu_custom_call" | custom-call | tf_op jit(solution)/shard_map/attention_grad/pallas_call | solution.py:1061
  172.0 41.3 %input_grad.1 = (bf16[1,192,1024]{2,1,0:T(8,128)(2,1)}, f32[8,3072]{1,0:T(8,128)}, f32[8,128]{1,0:T(8,128)}) custom-call(bf16[16,288,128]{2,1,0:T(8,128)(2,1)} %get-tuple-element.39.dqkv_in, bf16[1,192,1024]{2,1,0:T(8,128)(2,1)} %x_ref.5, f32[192,1024]{1,0:T(8,128)} %get-tuple-element.40.dx1_ref, f32[1,1024]{1,0:T(1,128)} %bitcast.3, ...), custom_call_target="tpu_custom_call" | custom-call | tf_op jit(solution)/shard_map/input_grad/pallas_call | solution.py:1184
  213.3 2.3 %deliver.1 = (bf16[1,192,1024]{2,1,0:T(8,128)(2,1)}, bf16[1,192,1024]{2,1,0:T(8,128)(2,1)}, f32[8,3072]{1,0:T(8,128)}, f32[8,1024]{1,0:T(8,128)}, f32[8,4096]{1,...) custom-call(bf16[1,192,1024]{2,1,0:T(8,128)(2,1)} %get-tuple-element.33.refs_0_, ...), custom_call_target="tpu_custom_call" | custom-call | tf_op jit(solution)/shard_map/deliver/pallas_call | solution.py:1230

commit v3 on v2

v3 whole, which is shorter than its diff:
```python
import functools
import math

import jax
import jax.numpy as jnp
from jax import lax
from jax.experimental import pallas as pl
from jax.experimental.pallas import tpu as pltpu
from jax.sharding import PartitionSpec as P

MESH = pl.DeviceIdType.MESH
f32 = jnp.float32
bf16 = jnp.bfloat16

D = 1024
H = 16
HD = 64
FF = 4096
T = 192
HT = T // 2
BLOCKS = 32
TILE = 768
TILES = 8
PACK = 304
GRAD = 288
EPS = 1e-05
NEG = -1e30
LOG2E = math.log2(math.e)
LN2 = math.log(2.0)
SCALE = HD**-0.5
VMEM_LIMIT = 60 * 1024 * 1024

ANY = pl.BlockSpec(memory_space=pl.ANY)
VM = pl.BlockSpec(memory_space=pltpu.VMEM)


def dot(a, b):
    return jnp.dot(a, b, preferred_element_type=f32)


def dot_nt(a, b):
    return lax.dot_general(a, b, (((1,), (1,)), ((), ())), preferred_element_type=f32)


def transposed(v):
    return v.astype(f32).T.astype(bf16)


def swap_halves(first, second):
    lane = lax.broadcasted_iota(jnp.int32, first.shape, 1)
    low = lane < HD
    first, second = first.astype(f32), second.astype(f32)
    return (
        jnp.where(low, first, pltpu.roll(second, HD, 1)).astype(bf16),
        jnp.where(low, pltpu.roll(first, HD, 1), second).astype(bf16),
    )


class Place:
    def __init__(self):
        self.s = lax.axis_index("seq")
        self.r = lax.axis_index("row")
        self.y_lo = lax.div(self.s, 16)
        self.head = lax.rem(self.s, 16)
        self.y_hi = lax.div(self.r, 2)
        self.core = lax.rem(self.r, 2)
        tile = lax.div(self.s, 4)
        self.block_core = lax.rem(lax.div(tile + 1, 2), 2)
        self.slot = lax.div(self.s, 8) * 4 + lax.rem(self.s, 4)
        self.partner = (self.s, self.r + 1 - 2 * self.core)
        self.self_served = jnp.logical_and(self.y_lo == self.core, self.block_core == self.core)
        self.self_count = jnp.where(self.self_served, 1, 0)

    def head_device(self, h):
        return (self.core * 16 + h, self.y_hi * 2 + self.block_core)

    def own_tile(self, j, core=None):
        core = self.core if core is None else core
        return 2 * j + lax.rem(j + core, 2)

    def own_block(self, n):
        return self.own_tile(lax.div(n, 4)) * 4 + lax.rem(n, 4)

    def block_device(self, n):
        return (self.own_block(n), self.y_hi * 2 + self.y_lo)

    def is_self(self, device):
        return jnp.logical_and(device[0] == self.s, device[1] == self.r)


def remote(src, dst, send, recv, device):
    return pltpu.make_async_remote_copy(
        src_ref=src, dst_ref=dst, send_sem=send, recv_sem=recv, device_id=device, device_id_type=MESH
    )


def send_to(place, src, dst, send, recv, device):
    own = place.is_self(device)

    @pl.when(own)
    def _():
        pltpu.make_async_copy(src, dst, recv).start()

    @pl.when(jnp.logical_not(own))
    def _():
        remote(src, dst, send, recv, device).start()


def sent_to(place, src, dst, send, recv, device):
    @pl.when(jnp.logical_not(place.is_self(device)))
    def _():
        remote(src, dst, send, recv, device).wait_send()


def arrived(dst, recv):
    pltpu.make_async_copy(dst, dst, recv).wait()


def greet(barrier, device):
    pl.semaphore_signal(barrier, inc=1, device_id=device, device_id_type=MESH)


def greet_all(place, barrier, device_of):
    def one(n, carry):
        device = device_of(n)

        @pl.when(jnp.logical_not(place.is_self(device)))
        def _():
            greet(barrier, device)

        return carry

    lax.fori_loop(0, 16, one, 0)


def loop(count, body):
    def one(n, carry):
        body(n)
        return carry

    lax.fori_loop(0, count, one, 0)


def params(collective_id):
    return pltpu.CompilerParams(
        collective_id=collective_id, has_side_effects=True, vmem_limit_bytes=VMEM_LIMIT
    )


def seg_column(pk_ref, block):
    tile = pk_ref[block, T + HT : PACK].astype(f32)
    return jnp.concatenate(
        [
            jnp.broadcast_to(tile[0:1], (128, 128)).T,
            jnp.broadcast_to(tile[1:2], (128, 128)).T[: T - 128],
        ],
        axis=0,
    )


def fill_segments(pk_ref, seg):
    first = seg_column(pk_ref, 0)
    last = seg_column(pk_ref, BLOCKS - 1)
    common = jnp.broadcast_to(first[T - 1 : T], (TILE, 128))
    seg[0] = common
    seg[1] = common
    seg[2] = common
    seg[0, 0:T] = first
    seg[2, TILE - T : TILE] = last


def seg_kind(tile):
    return jnp.where(tile == 0, 0, jnp.where(tile == TILES - 1, 2, 1))


def fill_operands(place, pk_ref, seg, keys, queries):
    fill_segments(pk_ref, seg)
    lane = lax.broadcasted_iota(jnp.int32, (TILE, 128), 1)
    number = lane.astype(f32)

    def key_tile(t):
        keys[t, :, 0:128] = load_keys(pk_ref, t)
        keys[t, :, 128:256] = jnp.where(seg[seg_kind(t)] == number, 1.0, 0.0).astype(bf16)

    loop(TILES, key_tile)
    low = lax.broadcasted_iota(jnp.int32, (HT, 128), 1) < HD

    def query_tile(j):
        tile = place.own_tile(j)
        for b in range(4):
            packed = pk_ref[tile * 4 + b, T : T + HT].astype(f32)
            queries[j, b * T : b * T + HT, 0:128] = jnp.where(low, packed, 0.0).astype(bf16)
            queries[j, b * T + HT : b * T + T, 0:128] = jnp.where(low, pltpu.roll(packed, HD, 1), 0.0).astype(bf16)
        other = jnp.logical_and(lane < 8, seg[seg_kind(tile)] != number)
        queries[j, :, 128:256] = jnp.where(other, NEG, 0.0).astype(bf16)

    loop(4, query_tile)


STEPS = 18


def walk(place, n):
    turn = lax.div(place.head, 4)
    j, start, end = lax.rem(turn, 4), 0, 0
    end = place.own_tile(j) + 1
    for k in range(1, 4):
        past = n >= end
        following = lax.rem(turn + k, 4)
        j = jnp.where(past, following, j)
        start = jnp.where(past, end, start)
        end = jnp.where(past, end + place.own_tile(following) + 1, end)
    at = n - start
    k_tile = jnp.where(at == 0, place.own_tile(j), at - 1)
    return j, k_tile, at == 0, n + 1 == end


def key_order(place, i):
    turn = lax.div(place.head, 4)
    return jnp.where(i == 7, 0, 7 - lax.rem(i + 2 * turn, 7))


def causal(scores):
    k = lax.broadcasted_iota(jnp.int32, scores.shape, 0)
    q = lax.broadcasted_iota(jnp.int32, scores.shape, 1)
    return jnp.where(k <= q, scores, NEG)


def load_keys(pk_ref, tile):
    return pk_ref[pl.ds(tile * 4, 4), 0:T].reshape(TILE, 128)


def pack_transposed(value_t):
    both = jnp.concatenate([value_t, value_t], axis=0).T
    lane = lax.broadcasted_iota(jnp.int32, (HT, 128), 1)
    return [
        jnp.where(lane < HD, both[b * T : b * T + HT], both[b * T + HT : b * T + T]).astype(bf16)
        for b in range(4)
    ]


def forward_kernel(
    x_ref, seg_ref, gain_ref, w_ref, pk_out, o_in, lse_ref, ot_ref,
    w_scr, packets, pk, seg, keys, queries, vt, top, acc, even, odd, stage,
    w_sem, a_send, a_recv, f_send, f_recv, k_sem, send, recv,
):
    place = Place()

    def weight(g, part):
        return pltpu.make_async_copy(
            w_ref.at[:, pl.ds(part * D + g * 256, 256)], w_scr.at[g, part], w_sem.at[g, part]
        )

    for g in range(4):
        for part in range(3):
            weight(g, part).start()
    barrier = pltpu.get_barrier_semaphore()
    greet_all(place, barrier, place.block_device)
    greet_all(place, barrier, place.head_device)
    greet(barrier, place.partner)

    x = x_ref[0].astype(f32)
    a = (x * lax.rsqrt(jnp.mean(x * x, axis=-1, keepdims=True) + EPS) * gain_ref[...]).astype(bf16)
    numbers = seg_ref[...].astype(f32)
    row = lax.broadcasted_iota(jnp.int32, (16, 128), 0)
    rest = jnp.concatenate([numbers[:, 128:T], jnp.zeros((1, 256 - T), f32)], axis=1)
    seg_tile = jnp.where(row == 0, numbers[:, :128], jnp.where(row == 1, rest, 0.0)).astype(bf16)
    pl.semaphore_wait(barrier, 33 - 2 * place.self_count)

    def packet_hop(h):
        return (
            packets.at[h], pk.at[place.s], a_send.at[h], a_recv.at[place.slot], place.head_device(h),
        )

    for g in range(4):
        for part in range(3):
            weight(g, part).wait()
        q = dot(a, w_scr[g, 0]) * (SCALE * LOG2E)
        k = dot(a, w_scr[g, 1])
        v = dot(a, w_scr[g, 2])
        for m in range(2):
            lanes = slice(128 * m, 128 * m + 128)
            h = 4 * g + 2 * m
            kv = swap_halves(k[:, lanes].astype(bf16), v[:, lanes].astype(bf16))
            qq = q[:, lanes].astype(bf16)
            qp = swap_halves(qq[:HT], qq[HT:])
            for e in range(2):
                packets[h + e, 0:T] = kv[e]
                packets[h + e, T : T + HT] = qp[e]
                packets[h + e, T + HT : PACK] = seg_tile
                send_to(place, *packet_hop(h + e))

    def forward(n):
        i = place.own_block(n)
        return remote(pk.at[i], pk.at[i], f_send.at[n], f_recv.at[n], place.partner)

    def keep(n, core):
        i = place.own_tile(lax.div(n, 4), core) * 4 + lax.rem(n, 4)
        return pltpu.make_async_copy(pk.at[i], pk_out.at[i], k_sem.at[n])

    def pass_on(n):
        arrived(pk.at[place.own_block(n)], a_recv.at[n])
        forward(n).start()
        keep(n, place.core).start()

    loop(16, pass_on)
    one = jnp.where(lax.broadcasted_iota(jnp.int32, (16, TILE), 0) == 0, 1.0, 0.0).astype(bf16)

    def kept_all(n):
        keep(n, place.core).wait()
        forward(n).wait_recv()
        keep(n, 1 - place.core).start()

    loop(16, kept_all)
    fill_operands(place, pk, seg, keys, queries)

    def prepare(t):
        vt[t, 0:HD] = transposed(keys[t, :, 0:128])[HD:]
        vt[t, HD : HD + 16] = one

    loop(TILES, prepare)

    def score(n, scores):
        j, k_tile, _, _ = walk(place, jnp.minimum(n, STEPS - 1))
        scores[...] = dot_nt(keys[k_tile], queries[j])

    def out_hop(m):
        return (
            stage.at[m], o_in.at[place.head], send.at[m], recv.at[place.head], place.block_device(m),
        )

    def body(n, now, later):
        j, k_tile, first, last = walk(place, n)

        @pl.when(first)
        def _():
            score(n + 1, later)
            scores = causal(now[...])
            peak = jnp.max(scores, axis=0, keepdims=True)
            top[...] = peak
            acc[...] = dot(vt[k_tile], jnp.exp2(scores - peak).astype(bf16))

        @pl.when(jnp.logical_not(first))
        def _():
            score(n + 1, later)
            scores = now[...]
            peak = jnp.maximum(top[...], jnp.max(scores, axis=0, keepdims=True))
            fade = jnp.exp2(top[...] - peak)
            top[...] = peak
            acc[...] = acc[...] * fade + dot(vt[k_tile], jnp.exp2(scores - peak).astype(bf16))

        @pl.when(last)
        def _():
            total = acc[HD : HD + 1]
            out_t = acc[0:HD] / total
            lse_ref[j] = top[...] + jnp.log2(total)
            ot_ref[j] = out_t
            packed = pack_transposed(out_t)
            for b in range(4):
                m = j * 4 + b
                stage[m] = packed[b]
                send_to(place, *out_hop(m))

    score(0, even)

    def pair(i):
        body(2 * i, even, odd)
        body(2 * i + 1, odd, even)

    loop(STEPS // 2, pair)

    def finish(n):
        sent_to(place, *packet_hop(n))
        forward(n).wait_send()
        keep(n, 1 - place.core).wait()
        sent_to(place, *out_hop(n))
        arrived(o_in.at[n], recv.at[n])

    loop(16, finish)


def forward_call(frames, segment_ids, gain, w_qkv):
    return pl.pallas_call(
        forward_kernel,
        name="attention",
        out_shape=(
            jax.ShapeDtypeStruct((BLOCKS, PACK, 128), bf16),
            jax.ShapeDtypeStruct((16, HT, 128), bf16),
            jax.ShapeDtypeStruct((4, 1, TILE), f32),
            jax.ShapeDtypeStruct((4, HD, TILE), f32),
        ),
        in_specs=[VM, VM, VM, ANY],
        out_specs=(ANY, ANY, VM, VM),
        scratch_shapes=[
            pltpu.VMEM((4, 3, D, 256), bf16),
            pltpu.VMEM((16, PACK, 128), bf16),
            pltpu.VMEM((BLOCKS, PACK, 128), bf16),
            pltpu.VMEM((3, TILE, 128), f32),
            pltpu.VMEM((TILES, TILE, 256), bf16),
            pltpu.VMEM((4, TILE, 256), bf16),
            pltpu.VMEM((TILES, HD + 16, TILE), bf16),
            pltpu.VMEM((1, TILE), f32),
            pltpu.VMEM((HD + 16, TILE), f32),
            pltpu.VMEM((TILE, TILE), f32),
            pltpu.VMEM((TILE, TILE), f32),
            pltpu.VMEM((16, HT, 128), bf16),
            pltpu.SemaphoreType.DMA((4, 3)),
            pltpu.SemaphoreType.DMA((16,)),
            pltpu.SemaphoreType.DMA((16,)),
            pltpu.SemaphoreType.DMA((16,)),
            pltpu.SemaphoreType.DMA((16,)),
            pltpu.SemaphoreType.DMA((16,)),
            pltpu.SemaphoreType.DMA((16,)),
            pltpu.SemaphoreType.DMA((16,)),
        ],
        compiler_params=params(0),
    )(frames, segment_ids, gain, w_qkv)


FIRST = lambda c: ((c + 1) // 2) % 2
SECOND = lambda c: c // 2


def chip_bits(x, y, z):
    return [FIRST(x), FIRST(y), FIRST(z), SECOND(x), SECOND(y), SECOND(z)]


def position(part, y_lo, x, z, y_hi):
    bits = chip_bits(x, y_hi * 2 + y_lo, z)
    at = 0
    for k in range(6):
        at = at * 2 + bits[(part + k) % 6]
    return at


class Part:
    def __init__(self, net, acc, land, at, count, turn, send, recv, pieces=()):
        self.net, self.acc, self.land, self.turn, self.pieces = net, acc, land, turn, pieces
        self.units = pl.ds(at, count)
        self.count, self.send, self.recv = count, send, recv

    def bit(self, stage):
        return self.net.bits[(self.turn + stage) % 6]

    def base(self, stage):
        at = 0
        for k in range(stage + 1):
            at = at + self.bit(k) * (32 >> k)
        return at

    def landing(self, stage):
        return sum(32 >> k for k in range(stage))

    def hop(self, stage):
        half = 32 >> stage
        base = self.base(stage - 1) + (1 - self.bit(stage)) * half
        return remote(
            self.acc.at[self.units, pl.ds(base, half)],
            self.land.at[self.units, pl.ds(self.landing(stage), half)],
            self.send[0].at[self.send[1], stage],
            self.recv[0].at[self.recv[1], stage],
            self.net.neighbours[(self.turn + stage) % 6],
        )

    def start(self):
        self.hop(0).start()

    def hops(self, stage):
        return list(self.pieces) if stage == 0 and self.pieces else [self.hop(stage)]

    def add(self, base, landed, count):
        group = min(count, 4)

        def body(i):
            here = pl.ds(base + i * group, group)
            there = pl.ds(landed + i * group, group)
            total = self.acc[self.units, here].astype(f32) + self.land[self.units, there].astype(f32)
            self.acc[self.units, here] = total.astype(bf16)

        loop(count // group, body)

    def advance(self, stage):
        for hop in self.hops(stage):
            hop.wait_recv()
        half = 16 >> stage
        base, landed = self.base(stage), self.landing(stage)
        bit = self.bit(stage + 1)
        self.add(base + (1 - bit) * half, landed + (1 - bit) * half, half)
        self.hop(stage + 1).start()
        self.add(base + bit * half, landed + bit * half, half)

    def last(self):
        self.hop(5).wait_recv()
        return (
            self.acc[self.units, pl.ds(self.base(5), 1)].astype(f32)
            + self.land[self.units, pl.ds(self.landing(5), 1)].astype(f32)
        )[:, 0]

    def finish(self):
        for stage in range(6):
            for hop in self.hops(stage):
                hop.wait_send()


class Net:
    def __init__(self, place):
        x, z = lax.div(place.head, 4), lax.rem(place.head, 4)
        y = place.y_hi * 2 + place.y_lo
        self.bits = [
            lax.rem(lax.div(x + 1, 2), 2), lax.rem(lax.div(y + 1, 2), 2), lax.rem(lax.div(z + 1, 2), 2),
            lax.div(x, 2), lax.div(y, 2), lax.div(z, 2),
        ]

        def device(x, y, z):
            return (lax.rem(y, 2) * 16 + x * 4 + z, lax.div(y, 2) * 2 + place.core)

        flip = lambda c: c + 1 - 2 * lax.rem(c, 2)
        self.neighbours = [
            device(flip(x), y, z), device(x, flip(y), z), device(x, y, flip(z)),
            device(3 - x, y, z), device(x, 3 - y, z), device(x, y, 3 - z),
        ]

    def greet(self, barrier):
        for device in self.neighbours:
            greet(barrier, device)


TURN = [u % 6 for u in range(18)]
COUNTS = [3, 3, 3, 3, 2, 2]
STARTS = [0, 3, 6, 9, 12, 14]
SLOT = [STARTS[u % 6] + u // 6 for u in range(16)]
FINAL = list(range(8)) + [10 + (v % 4) * 2 + v // 4 for v in range(8)] + [8, 9]


class MidSums:
    def __init__(self, place, fin, side, down, sem, up_out, out_out, down_out):
        self.place, self.fin, self.side, self.down, self.sem = place, fin, side, down, sem
        self.up_out, self.out_out, self.down_out = up_out, out_out, down_out

    def targets(self):
        return [(self.place.core * 16 + self.place.head, self.place.y_hi * 2 + k) for k in range(2)]

    def sources(self):
        return [(m * 16 + self.place.head, self.place.y_hi * 2 + self.place.y_lo) for m in range(2)]

    def self_count(self):
        return jnp.where(self.place.y_lo == self.place.core, 1, 0)

    def greet(self, barrier):
        greet(barrier, self.place.partner)
        for device in self.sources():

            @pl.when(jnp.logical_not(self.place.is_self(device)))
            def _(device=device):
                greet(barrier, device)

    def greetings(self):
        return 3 - self.self_count()

    def store(self, unit, value):
        self.fin[FINAL[unit]] = value.reshape(2, 8, 256)

    def aside(self):
        return remote(
            self.fin.at[0:10, 1 - self.place.core], self.side, self.sem.at[0], self.sem.at[1], self.place.partner
        )

    def down_hop(self, k):
        return (
            self.fin.at[10 + 4 * k : 14 + 4 * k],
            self.down.at[self.place.y_lo],
            self.sem.at[2 + k],
            self.sem.at[4 + self.place.y_lo],
            self.targets()[k],
        )

    def start(self):
        self.aside().start()
        for k in range(2):
            send_to(self.place, *self.down_hop(k))

    def finish(self):
        place = self.place
        self.aside().wait_recv()
        mine, other = place.core, 1 - place.core
        for u in range(8):
            self.up_out[:, pl.ds(mine * 2048 + u * 256, 256)] = self.fin[u, mine]
            self.up_out[:, pl.ds(other * 2048 + u * 256, 256)] = self.side[u]
        for u in range(2):
            self.out_out[:, pl.ds(mine * 512 + u * 256, 256)] = self.fin[8 + u, mine]
            self.out_out[:, pl.ds(other * 512 + u * 256, 256)] = self.side[8 + u]
        for m in range(2):
            arrived(self.down.at[m], self.sem.at[4 + m])
            for v in range(4):
                group, half = v // 2, v % 2
                self.down_out[group * 16 : group * 16 + 16, m * 512 + half * 256 : m * 512 + half * 256 + 256] = (
                    self.down[m, v].reshape(16, 256)
                )
        self.aside().wait_send()
        for k in range(2):
            sent_to(place, *self.down_hop(k))


MID_OUT = (
    jax.ShapeDtypeStruct((8, FF), f32),
    jax.ShapeDtypeStruct((8, D), f32),
    jax.ShapeDtypeStruct((32, D), f32),
)
MID_SCRATCH = [
    pltpu.VMEM((18, 2, 8, 256), f32),
    pltpu.VMEM((10, 8, 256), f32),
    pltpu.VMEM((2, 4, 2, 8, 256), f32),
    pltpu.SemaphoreType.DMA((6,)),
]


def spread(target, unit_slot, turn, block):
    for chip in range(64):
        y_lo, x, z, y_hi = chip // 32, chip // 8 % 4, chip // 2 % 4, chip % 2
        target[unit_slot, position(turn, y_lo, x, z, y_hi)] = block[chip * 16 : chip * 16 + 16]


ROOT = math.sqrt(2.0 / math.pi)
CUBE = 0.044715


HOOKS = (3, 7, 10, 12, 13, 14, 15, 17)


def rest_kernel(
    o_in, x_ref, dy_ref, gain1_ref, gain2_ref, lse_ref, w_out, w_up, w_down, w_qkv, pk_in, ot_in,
    y_ref, dx_ref, qkv_out, gain_out, up_out, out_out, down_out,
    o2, b2, dm2, yside, hside, da_side, dx1s, gain2_grad, gs, land, outg, land2, da_in, stage1,
    part, landed, dqkv_in, stage2, fin, side, down, a2, dhalf, gs3, land3, gain_acc, gain_land, fin3, side3,
    w_sem, l_sem, p_send, p_recv, q_send, q_recv, h_send, h_recv, a_send, a_recv, b_send, b_recv,
    n_send, n_recv, t_send, t_recv, m_sem,
):
    place = Place()
    core = place.core
    net = Net(place)

    def across(k, src, dst):
        return remote(src, dst, p_send.at[k], p_recv.at[k], place.partner)

    def first_hop(unit):
        bit = net.bits[TURN[unit]]
        return remote(
            gs.at[SLOT[unit], pl.ds((1 - bit) * 32, 32)], land.at[SLOT[unit], 0:32],
            h_send.at[unit], h_recv.at[unit], net.neighbours[TURN[unit]],
        )

    main = [
        Part(
            net, gs, land, STARTS[p], COUNTS[p], p, (n_send, p), (n_recv, p),
            [first_hop(p + 6 * k) for k in range(COUNTS[p])],
        )
        for p in range(6)
    ]
    outs = [Part(net, outg, land2, u, 1, TURN[16 + u], (n_send, 6 + u), (n_recv, 6 + u)) for u in range(2)]
    mid = MidSums(place, fin, side, down, m_sem, up_out, out_out, down_out)
    sums = [Part(net, gs3, land3, u, 1, u, (t_send, u), (t_recv, u)) for u in range(6)]
    gains = Part(net, gain_acc, gain_land, 0, 1, 0, (t_send, 6), (t_recv, 6))

    barrier = pltpu.get_barrier_semaphore()
    greet_all(place, barrier, place.block_device)
    greet_all(place, barrier, place.head_device)
    net.greet(barrier)
    mid.greet(barrier)

    def da_hop(h):
        return (
            stage1.at[h], da_in.at[place.slot], a_send.at[h], a_recv.at[place.slot], place.head_device(h),
        )

    a_hop = across(6, a2.at[0:T], a2.at[T : 2 * T])

    def feed_forward(wo, wu, wd, b2t, gzt, x1s, ysum, hsum):
        def up_copy(j):
            at = pl.multiple_of(core * 2048 + j * 512, 512)
            return pltpu.make_async_copy(w_up.at[:, pl.ds(at, 512)], wu.at[j], w_sem.at[1 + j])

        def down_copy(j):
            at = pl.multiple_of(core * 2048 + j * 512, 512)
            return pltpu.make_async_copy(w_down.at[pl.ds(at, 512)], wd.at[j], w_sem.at[5 + j])

        out_copy = pltpu.make_async_copy(w_out, wo, w_sem.at[0])
        out_copy.start()
        for j in range(4):
            up_copy(j).start()
            down_copy(j).start()
        dm2[0:T] = dy_ref[0]
        for m in range(8):
            lo, hi = swap_halves(o_in[2 * m], o_in[2 * m + 1])
            o2[0:HT, 128 * m : 128 * m + 128] = lo
            o2[HT:T, 128 * m : 128 * m + 128] = hi
        pl.semaphore_wait(barrier, 2 * (16 - place.self_count) + 6 + mid.greetings())
        dm_hop = across(0, dm2.at[0:T], dm2.at[T : 2 * T])
        o_hop = across(1, o2.at[0:T], o2.at[T : 2 * T])
        dm_hop.start()
        o_hop.start()
        out_copy.wait()
        x1 = x_ref[0].astype(f32) + dot(o2[0:T], wo[...])
        x1s[...] = x1
        scale1 = lax.rsqrt(jnp.mean(x1 * x1, axis=-1, keepdims=True) + EPS)
        b2[0:T] = (x1 * scale1 * gain2_ref[...]).astype(bf16)
        b_hop = across(2, b2.at[0:T], b2.at[T : 2 * T])
        b_hop.start()
        x = x_ref[0].astype(f32)
        a2[0:T] = (x * lax.rsqrt(jnp.mean(x * x, axis=-1, keepdims=True) + EPS) * gain1_ref[...]).astype(bf16)
        a_hop.start()
        dm_hop.wait_recv()
        b_hop.wait_recv()
        b2t[...] = transposed(b2[...])

        for j in range(4):
            up_copy(j).wait()
            down_copy(j).wait()
            z = dot(b2[...], wu[j])
            zz = z * z
            th = jnp.tanh(ROOT * z * (1.0 + CUBE * zz))
            half = 0.5 * (1.0 + th)
            gz = (z * half).astype(bf16)
            slope = half + 0.5 * z * (1.0 - th * th) * (ROOT * (1.0 + 3.0 * CUBE * zz))
            dz = (dot_nt(dm2[...], wd[j]) * slope).astype(bf16)
            gzt[j * 512 : (j + 1) * 512] = transposed(gz)
            yj = dot(gz, wd[j])
            hj = dot_nt(dz, wu[j])
            if j == 0:
                ysum[...] = yj
                hsum[...] = hj
            else:
                ysum[...] += yj
                hsum[...] += hj
            up = dot(b2t[...], dz).astype(bf16)
            for u in range(2):
                unit = 2 * j + u
                spread(gs, SLOT[unit], TURN[unit], up[:, u * 256 : u * 256 + 256])
                first_hop(unit).start()

        y_hop = across(3, ysum.at[T : 2 * T], yside)
        h_hop = across(4, hsum.at[T : 2 * T], hside)
        h_hop.start()
        y_hop.start()

        def down_units(u):
            for y_lo in range(2):
                at = y_lo * 512 + u * 256
                grad = dot(gzt[...], dm2[:, at : at + 256]).astype(bf16)
                for owner in range(32):
                    for group in range(4):
                        unit = 8 + u * 4 + group
                        place_at = position(TURN[unit], y_lo, owner // 8, owner // 2 % 4, owner % 2)
                        gs[SLOT[unit], place_at] = grad[owner * 64 + group * 16 : owner * 64 + group * 16 + 16]
            for group in range(4):
                first_hop(8 + u * 4 + group).start()

        down_units(0)
        h_hop.wait_recv()
        x1 = x1s[...]
        scale1 = lax.rsqrt(jnp.mean(x1 * x1, axis=-1, keepdims=True) + EPS)
        dh2 = hsum[0:T] + hside[...]
        gain2_grad[...] = jnp.sum(dh2 * x1 * scale1, axis=0, keepdims=True)
        dn = dh2 * gain2_ref[...]
        back = scale1 * dn - x1 * (scale1 * scale1 * scale1) * jnp.mean(dn * x1, axis=-1, keepdims=True)
        dx1 = dy_ref[0].astype(f32) + back
        dx1s[...] = dx1
        da = dx1.astype(bf16)
        da_side[0, 0:T] = da[:, 0:512]
        da_side[1, 0:T] = da[:, 512:1024]
        side_hop = across(5, da_side.at[1 - core, 0:T], da_side.at[1 - core, T : 2 * T])
        side_hop.start()
        for g in range(4):
            dattn = dot_nt(da, wo[256 * g : 256 * g + 256]).astype(bf16)
            for m in range(2):
                tile = dattn[:, 128 * m : 128 * m + 128]
                packed = swap_halves(tile[:HT], tile[HT:])
                for e in range(2):
                    h = 4 * g + 2 * m + e
                    stage1[h] = packed[e]
                    send_to(place, *da_hop(h))
        down_units(1)
        y_hop.wait_recv()
        y_ref[0] = (x1 + ysum[0:T] + yside[...]).astype(bf16)
        o_hop.wait_recv()
        side_hop.wait_recv()
        out = dot(transposed(o2[...]), da_side[core]).astype(bf16)
        for u in range(2):
            spread(outg, u, TURN[16 + u], out[:, u * 256 : u * 256 + 256])
            outs[u].start()
        for hop in (dm_hop, o_hop, b_hop, y_hop, h_hop, side_hop):
            hop.wait_send()

    pl.run_scoped(
        feed_forward,
        pltpu.VMEM((D, D), bf16),
        pltpu.VMEM((4, D, 512), bf16),
        pltpu.VMEM((4, 512, D), bf16),
        pltpu.VMEM((D, 2 * T), bf16),
        pltpu.VMEM((2048, 2 * T), bf16),
        pltpu.VMEM((T, D), f32),
        pltpu.VMEM((2 * T, D), f32),
        pltpu.VMEM((2 * T, D), f32),
    )

    def key_hop(m):
        return (
            stage2.at[m, 0:T], dqkv_in.at[place.head, 0:T], b_send.at[0, m], b_recv.at[0, place.head],
            place.block_device(m),
        )

    def query_hop(m):
        return (
            stage2.at[m, T:GRAD], dqkv_in.at[place.head, T:GRAD], b_send.at[1, m], b_recv.at[1, place.head],
            place.block_device(m),
        )

    def part_hop(j):
        return remote(part.at[j], landed.at[j], q_send.at[j], q_recv.at[j], place.partner)

    def attention(pk, ot, seg, keys, queries, kt, gp, delta, dq, dkv):
        pk_copy = pltpu.make_async_copy(pk_in, pk, l_sem.at[0])
        ot_copy = pltpu.make_async_copy(ot_in, ot, l_sem.at[1])
        pk_copy.start()
        ot_copy.start()
        pk_copy.wait()
        fill_operands(place, pk, seg, keys, queries)
        low = lax.broadcasted_iota(jnp.int32, (HT, 128), 1) < HD

        def prepare(t):
            kt[t] = transposed(keys[t, :, 0:128])[:HD]
            dkv[t] = jnp.zeros((TILE, 128), f32)

        loop(TILES, prepare)
        ot_copy.wait()

        def prepare_query(j):
            for b in range(4):
                m = j * 4 + b
                arrived(da_in.at[m], a_recv.at[m])
                packed = da_in[m].astype(f32)
                gp[j, b * T : b * T + HT] = jnp.where(low, 0.0, pltpu.roll(packed, HD, 1)).astype(bf16)
                gp[j, b * T + HT : b * T + T] = jnp.where(low, 0.0, packed).astype(bf16)
            delta[j] = jnp.sum(gp[j].astype(f32).T[HD:] * ot[j], axis=0, keepdims=True)
            dq[j] = jnp.zeros((HD, TILE), f32)

        loop(4, prepare_query)
        factor = jnp.where(lax.broadcasted_iota(jnp.int32, (1, 128), 1) < HD, LN2, 1.0)

        def give(j):
            part[j] = (dkv[place.own_tile(j, 1 - core)] * factor).astype(bf16)
            part_hop(j).start()

        def take(j):
            alone = jnp.logical_and(core == 0, j == 3)

            @pl.when(jnp.logical_not(alone))
            def _():
                part_hop(j).wait_recv()

            total = dkv[place.own_tile(j)] * factor
            total = (total + jnp.where(alone, 0.0, landed[j].astype(f32))).astype(bf16)
            for b in range(4):
                m = j * 4 + b
                stage2[m, 0:T] = total[b * T : (b + 1) * T]
                send_to(place, *key_hop(m))

        def step(j, k_tile, diagonal):
            rows = keys[k_tile]
            scores = dot_nt(rows, queries[j])
            if diagonal:
                scores = causal(scores)
            weights = jnp.exp2(scores - lse_ref[j])
            slopes = (weights * (dot_nt(rows[:, 0:128], gp[j]) - delta[j])).astype(bf16)
            weights = weights.astype(bf16)
            dkv[k_tile] += dot(weights, gp[j]) + dot(slopes, queries[j, :, 0:128])
            dq[j] += dot(kt[k_tile], slopes)

        def hooks(n):
            for stage in range(5):

                @pl.when(n == HOOKS[stage])
                def _(stage=stage):
                    for sums_of in main:
                        sums_of.advance(stage)
                    if stage > 0:
                        for sums_of in outs:
                            sums_of.advance(stage - 1)

            @pl.when(n == HOOKS[5])
            def _():
                for p, sums_of in enumerate(main):
                    total = sums_of.last()
                    for k in range(COUNTS[p]):
                        mid.store(p + 6 * k, total[k])
                for sums_of in outs:
                    sums_of.advance(4)

            @pl.when(n == HOOKS[6])
            def _():
                for u, sums_of in enumerate(outs):
                    mid.store(16 + u, sums_of.last()[0])
                mid.start()

            @pl.when(n == HOOKS[7])
            def _():
                mid.finish()

        turn = lax.div(place.head, 4)

        def owned(k_tile):
            return lax.rem(lax.div(k_tile + 1, 2), 2) == core

        def key_tile(i, n):
            k_tile = key_order(place, i)
            skip = 0
            for j in range(4):
                skip = skip + jnp.where(place.own_tile(j) < k_tile, 1, 0)

            def query_tile(at, n):
                hooks(n)
                j = jnp.where(k_tile == 0, lax.rem(at + turn, 4), at)
                diagonal = place.own_tile(j) == k_tile

                @pl.when(diagonal)
                def _():
                    step(j, k_tile, True)

                @pl.when(jnp.logical_not(diagonal))
                def _():
                    step(j, k_tile, False)

                @pl.when(k_tile == 0)
                def _():
                    packed = pack_transposed(dq[j] * SCALE)
                    for b in range(4):
                        m = j * 4 + b
                        stage2[m, T:GRAD] = packed[b]
                        send_to(place, *query_hop(m))

                return n + 1

            n = lax.fori_loop(skip, 4, query_tile, n)
            mine = owned(k_tile)
            before = key_order(place, jnp.maximum(i - 1, 0))

            @pl.when(jnp.logical_and(jnp.logical_not(mine), jnp.logical_not(jnp.logical_and(core == 1, k_tile == 7))))
            def _():
                give(lax.div(k_tile, 2))

            @pl.when(jnp.logical_and(i > 0, owned(before)))
            def _():
                take(lax.div(before, 2))

            return n

        lax.fori_loop(0, TILES, key_tile, 0)

        @pl.when(core == 0)
        def _():
            take(0)

    pl.run_scoped(
        attention,
        pltpu.VMEM((BLOCKS, PACK, 128), bf16),
        pltpu.VMEM((4, HD, TILE), f32),
        pltpu.VMEM((3, TILE, 128), f32),
        pltpu.VMEM((TILES, TILE, 256), bf16),
        pltpu.VMEM((4, TILE, 256), bf16),
        pltpu.VMEM((TILES, HD, TILE), bf16),
        pltpu.VMEM((4, TILE, 128), bf16),
        pltpu.VMEM((4, 1, TILE), f32),
        pltpu.VMEM((4, HD, TILE), f32),
        pltpu.VMEM((TILES, TILE, 128), f32),
    )

    def last(w_scr, dn, a2t):
        weight = pltpu.make_async_copy(w_qkv, w_scr, l_sem.at[2])
        weight.start()
        a_hop.wait_recv()
        a2t[...] = transposed(a2[...])
        for m in range(8):
            for h in (2 * m, 2 * m + 1):
                arrived(dqkv_in.at[h, 0:T], b_recv.at[0, h])
                arrived(dqkv_in.at[h, T:GRAD], b_recv.at[1, h])
            lo, hi = swap_halves(dqkv_in[2 * m, T:GRAD], dqkv_in[2 * m + 1, T:GRAD])
            dk, dv = swap_halves(dqkv_in[2 * m, 0:T], dqkv_in[2 * m + 1, 0:T])
            dn[0:HT, 128 * m : 128 * m + 128] = lo
            dn[HT:T, 128 * m : 128 * m + 128] = hi
            dn[:, D + 128 * m : D + 128 * m + 128] = dk
            dn[:, 2 * D + 128 * m : 2 * D + 128 * m + 128] = dv
            at = 128 * (m % 4)
            dhalf[m // 4, 0:HT, at : at + 128] = lo
            dhalf[m // 4, HT:T, at : at + 128] = hi
            dhalf[m // 4, 0:T, 512 + at : 512 + at + 128] = dk
            dhalf[m // 4, 0:T, 1024 + at : 1024 + at + 128] = dv
        d_hop = across(7, dhalf.at[1 - core, 0:T], dhalf.at[1 - core, T : 2 * T])
        d_hop.start()
        d_hop.wait_recv()
        for u in range(6):
            spread(gs3, u, u, dot(a2t[...], dhalf[core, :, u * 256 : u * 256 + 256]).astype(bf16))
            sums[u].start()
        weight.wait()
        x = x_ref[0].astype(f32)
        scale = lax.rsqrt(jnp.mean(x * x, axis=-1, keepdims=True) + EPS)
        dh1 = dot_nt(dn[...], w_scr[...])
        gain1_grad = jnp.sum(dh1 * x * scale, axis=0, keepdims=True)
        row = lax.broadcasted_iota(jnp.int32, (128, D), 0)
        both = jnp.where(row == 0, gain1_grad, jnp.where(row == 1, gain2_grad[...], 0.0))
        columns = both.T.astype(bf16)
        for chip in range(64):
            y_lo, cx, z, y_hi = chip // 32, chip // 8 % 4, chip // 2 % 4, chip % 2
            gain_acc[0, position(0, y_lo, cx, z, y_hi)] = columns[chip * 16 : chip * 16 + 16]
        gains.start()
        dxn = dh1 * gain1_ref[...]
        back = scale * dxn - x * (scale * scale * scale) * jnp.mean(dxn * x, axis=-1, keepdims=True)
        dx_ref[0] = (dx1s[...] + back).astype(bf16)

        for stage in range(5):
            for sums_of in sums + [gains]:
                sums_of.advance(stage)
        for u in range(6):
            fin3[u] = sums[u].last()[0].reshape(2, 8, 256)
        gain_rows = gains.last()[0]
        fin3[6] = jnp.concatenate([gain_rows, jnp.zeros((16, 128), f32)], axis=1).reshape(2, 8, 256)
        aside = across(8, fin3.at[:, 1 - core], side3)
        aside.start()
        aside.wait_recv()
        mine, other = core, 1 - core
        for u in range(6):
            at = (u // 2) * D + (u % 2) * 256
            qkv_out[:, pl.ds(at + mine * 512, 256)] = fin3[u, mine]
            qkv_out[:, pl.ds(at + other * 512, 256)] = side3[u]
        both = fin3[6, mine][:, 0:128] + side3[6][:, 0:128]
        wide = jnp.concatenate([both] + [jnp.zeros((8, 128), f32)] * 15, axis=0).T
        gain_out[...] = wide[0:8]
        for hop in (a_hop, d_hop, aside):
            hop.wait_send()

    pl.run_scoped(
        last,
        pltpu.VMEM((D, 3 * D), bf16),
        pltpu.VMEM((T, 3 * D), bf16),
        pltpu.VMEM((D, 2 * T), bf16),
    )

    def finish(n):
        sent_to(place, *da_hop(n))
        sent_to(place, *key_hop(n))
        sent_to(place, *query_hop(n))

    loop(16, finish)

    def given(j, carry):
        part_hop(j).wait_send()
        return carry

    lax.fori_loop(0, 4 - core, given, 0)
    for sums_of in main + outs + sums + [gains]:
        sums_of.finish()


def rest_call(o_in, frames, out_grad, gain1, gain2, lse, w_out, w_up, w_down, w_qkv, pk, ot):
    dma = pltpu.SemaphoreType.DMA
    return pl.pallas_call(
        rest_kernel,
        name="feed_forward_and_back",
        out_shape=(
            jax.ShapeDtypeStruct((1, T, D), bf16),
            jax.ShapeDtypeStruct((1, T, D), bf16),
            jax.ShapeDtypeStruct((8, 3 * D), f32),
            jax.ShapeDtypeStruct((8, 128), f32),
            jax.ShapeDtypeStruct((8, FF), f32),
            jax.ShapeDtypeStruct((8, D), f32),
            jax.ShapeDtypeStruct((32, D), f32),
        ),
        in_specs=[VM] * 6 + [ANY] * 6,
        out_specs=(VM,) * 7,
        scratch_shapes=[
            pltpu.VMEM((2 * T, D), bf16),
            pltpu.VMEM((2 * T, D), bf16),
            pltpu.VMEM((2 * T, D), bf16),
            pltpu.VMEM((T, D), f32),
            pltpu.VMEM((T, D), f32),
            pltpu.VMEM((2, 2 * T, 512), bf16),
            pltpu.VMEM((T, D), f32),
            pltpu.VMEM((1, D), f32),
            pltpu.VMEM((16, 64, 16, 256), bf16),
            pltpu.VMEM((16, 64, 16, 256), bf16),
            pltpu.VMEM((2, 64, 16, 256), bf16),
            pltpu.VMEM((2, 64, 16, 256), bf16),
            pltpu.VMEM((16, HT, 128), bf16),
            pltpu.VMEM((16, HT, 128), bf16),
            pltpu.VMEM((4, TILE, 128), bf16),
            pltpu.VMEM((4, TILE, 128), bf16),
            pltpu.VMEM((16, GRAD, 128), bf16),
            pltpu.VMEM((16, GRAD, 128), bf16),
            pltpu.VMEM((18, 2, 8, 256), f32),
            pltpu.VMEM((10, 8, 256), f32),
            pltpu.VMEM((2, 4, 2, 8, 256), f32),
            pltpu.VMEM((2 * T, D), bf16),
            pltpu.VMEM((2, 2 * T, 1536), bf16),
            pltpu.VMEM((6, 64, 16, 256), bf16),
            pltpu.VMEM((6, 64, 16, 256), bf16),
            pltpu.VMEM((1, 64, 16, 128), bf16),
            pltpu.VMEM((1, 64, 16, 128), bf16),
            pltpu.VMEM((7, 2, 8, 256), f32),
            pltpu.VMEM((7, 8, 256), f32),
            dma((9,)), dma((3,)), dma((9,)), dma((9,)), dma((4,)), dma((4,)), dma((16,)), dma((16,)),
            dma((16,)), dma((16,)), dma((2, 16)), dma((2, 16)), dma((8, 6)), dma((8, 6)), dma((7, 6)), dma((7, 6)),
            dma((6,)),
        ],
        compiler_params=params(1),
    )(o_in, frames, out_grad, gain1, gain2, lse, w_out, w_up, w_down, w_qkv, pk, ot)


def deliver_kernel(*refs):
    count = len(refs) // 2 - 2
    sources, gains, targets = refs[:count], refs[count], refs[count + 1 : 2 * count + 1]
    gain1, gain2, sem = refs[2 * count + 1 :]
    del sem
    for k in range(count):
        targets[k][...] = sources[k][...]
    gain1[...] = gains[0, 0:8]
    gain2[...] = gains[1, 0:8]


def deliver(arrays, gains):
    count = len(arrays)
    small = jax.ShapeDtypeStruct((8,), f32)
    return pl.pallas_call(
        deliver_kernel,
        name="deliver",
        out_shape=tuple(jax.ShapeDtypeStruct(v.shape, v.dtype) for v in arrays) + (small, small),
        in_specs=[VM] * (count + 1),
        out_specs=(VM,) * (count + 2),
        scratch_shapes=[pltpu.SemaphoreType.DMA((count,))],
    )(*arrays, gains)


def shards(frames, segment_ids, norm1_gain, w_qkv, w_out, norm2_gain, w_up, w_down, out_grad):
    gain1, gain2 = norm1_gain[None], norm2_gain[None]
    pk, o_in, lse, ot = forward_call(frames, segment_ids, gain1, w_qkv)
    y, dx, qkv_sum, gain_sums, up_sum, out_sum, down_sum = rest_call(
        o_in, frames, out_grad, gain1, gain2, lse, w_out, w_up, w_down, w_qkv, pk, ot
    )
    y, dx, qkv_sum, out_sum, up_sum, down_sum, gain1_sum, gain2_sum = deliver(
        (y, dx, qkv_sum, out_sum, up_sum, down_sum), gain_sums
    )
    return (y, dx, gain1_sum, qkv_sum, out_sum, gain2_sum, up_sum, down_sum)


def solution(mesh):
    return jax.shard_map(
        shards,
        mesh=mesh,
        in_specs=(
            P("row", "seq", None),
            P("row", "seq"),
            P(),
            P(),
            P(),
            P(),
            P(),
            P(),
            P("row", "seq", None),
        ),
        out_specs=(
            P("row", "seq", None),
            P("row", "seq", None),
            P(("seq", "row")),
            P(("seq", "row"), None),
            P(("seq", "row"), None),
            P(("seq", "row")),
            P(("seq", "row"), None),
            P(("seq", "row"), None),
        ),
        check_vma=False,
    )
```

time: 216 us -> 203 us (0.940)
  Pallas kernels: 215 us -> 201 us
    pallas_call x4 -> x1, Pallas kernels: 181 us -> 142 us  [rest_call(): pl.pallas_call(rest_kernel, name='feed_forward_and_back', out_shape=(jax....]
    pallas_call x1, Pallas kernels: 31.6 us -> 56.7 us  [forward_call(): pl.pallas_call(forward_kernel, name='attention', out_shape=(jax.ShapeDtyp...]
where the time goes in v3:
time: 203 us; the launch traced here: 202 us
  Pallas kernels  201 us (99%)
    pallas_call x1, Pallas kernels, rest_call(): pl.pallas_call(rest_kernel, name='feed_forward_and_back', out_shape=(jax....  142 us
    pallas_call x1, Pallas kernels, forward_call(): pl.pallas_call(forward_kernel, name='attention', out_shape=(jax.ShapeDtyp...  56.7 us

profile of v3, /device:TPU:1, one launch (start us, length us, event | category | flops | bytes accessed | tf_op | source)
XLA Modules:
  0.0 202.2 jit_solution(14696099708808747864)
XLA Ops:
  0.6 56.7 %attention.1 = (bf16[32,304,128]{2,1,0:T(8,128)(2,1)}, bf16[16,96,128]{2,1,0:T(8,128)(2,1)}, f32[4,1,768]{2,1,0:T(1,128)}, f32[4,64,768]{2,1,0:T(8,128)}) custom-call(bf16[1,192,1024]{2,1,0:T(8,128)(2,1)} %x_ref.3, s32[1,192]{1,0:T(1,128)} %seg_ref.1, f32[1,1024]{1,0:T(1,128)} %bitcast.2, bf16[1024,3072]{1,0:T(8,128)(2,1)} %w_qkv.1), custom_call_target="tpu_custom_call" | custom-call | tf_op jit(solution)/shard_map/attention/pallas_call | solution.py:383
  57.3 142.4 %feed_forward_and_back.1 = (bf16[1,192,1024]{2,1,0:T(8,128)(2,1)}, bf16[1,192,1024]{2,1,0:T(8,128)(2,1)}, f32[8,3072]{1,0:T(8,128)}, f32[8,128]{1,0:T(8,128)}, f...) custom-call(bf16[16,96,128]{2,1,0:T(8,128)(2,1)} %get-tuple-element.27.o_in, bf16[1,192,1024]{2,1,0:T(8,128)(2,1)} %x_ref.3, ...), custom_call_target="tpu_custom_call" | custom-call | tf_op jit(solution)/shard_map/feed_forward_and_back/pallas_call | solution.py:1064
  199.7 2.3 %deliver.1 = (bf16[1,192,1024]{2,1,0:T(8,128)(2,1)}, bf16[1,192,1024]{2,1,0:T(8,128)(2,1)}, f32[8,3072]{1,0:T(8,128)}, f32[8,1024]{1,0:T(8,128)}, f32[8,4096]{1,...) custom-call(bf16[1,192,1024]{2,1,0:T(8,128)(2,1)} %get-tuple-element.31.refs_0_, ...), custom_call_target="tpu_custom_call" | custom-call | tf_op jit(solution)/shard_map/deliver/pallas_call | solution.py:1130

commit v4 on v3

--- a/solution.py
+++ b/solution.py
@@ -425,22 +425,52 @@
     return [FIRST(x), FIRST(y), FIRST(z), SECOND(x), SECOND(y), SECOND(z)]
 
 
+ORDER = [[(p + k) % 3 + 3 * (p // 3) for k in range(3)] + [k + 3 * (1 - p // 3) for k in range(3)] for p in range(6)]
+
+
 def position(part, y_lo, x, z, y_hi):
     bits = chip_bits(x, y_hi * 2 + y_lo, z)
     at = 0
     for k in range(6):
-        at = at * 2 + bits[(part + k) % 6]
+        at = at * 2 + bits[ORDER[part][k]]
     return at
 
 
+class Net:
+    def __init__(self, place):
+        self.x, self.z = lax.div(place.head, 4), lax.rem(place.head, 4)
+        self.y = place.y_hi * 2 + place.y_lo
+        self.core = place.core
+        self.bits = [lax.rem(lax.div(c + 1, 2), 2) for c in (self.x, self.y, self.z)]
+        self.bits += [lax.div(c, 2) for c in (self.x, self.y, self.z)]
+
+    def across(self, pairing, mask):
+        moved = []
+        for k, c in enumerate((self.x, self.y, self.z)):
+            far = c + 1 - 2 * lax.rem(c, 2) if pairing == 0 else 3 - c
+            moved.append(far if mask >> (2 - k) & 1 else c)
+        x, y, z = moved
+        return (lax.rem(y, 2) * 16 + x * 4 + z, lax.div(y, 2) * 2 + self.core)
+
+    def neighbour(self, dim):
+        return self.across(dim // 3, 4 >> dim % 3)
+
+    def greet(self, barrier):
+        for pairing in range(2):
+            for mask in range(1, 8):
+                greet(barrier, self.across(pairing, mask))
+
+    GREETINGS = 14
+
+
 class Part:
-    def __init__(self, net, acc, land, at, count, turn, send, recv, pieces=()):
-        self.net, self.acc, self.land, self.turn, self.pieces = net, acc, land, turn, pieces
-        self.units = pl.ds(at, count)
+    def __init__(self, net, acc, land, tail, at, tail_at, count, part, send, recv, pieces=()):
+        self.net, self.acc, self.land, self.tail, self.part, self.pieces = net, acc, land, tail, part, pieces
+        self.units, self.tail_units = pl.ds(at, count), pl.ds(tail_at, count)
         self.count, self.send, self.recv = count, send, recv
 
     def bit(self, stage):
-        return self.net.bits[(self.turn + stage) % 6]
+        return self.net.bits[ORDER[self.part][stage]]
 
     def base(self, stage):
         at = 0
@@ -459,7 +489,7 @@
             self.land.at[self.units, pl.ds(self.landing(stage), half)],
             self.send[0].at[self.send[1], stage],
             self.recv[0].at[self.recv[1], stage],
-            self.net.neighbours[(self.turn + stage) % 6],
+            self.net.neighbour(ORDER[self.part][stage]),
         )
 
     def start(self):
@@ -468,14 +498,16 @@
     def hops(self, stage):
         return list(self.pieces) if stage == 0 and self.pieces else [self.hop(stage)]
 
+    def total(self, base, landed, group):
+        mine = self.acc[self.units, pl.ds(base, group)].astype(f32)
+        return (mine + self.land[self.units, pl.ds(landed, group)].astype(f32)).astype(bf16)
+
     def add(self, base, landed, count):
         group = min(count, 4)
 
         def body(i):
             here = pl.ds(base + i * group, group)
-            there = pl.ds(landed + i * group, group)
-            total = self.acc[self.units, here].astype(f32) + self.land[self.units, there].astype(f32)
-            self.acc[self.units, here] = total.astype(bf16)
+            self.acc[self.units, here] = self.total(base + i * group, landed + i * group, group)
 
         loop(count // group, body)
 
@@ -489,40 +521,85 @@
         self.hop(stage + 1).start()
         self.add(base + bit * half, landed + bit * half, half)
 
-    def last(self):
-        self.hop(5).wait_recv()
-        return (
-            self.acc[self.units, pl.ds(self.base(5), 1)].astype(f32)
-            + self.land[self.units, pl.ds(self.landing(5), 1)].astype(f32)
-        )[:, 0]
+    def settle(self):
+        self.hop(2).wait_recv()
+        for at in range(0, 8, 4):
+            self.tail[self.tail_units, at : at + 4] = self.total(self.base(2) + at, self.landing(2) + at, 4)
 
     def finish(self):
-        for stage in range(6):
+        for stage in range(3):
             for hop in self.hops(stage):
                 hop.wait_send()
 
 
-class Net:
-    def __init__(self, place):
-        x, z = lax.div(place.head, 4), lax.rem(place.head, 4)
-        y = place.y_hi * 2 + place.y_lo
-        self.bits = [
-            lax.rem(lax.div(x + 1, 2), 2), lax.rem(lax.div(y + 1, 2), 2), lax.rem(lax.div(z + 1, 2), 2),
-            lax.div(x, 2), lax.div(y, 2), lax.div(z, 2),
+class Exchange:
+    def __init__(self, net, pairing, tail, land, send, recv):
+        self.net, self.pairing, self.tail, self.land, self.send, self.recv = net, pairing, tail, land, send, recv
+
+    def row(self, mask):
+        at = 0
+        for k in range(3):
+            bit = self.net.bits[3 * self.pairing + k]
+            at = at + (1 - bit if mask >> (2 - k) & 1 else bit) * (4 >> k)
+        return at
+
+    def hop(self, mask):
+        return remote(
+            self.tail.at[:, self.row(mask)], self.land.at[mask - 1],
+            self.send.at[mask - 1], self.recv.at[mask - 1], self.net.across(self.pairing, mask),
+        )
+
+    def start(self):
+        for mask in range(1, 8):
+            self.hop(mask).start()
+
+    def result(self, unit):
+        total = self.tail[unit, self.row(0)].astype(f32)
+        for mask in range(1, 8):
+            total = total + self.land[mask - 1, unit].astype(f32)
+        return total
+
+    def wait(self):
+        for mask in range(1, 8):
+            self.hop(mask).wait_recv()
+
+    def finish(self):
+        for mask in range(1, 8):
+            self.hop(mask).wait_send()
+
+
+class Shared:
+    def __init__(self, net, place, value, land, send, recv):
+        self.net, self.place, self.value, self.land, self.send, self.recv = net, place, value, land, send, recv
+
+    def hops(self, pairing):
+        if pairing == 2:
+            return [
+                remote(self.value.at[2], self.land.at[2, 0], self.send.at[2, 0], self.recv.at[2, 0], self.place.partner)
+            ]
+        return [
+            remote(
+                self.value.at[pairing], self.land.at[pairing, mask - 1],
+                self.send.at[pairing, mask - 1], self.recv.at[pairing, mask - 1], self.net.across(pairing, mask),
+            )
+            for mask in range(1, 8)
         ]
 
-        def device(x, y, z):
-            return (lax.rem(y, 2) * 16 + x * 4 + z, lax.div(y, 2) * 2 + place.core)
-
-        flip = lambda c: c + 1 - 2 * lax.rem(c, 2)
-        self.neighbours = [
-            device(flip(x), y, z), device(x, flip(y), z), device(x, y, flip(z)),
-            device(3 - x, y, z), device(x, 3 - y, z), device(x, y, 3 - z),
-        ]
-
-    def greet(self, barrier):
-        for device in self.neighbours:
-            greet(barrier, device)
+    def start(self, pairing):
+        for hop in self.hops(pairing):
+            hop.start()
+
+    def take(self, pairing):
+        total = self.value[pairing]
+        for k, hop in enumerate(self.hops(pairing)):
+            hop.wait_recv()
+            total = total + self.land[pairing, k]
+        self.value[pairing + 1] = total
+
+    def finish(self):
+        for pairing in range(3):
+            for hop in self.hops(pairing):
+                hop.wait_send()
 
 
 TURN = [u % 6 for u in range(18)]
@@ -624,16 +701,17 @@
 CUBE = 0.044715
 
 
-HOOKS = (3, 7, 10, 12, 13, 14, 15, 17)
+HOOKS = (1, 7, 18, 19, 20, 22)
 
 
 def rest_kernel(
     o_in, x_ref, dy_ref, gain1_ref, gain2_ref, lse_ref, w_out, w_up, w_down, w_qkv, pk_in, ot_in,
     y_ref, dx_ref, qkv_out, gain_out, up_out, out_out, down_out,
-    o2, b2, dm2, yside, hside, da_side, dx1s, gain2_grad, gs, land, outg, land2, da_in, stage1,
-    part, landed, dqkv_in, stage2, fin, side, down, a2, dhalf, gs3, land3, gain_acc, gain_land, fin3, side3,
+    o2, b2, dm2, yside, hside, da_side, gain2_grad, gs, land, outg, land2, tail, tail_land, da_in, stage1,
+    part, landed, dqkv_in, stage2, fin, side, down, a2, dhalf, gs3, land3, tail3, tail_land3, gain_value, gain_land,
+    fin3, side3,
     w_sem, l_sem, p_send, p_recv, q_send, q_recv, h_send, h_recv, a_send, a_recv, b_send, b_recv,
-    n_send, n_recv, t_send, t_recv, m_sem,
+    n_send, n_recv, t_send, t_recv, e_send, e_recv, g_send, g_recv, m_sem,
 ):
     place = Place()
     core = place.core
@@ -646,20 +724,29 @@
         bit = net.bits[TURN[unit]]
         return remote(
             gs.at[SLOT[unit], pl.ds((1 - bit) * 32, 32)], land.at[SLOT[unit], 0:32],
-            h_send.at[unit], h_recv.at[unit], net.neighbours[TURN[unit]],
+            h_send.at[unit], h_recv.at[unit], net.neighbour(TURN[unit]),
         )
 
+    tails = [tail.at[0:9], tail.at[9:18]]
     main = [
         Part(
-            net, gs, land, STARTS[p], COUNTS[p], p, (n_send, p), (n_recv, p),
+            net, gs, land, tail, STARTS[p], STARTS[p], COUNTS[p], p, (n_send, p), (n_recv, p),
             [first_hop(p + 6 * k) for k in range(COUNTS[p])],
         )
         for p in range(6)
     ]
-    outs = [Part(net, outg, land2, u, 1, TURN[16 + u], (n_send, 6 + u), (n_recv, 6 + u)) for u in range(2)]
+    outs = [
+        Part(net, outg, land2, tail, u, 16 + u, 1, TURN[16 + u], (n_send, 6 + u), (n_recv, 6 + u))
+        for u in range(2)
+    ]
+    ends = [Exchange(net, 1 - g, tails[g], tail_land.at[g], e_send.at[g], e_recv.at[g]) for g in range(2)]
     mid = MidSums(place, fin, side, down, m_sem, up_out, out_out, down_out)
-    sums = [Part(net, gs3, land3, u, 1, u, (t_send, u), (t_recv, u)) for u in range(6)]
-    gains = Part(net, gain_acc, gain_land, 0, 1, 0, (t_send, 6), (t_recv, 6))
+    sums = [Part(net, gs3, land3, tail3, u, u, 1, u, (t_send, u), (t_recv, u)) for u in range(6)]
+    ends3 = [
+        Exchange(net, 1 - g, tail3.at[3 * g : 3 * g + 3], tail_land3.at[g], e_send.at[2 + g], e_recv.at[2 + g])
+        for g in range(2)
+    ]
+    gains = Shared(net, place, gain_value, gain_land, g_send, g_recv)
 
     barrier = pltpu.get_barrier_semaphore()
     greet_all(place, barrier, place.block_device)
@@ -693,7 +780,7 @@
             lo, hi = swap_halves(o_in[2 * m], o_in[2 * m + 1])
             o2[0:HT, 128 * m : 128 * m + 128] = lo
             o2[HT:T, 128 * m : 128 * m + 128] = hi
-        pl.semaphore_wait(barrier, 2 * (16 - place.self_count) + 6 + mid.greetings())
+        pl.semaphore_wait(barrier, 2 * (16 - place.self_count) + Net.GREETINGS + mid.greetings())
         dm_hop = across(0, dm2.at[0:T], dm2.at[T : 2 * T])
         o_hop = across(1, o2.at[0:T], o2.at[T : 2 * T])
         dm_hop.start()
@@ -763,7 +850,7 @@
         dn = dh2 * gain2_ref[...]
         back = scale1 * dn - x1 * (scale1 * scale1 * scale1) * jnp.mean(dn * x1, axis=-1, keepdims=True)
         dx1 = dy_ref[0].astype(f32) + back
-        dx1s[...] = dx1
+        hside[...] = dx1
         da = dx1.astype(bf16)
         da_side[0, 0:T] = da[:, 0:512]
         da_side[1, 0:T] = da[:, 512:1024]
@@ -802,6 +889,35 @@
         pltpu.VMEM((2 * T, D), f32),
     )
 
+    def hook(which):
+        if which < 2:
+            for sums_of in main:
+                sums_of.advance(which)
+            if which == 1:
+                for sums_of in outs:
+                    sums_of.advance(0)
+        elif which == 2:
+            for sums_of in main:
+                sums_of.settle()
+            ends[0].start()
+            for sums_of in outs:
+                sums_of.advance(1)
+        elif which == 3:
+            for sums_of in outs:
+                sums_of.settle()
+            ends[1].start()
+        elif which == 4:
+            for end in ends:
+                end.wait()
+            for unit in range(16):
+                group = SLOT[unit] // 9
+                mid.store(unit, ends[group].result(SLOT[unit] - 9 * group))
+            for u in range(2):
+                mid.store(16 + u, ends[1].result(7 + u))
+            mid.start()
+        else:
+            mid.finish()
+
     def key_hop(m):
         return (
             stage2.at[m, 0:T], dqkv_in.at[place.head, 0:T], b_send.at[0, m], b_recv.at[0, place.head],
@@ -876,34 +992,12 @@
             dq[j] += dot(kt[k_tile], slopes)
 
         def hooks(n):
-            for stage in range(5):
-
-                @pl.when(n == HOOKS[stage])
-                def _(stage=stage):
-                    for sums_of in main:
-                        sums_of.advance(stage)
-                    if stage > 0:
-                        for sums_of in outs:
-                            sums_of.advance(stage - 1)
-
-            @pl.when(n == HOOKS[5])
-            def _():
-                for p, sums_of in enumerate(main):
-                    total = sums_of.last()
-                    for k in range(COUNTS[p]):
-                        mid.store(p + 6 * k, total[k])
-                for sums_of in outs:
-                    sums_of.advance(4)
-
-            @pl.when(n == HOOKS[6])
-            def _():
-                for u, sums_of in enumerate(outs):
-                    mid.store(16 + u, sums_of.last()[0])
-                mid.start()
-
-            @pl.when(n == HOOKS[7])
-            def _():
-                mid.finish()
+            for which in range(6):
+                if HOOKS[which] < STEPS:
+
+                    @pl.when(n == HOOKS[which])
+                    def _(which=which):
+                        hook(which)
 
         turn = lax.div(place.head, 4)
 
@@ -958,6 +1052,10 @@
         @pl.when(core == 0)
         def _():
             take(0)
+
+        for which in range(6):
+            if HOOKS[which] == STEPS:
+                hook(which)
 
     pl.run_scoped(
         attention,
@@ -1004,35 +1102,50 @@
         scale = lax.rsqrt(jnp.mean(x * x, axis=-1, keepdims=True) + EPS)
         dh1 = dot_nt(dn[...], w_scr[...])
         gain1_grad = jnp.sum(dh1 * x * scale, axis=0, keepdims=True)
-        row = lax.broadcasted_iota(jnp.int32, (128, D), 0)
-        both = jnp.where(row == 0, gain1_grad, jnp.where(row == 1, gain2_grad[...], 0.0))
-        columns = both.T.astype(bf16)
-        for chip in range(64):
-            y_lo, cx, z, y_hi = chip // 32, chip // 8 % 4, chip // 2 % 4, chip % 2
-            gain_acc[0, position(0, y_lo, cx, z, y_hi)] = columns[chip * 16 : chip * 16 + 16]
-        gains.start()
+        both = [gain1_grad[:, 128 * k : 128 * k + 128] for k in range(8)]
+        both += [gain2_grad[:, 128 * k : 128 * k + 128] for k in range(8)]
+        gain_value[0] = jnp.concatenate(both, axis=0)
+        gains.start(0)
         dxn = dh1 * gain1_ref[...]
         back = scale * dxn - x * (scale * scale * scale) * jnp.mean(dxn * x, axis=-1, keepdims=True)
-        dx_ref[0] = (dx1s[...] + back).astype(bf16)
-
-        for stage in range(5):
-            for sums_of in sums + [gains]:
+        dx_ref[0] = (hside[...] + back).astype(bf16)
+
+        for stage in range(2):
+            for sums_of in sums:
                 sums_of.advance(stage)
-        for u in range(6):
-            fin3[u] = sums[u].last()[0].reshape(2, 8, 256)
-        gain_rows = gains.last()[0]
-        fin3[6] = jnp.concatenate([gain_rows, jnp.zeros((16, 128), f32)], axis=1).reshape(2, 8, 256)
+            gains.take(stage)
+            gains.start(stage + 1)
+            for which in range(6):
+                if HOOKS[which] == STEPS + 1 + stage:
+                    hook(which)
+        for g in range(2):
+            for sums_of in sums[3 * g : 3 * g + 3]:
+                sums_of.settle()
+            ends3[g].start()
+        gains.take(2)
+        for which in range(6):
+            if HOOKS[which] == STEPS + 3:
+                hook(which)
+        for g in range(2):
+            ends3[g].wait()
+            for u in range(3):
+                fin3[3 * g + u] = ends3[g].result(u).reshape(2, 8, 256)
         aside = across(8, fin3.at[:, 1 - core], side3)
         aside.start()
+        for which in range(6):
+            if HOOKS[which] == STEPS + 4:
+                hook(which)
+        shard = place.s * 4 + place.r
+        turn = lax.rem(128 - lax.rem(shard, 16) * 8, 128)
+        for k in range(2):
+            row = gain_value[3, pl.ds(8 * k + lax.div(shard, 16), 1)]
+            gain_out[k : k + 1] = pltpu.roll(row, turn, 1)
         aside.wait_recv()
         mine, other = core, 1 - core
         for u in range(6):
             at = (u // 2) * D + (u % 2) * 256
             qkv_out[:, pl.ds(at + mine * 512, 256)] = fin3[u, mine]
             qkv_out[:, pl.ds(at + other * 512, 256)] = side3[u]
-        both = fin3[6, mine][:, 0:128] + side3[6][:, 0:128]
-        wide = jnp.concatenate([both] + [jnp.zeros((8, 128), f32)] * 15, axis=0).T
-        gain_out[...] = wide[0:8]
         for hop in (a_hop, d_hop, aside):
             hop.wait_send()
 
@@ -1055,7 +1168,7 @@
         return carry
 
     lax.fori_loop(0, 4 - core, given, 0)
-    for sums_of in main + outs + sums + [gains]:
+    for sums_of in main + outs + sums + ends + ends3 + [gains]:
         sums_of.finish()
 
 
@@ -1082,12 +1195,13 @@
             pltpu.VMEM((T, D), f32),
             pltpu.VMEM((T, D), f32),
             pltpu.VMEM((2, 2 * T, 512), bf16),
-            pltpu.VMEM((T, D), f32),
             pltpu.VMEM((1, D), f32),
             pltpu.VMEM((16, 64, 16, 256), bf16),
-            pltpu.VMEM((16, 64, 16, 256), bf16),
+            pltpu.VMEM((16, 56, 16, 256), bf16),
             pltpu.VMEM((2, 64, 16, 256), bf16),
-            pltpu.VMEM((2, 64, 16, 256), bf16),
+            pltpu.VMEM((2, 56, 16, 256), bf16),
+            pltpu.VMEM((18, 8, 16, 256), bf16),
+            pltpu.VMEM((2, 7, 9, 16, 256), bf16),
             pltpu.VMEM((16, HT, 128), bf16),
             pltpu.VMEM((16, HT, 128), bf16),
             pltpu.VMEM((4, TILE, 128), bf16),
@@ -1100,14 +1214,16 @@
             pltpu.VMEM((2 * T, D), bf16),
             pltpu.VMEM((2, 2 * T, 1536), bf16),
             pltpu.VMEM((6, 64, 16, 256), bf16),
-            pltpu.VMEM((6, 64, 16, 256), bf16),
-            pltpu.VMEM((1, 64, 16, 128), bf16),
-            pltpu.VMEM((1, 64, 16, 128), bf16),
-            pltpu.VMEM((7, 2, 8, 256), f32),
-            pltpu.VMEM((7, 8, 256), f32),
+            pltpu.VMEM((6, 56, 16, 256), bf16),
+            pltpu.VMEM((6, 8, 16, 256), bf16),
+            pltpu.VMEM((2, 7, 3, 16, 256), bf16),
+            pltpu.VMEM((4, 16, 128), f32),
+            pltpu.VMEM((3, 7, 16, 128), f32),
+            pltpu.VMEM((6, 2, 8, 256), f32),
+            pltpu.VMEM((6, 8, 256), f32),
             dma((9,)), dma((3,)), dma((9,)), dma((9,)), dma((4,)), dma((4,)), dma((16,)), dma((16,)),
-            dma((16,)), dma((16,)), dma((2, 16)), dma((2, 16)), dma((8, 6)), dma((8, 6)), dma((7, 6)), dma((7, 6)),
-            dma((6,)),
+            dma((16,)), dma((16,)), dma((2, 16)), dma((2, 16)), dma((8, 3)), dma((8, 3)), dma((6, 3)), dma((6, 3)),
+            dma((4, 7)), dma((4, 7)), dma((3, 7)), dma((3, 7)), dma((6,)),
         ],
         compiler_params=params(1),
     )(o_in, frames, out_grad, gain1, gain2, lse, w_out, w_up, w_down, w_qkv, pk, ot)

time: 203 us -> 186 us (0.916)
  Pallas kernels: 201 us -> 185 us
    pallas_call x1, Pallas kernels: 142 us -> 126 us  [rest_call(): pl.pallas_call(rest_kernel, name='feed_forward_and_back', out_shape=(jax....]
where the time goes in v4:
time: 186 us
  Pallas kernels  185 us (99%)
    pallas_call x1, Pallas kernels, rest_call(): pl.pallas_call(rest_kernel, name='feed_forward_and_back', out_shape=(jax....  126 us
    pallas_call x1, Pallas kernels, forward_call(): pl.pallas_call(forward_kernel, name='attention', out_shape=(jax.ShapeDtyp...  56.7 us

profile of v4, /device:TPU:1, one launch (start us, length us, event | category | flops | bytes accessed | tf_op | source)
XLA Modules:
  0.0 185.6 jit_solution(7882192252571038551)
XLA Ops:
  0.6 56.7 %attention.1 = (bf16[32,304,128]{2,1,0:T(8,128)(2,1)}, bf16[16,96,128]{2,1,0:T(8,128)(2,1)}, f32[4,1,768]{2,1,0:T(1,128)}, f32[4,64,768]{2,1,0:T(8,128)}) custom-call(bf16[1,192,1024]{2,1,0:T(8,128)(2,1)} %x_ref.3, s32[1,192]{1,0:T(1,128)} %seg_ref.1, f32[1,1024]{1,0:T(1,128)} %bitcast.2, bf16[1024,3072]{1,0:T(8,128)(2,1)} %w_qkv.1), custom_call_target="tpu_custom_call" | custom-call | tf_op jit(solution)/shard_map/attention/pallas_call | solution.py:383
  57.3 125.8 %feed_forward_and_back.1 = (bf16[1,192,1024]{2,1,0:T(8,128)(2,1)}, bf16[1,192,1024]{2,1,0:T(8,128)(2,1)}, f32[8,3072]{1,0:T(8,128)}, f32[8,128]{1,0:T(8,128)}, f...) custom-call(bf16[16,96,128]{2,1,0:T(8,128)(2,1)} %get-tuple-element.27.o_in, bf16[1,192,1024]{2,1,0:T(8,128)(2,1)} %x_ref.3, ...), custom_call_target="tpu_custom_call" | custom-call | tf_op jit(solution)/shard_map/feed_forward_and_back/pallas_call | solution.py:1177
  183.1 2.3 %deliver.1 = (bf16[1,192,1024]{2,1,0:T(8,128)(2,1)}, bf16[1,192,1024]{2,1,0:T(8,128)(2,1)}, f32[8,3072]{1,0:T(8,128)}, f32[8,1024]{1,0:T(8,128)}, f32[8,4096]{1,...) custom-call(bf16[1,192,1024]{2,1,0:T(8,128)(2,1)} %get-tuple-element.31.refs_0_, ...), custom_call_target="tpu_custom_call" | custom-call | tf_op jit(solution)/shard_map/deliver/pallas_call | solution.py:1246

commit v5 on v4

--- a/solution.py
+++ b/solution.py
@@ -173,28 +173,27 @@
     return jnp.where(tile == 0, 0, jnp.where(tile == TILES - 1, 2, 1))
 
 
-def fill_operands(place, pk_ref, seg, keys, queries):
-    fill_segments(pk_ref, seg)
+def key_marks(seg, tile):
+    number = lax.broadcasted_iota(jnp.int32, (TILE, 128), 1).astype(f32)
+    return jnp.where(seg[seg_kind(tile)] == number, 1.0, 0.0).astype(bf16)
+
+
+def query_marks(seg, tile):
     lane = lax.broadcasted_iota(jnp.int32, (TILE, 128), 1)
-    number = lane.astype(f32)
-
-    def key_tile(t):
-        keys[t, :, 0:128] = load_keys(pk_ref, t)
-        keys[t, :, 128:256] = jnp.where(seg[seg_kind(t)] == number, 1.0, 0.0).astype(bf16)
-
-    loop(TILES, key_tile)
+    other = jnp.logical_and(lane < 8, seg[seg_kind(tile)] != lane.astype(f32))
+    return jnp.where(other, NEG, 0.0).astype(bf16)
+
+
+def put_unpacked(packed, high, target):
     low = lax.broadcasted_iota(jnp.int32, (HT, 128), 1) < HD
-
-    def query_tile(j):
-        tile = place.own_tile(j)
-        for b in range(4):
-            packed = pk_ref[tile * 4 + b, T : T + HT].astype(f32)
-            queries[j, b * T : b * T + HT, 0:128] = jnp.where(low, packed, 0.0).astype(bf16)
-            queries[j, b * T + HT : b * T + T, 0:128] = jnp.where(low, pltpu.roll(packed, HD, 1), 0.0).astype(bf16)
-        other = jnp.logical_and(lane < 8, seg[seg_kind(tile)] != number)
-        queries[j, :, 128:256] = jnp.where(other, NEG, 0.0).astype(bf16)
-
-    loop(4, query_tile)
+    packed = packed.astype(f32)
+    turned = pltpu.roll(packed, HD, 1)
+    if high:
+        target[0:HT] = jnp.where(low, 0.0, turned).astype(bf16)
+        target[HT:T] = jnp.where(low, 0.0, packed).astype(bf16)
+    else:
+        target[0:HT] = jnp.where(low, packed, 0.0).astype(bf16)
+        target[HT:T] = jnp.where(low, turned, 0.0).astype(bf16)
 
 
 STEPS = 18
@@ -237,184 +236,6 @@
         jnp.where(lane < HD, both[b * T : b * T + HT], both[b * T + HT : b * T + T]).astype(bf16)
         for b in range(4)
     ]
-
-
-def forward_kernel(
-    x_ref, seg_ref, gain_ref, w_ref, pk_out, o_in, lse_ref, ot_ref,
-    w_scr, packets, pk, seg, keys, queries, vt, top, acc, even, odd, stage,
-    w_sem, a_send, a_recv, f_send, f_recv, k_sem, send, recv,
-):
-    place = Place()
-
-    def weight(g, part):
-        return pltpu.make_async_copy(
-            w_ref.at[:, pl.ds(part * D + g * 256, 256)], w_scr.at[g, part], w_sem.at[g, part]
-        )
-
-    for g in range(4):
-        for part in range(3):
-            weight(g, part).start()
-    barrier = pltpu.get_barrier_semaphore()
-    greet_all(place, barrier, place.block_device)
-    greet_all(place, barrier, place.head_device)
-    greet(barrier, place.partner)
-
-    x = x_ref[0].astype(f32)
-    a = (x * lax.rsqrt(jnp.mean(x * x, axis=-1, keepdims=True) + EPS) * gain_ref[...]).astype(bf16)
-    numbers = seg_ref[...].astype(f32)
-    row = lax.broadcasted_iota(jnp.int32, (16, 128), 0)
-    rest = jnp.concatenate([numbers[:, 128:T], jnp.zeros((1, 256 - T), f32)], axis=1)
-    seg_tile = jnp.where(row == 0, numbers[:, :128], jnp.where(row == 1, rest, 0.0)).astype(bf16)
-    pl.semaphore_wait(barrier, 33 - 2 * place.self_count)
-
-    def packet_hop(h):
-        return (
-            packets.at[h], pk.at[place.s], a_send.at[h], a_recv.at[place.slot], place.head_device(h),
-        )
-
-    for g in range(4):
-        for part in range(3):
-            weight(g, part).wait()
-        q = dot(a, w_scr[g, 0]) * (SCALE * LOG2E)
-        k = dot(a, w_scr[g, 1])
-        v = dot(a, w_scr[g, 2])
-        for m in range(2):
-            lanes = slice(128 * m, 128 * m + 128)
-            h = 4 * g + 2 * m
-            kv = swap_halves(k[:, lanes].astype(bf16), v[:, lanes].astype(bf16))
-            qq = q[:, lanes].astype(bf16)
-            qp = swap_halves(qq[:HT], qq[HT:])
-            for e in range(2):
-                packets[h + e, 0:T] = kv[e]
-                packets[h + e, T : T + HT] = qp[e]
-                packets[h + e, T + HT : PACK] = seg_tile
-                send_to(place, *packet_hop(h + e))
-
-    def forward(n):
-        i = place.own_block(n)
-        return remote(pk.at[i], pk.at[i], f_send.at[n], f_recv.at[n], place.partner)
-
-    def keep(n, core):
-        i = place.own_tile(lax.div(n, 4), core) * 4 + lax.rem(n, 4)
-        return pltpu.make_async_copy(pk.at[i], pk_out.at[i], k_sem.at[n])
-
-    def pass_on(n):
-        arrived(pk.at[place.own_block(n)], a_recv.at[n])
-        forward(n).start()
-        keep(n, place.core).start()
-
-    loop(16, pass_on)
-    one = jnp.where(lax.broadcasted_iota(jnp.int32, (16, TILE), 0) == 0, 1.0, 0.0).astype(bf16)
-
-    def kept_all(n):
-        keep(n, place.core).wait()
-        forward(n).wait_recv()
-        keep(n, 1 - place.core).start()
-
-    loop(16, kept_all)
-    fill_operands(place, pk, seg, keys, queries)
-
-    def prepare(t):
-        vt[t, 0:HD] = transposed(keys[t, :, 0:128])[HD:]
-        vt[t, HD : HD + 16] = one
-
-    loop(TILES, prepare)
-
-    def score(n, scores):
-        j, k_tile, _, _ = walk(place, jnp.minimum(n, STEPS - 1))
-        scores[...] = dot_nt(keys[k_tile], queries[j])
-
-    def out_hop(m):
-        return (
-            stage.at[m], o_in.at[place.head], send.at[m], recv.at[place.head], place.block_device(m),
-        )
-
-    def body(n, now, later):
-        j, k_tile, first, last = walk(place, n)
-
-        @pl.when(first)
-        def _():
-            score(n + 1, later)
-            scores = causal(now[...])
-            peak = jnp.max(scores, axis=0, keepdims=True)
-            top[...] = peak
-            acc[...] = dot(vt[k_tile], jnp.exp2(scores - peak).astype(bf16))
-
-        @pl.when(jnp.logical_not(first))
-        def _():
-            score(n + 1, later)
-            scores = now[...]
-            peak = jnp.maximum(top[...], jnp.max(scores, axis=0, keepdims=True))
-            fade = jnp.exp2(top[...] - peak)
-            top[...] = peak
-            acc[...] = acc[...] * fade + dot(vt[k_tile], jnp.exp2(scores - peak).astype(bf16))
-
-        @pl.when(last)
-        def _():
-            total = acc[HD : HD + 1]
-            out_t = acc[0:HD] / total
-            lse_ref[j] = top[...] + jnp.log2(total)
-            ot_ref[j] = out_t
-            packed = pack_transposed(out_t)
-            for b in range(4):
-                m = j * 4 + b
-                stage[m] = packed[b]
-                send_to(place, *out_hop(m))
-
-    score(0, even)
-
-    def pair(i):
-        body(2 * i, even, odd)
-        body(2 * i + 1, odd, even)
-
-    loop(STEPS // 2, pair)
-
-    def finish(n):
-        sent_to(place, *packet_hop(n))
-        forward(n).wait_send()
-        keep(n, 1 - place.core).wait()
-        sent_to(place, *out_hop(n))
-        arrived(o_in.at[n], recv.at[n])
-
-    loop(16, finish)
-
-
-def forward_call(frames, segment_ids, gain, w_qkv):
-    return pl.pallas_call(
-        forward_kernel,
-        name="attention",
-        out_shape=(
-            jax.ShapeDtypeStruct((BLOCKS, PACK, 128), bf16),
-            jax.ShapeDtypeStruct((16, HT, 128), bf16),
-            jax.ShapeDtypeStruct((4, 1, TILE), f32),
-            jax.ShapeDtypeStruct((4, HD, TILE), f32),
-        ),
-        in_specs=[VM, VM, VM, ANY],
-        out_specs=(ANY, ANY, VM, VM),
-        scratch_shapes=[
-            pltpu.VMEM((4, 3, D, 256), bf16),
-            pltpu.VMEM((16, PACK, 128), bf16),
-            pltpu.VMEM((BLOCKS, PACK, 128), bf16),
-            pltpu.VMEM((3, TILE, 128), f32),
-            pltpu.VMEM((TILES, TILE, 256), bf16),
-            pltpu.VMEM((4, TILE, 256), bf16),
-            pltpu.VMEM((TILES, HD + 16, TILE), bf16),
-            pltpu.VMEM((1, TILE), f32),
-            pltpu.VMEM((HD + 16, TILE), f32),
-            pltpu.VMEM((TILE, TILE), f32),
-            pltpu.VMEM((TILE, TILE), f32),
-            pltpu.VMEM((16, HT, 128), bf16),
-            pltpu.SemaphoreType.DMA((4, 3)),
-            pltpu.SemaphoreType.DMA((16,)),
-            pltpu.SemaphoreType.DMA((16,)),
-            pltpu.SemaphoreType.DMA((16,)),
-            pltpu.SemaphoreType.DMA((16,)),
-            pltpu.SemaphoreType.DMA((16,)),
-            pltpu.SemaphoreType.DMA((16,)),
-            pltpu.SemaphoreType.DMA((16,)),
-        ],
-        compiler_params=params(0),
-    )(frames, segment_ids, gain, w_qkv)
 
 
 FIRST = lambda c: ((c + 1) // 2) % 2
@@ -704,18 +525,21 @@
 HOOKS = (1, 7, 18, 19, 20, 22)
 
 
-def rest_kernel(
-    o_in, x_ref, dy_ref, gain1_ref, gain2_ref, lse_ref, w_out, w_up, w_down, w_qkv, pk_in, ot_in,
-    y_ref, dx_ref, qkv_out, gain_out, up_out, out_out, down_out,
-    o2, b2, dm2, yside, hside, da_side, gain2_grad, gs, land, outg, land2, tail, tail_land, da_in, stage1,
-    part, landed, dqkv_in, stage2, fin, side, down, a2, dhalf, gs3, land3, tail3, tail_land3, gain_value, gain_land,
+def block_kernel(
+    x_ref, seg_ref, dy_ref, gain1_ref, gain2_ref, w_qkv, w_out, w_up, w_down,
+    y_ref, dx_ref, qkv_out, gain_out, up_out, out_out, down_out, probs,
+    pk, o_in, ot, lse, peaks, o2, b2, dm2, yside, hside, das, da_side, gain2_grad,
+    gs, land, outg, land2, tail, tail_land, da_in, stage1,
+    part, landed, dqkv_in, stage2, fin, side, down, a2, d_side, land3, tail3, tail_land3, gain_value, gain_land,
     fin3, side3,
     w_sem, l_sem, p_send, p_recv, q_send, q_recv, h_send, h_recv, a_send, a_recv, b_send, b_recv,
     n_send, n_recv, t_send, t_recv, e_send, e_recv, g_send, g_recv, m_sem,
+    k_sem, x_send, x_recv, f_send, f_recv, c_send, c_recv, s_sem,
 ):
     place = Place()
     core = place.core
     net = Net(place)
+    turn = lax.rem(lax.div(place.s, 4), 4)
 
     def across(k, src, dst):
         return remote(src, dst, p_send.at[k], p_recv.at[k], place.partner)
@@ -741,7 +565,6 @@
     ]
     ends = [Exchange(net, 1 - g, tails[g], tail_land.at[g], e_send.at[g], e_recv.at[g]) for g in range(2)]
     mid = MidSums(place, fin, side, down, m_sem, up_out, out_out, down_out)
-    sums = [Part(net, gs3, land3, tail3, u, u, 1, u, (t_send, u), (t_recv, u)) for u in range(6)]
     ends3 = [
         Exchange(net, 1 - g, tail3.at[3 * g : 3 * g + 3], tail_land3.at[g], e_send.at[2 + g], e_recv.at[2 + g])
         for g in range(2)
@@ -753,13 +576,178 @@
     greet_all(place, barrier, place.head_device)
     net.greet(barrier)
     mid.greet(barrier)
+    a_hop = across(6, a2.at[0:T], a2.at[T : 2 * T])
+
+    def packet_hop(h):
+        return (stage2.at[h], pk.at[place.s], x_send.at[h], x_recv.at[place.slot], place.head_device(h))
+
+    def qkv(w_scr):
+        def weight(g, section):
+            at = pl.multiple_of(section * D + lax.rem(g + turn, 4) * 256, 256)
+            return pltpu.make_async_copy(w_qkv.at[:, pl.ds(at, 256)], w_scr.at[g, section], k_sem.at[g, section])
+
+        for g in range(4):
+            for section in range(3):
+                weight(g, section).start()
+        x = x_ref[0].astype(f32)
+        a = (x * lax.rsqrt(jnp.mean(x * x, axis=-1, keepdims=True) + EPS) * gain1_ref[...]).astype(bf16)
+        a2[0:T] = a
+        numbers = seg_ref[...].astype(f32)
+        row = lax.broadcasted_iota(jnp.int32, (16, 128), 0)
+        rest = jnp.concatenate([numbers[:, 128:T], jnp.zeros((1, 256 - T), f32)], axis=1)
+        seg_tile = jnp.where(row == 0, numbers[:, :128], jnp.where(row == 1, rest, 0.0)).astype(bf16)
+        pl.semaphore_wait(barrier, 2 * (16 - place.self_count) + Net.GREETINGS + mid.greetings())
+        for g in range(4):
+            for section in range(3):
+                weight(g, section).wait()
+            q = dot(a, w_scr[g, 0]) * (SCALE * LOG2E)
+            k = dot(a, w_scr[g, 1])
+            v = dot(a, w_scr[g, 2])
+            for m in range(2):
+                lanes = slice(128 * m, 128 * m + 128)
+                h = 4 * lax.rem(g + turn, 4) + 2 * m
+                kv = swap_halves(k[:, lanes].astype(bf16), v[:, lanes].astype(bf16))
+                qq = q[:, lanes].astype(bf16)
+                qp = swap_halves(qq[:HT], qq[HT:])
+                for e in range(2):
+                    stage2[h + e, 0:T] = kv[e]
+                    stage2[h + e, T : T + HT] = qp[e]
+                    stage2[h + e, T + HT : PACK] = seg_tile
+                    send_to(place, *packet_hop(h + e))
+        a_hop.start()
+
+    pl.run_scoped(qkv, pltpu.VMEM((4, 3, D, 256), bf16))
+
+    def out_hop(m):
+        return (stage1.at[m], o_in.at[place.head], c_send.at[m], c_recv.at[place.head], place.block_device(m))
+
+    def attention(seg, keys, queries, vt, top, acc, even, odd, even_p, odd_p):
+        one = jnp.where(lax.broadcasted_iota(jnp.int32, (16, TILE), 0) == 0, 1.0, 0.0).astype(bf16)
+
+        def forward(n):
+            i = place.own_block(n)
+            return remote(pk.at[i], pk.at[i], f_send.at[n], f_recv.at[n], place.partner)
+
+        def key_tile(t):
+            rows = load_keys(pk, t)
+            keys[t, :, 0:128] = rows
+            vt[t, 0:HD] = transposed(rows)[HD:]
+            vt[t, HD : HD + 16] = one
+
+        def own(j):
+            for b in range(4):
+                n = j * 4 + b
+                arrived(pk.at[place.own_block(n)], x_recv.at[n])
+                forward(n).start()
+            t = place.own_tile(j)
+            key_tile(t)
+            for b in range(4):
+                put_unpacked(pk[t * 4 + b, T : T + HT], False, queries.at[j, b * T : (b + 1) * T, 0:128])
+
+        loop(4, own)
+
+        def others(j):
+            for b in range(4):
+                forward(j * 4 + b).wait_recv()
+            key_tile(place.own_tile(j, 1 - core))
+
+        loop(4, others)
+        fill_segments(pk, seg)
+
+        def key_mark(t):
+            keys[t, :, 128:256] = key_marks(seg, t)
+
+        def query_mark(j):
+            queries[j, :, 128:256] = query_marks(seg, place.own_tile(j))
+
+        loop(TILES, key_mark)
+        loop(4, query_mark)
+
+        def score(n, scores):
+            j, k_tile, _, _ = walk(place, jnp.minimum(n, STEPS - 1))
+            scores[...] = dot_nt(keys[k_tile], queries[j])
+
+        def keep(j, k_tile, weights, which):
+            return pltpu.make_async_copy(weights, probs.at[j, k_tile], s_sem.at[which])
+
+        def body(n, now, later, weights, which):
+            j, k_tile, first, last = walk(place, n)
+
+            @pl.when(n >= 2)
+            def _():
+                keep(j, k_tile, weights, which).wait()
+
+            @pl.when(first)
+            def _():
+                score(n + 1, later)
+                scores = causal(now[...])
+                peak = jnp.max(scores, axis=0, keepdims=True)
+                top[...] = peak
+                value = jnp.exp2(scores - peak).astype(bf16)
+                weights[...] = value
+                acc[...] = dot(vt[k_tile], value)
+
+            @pl.when(jnp.logical_not(first))
+            def _():
+                score(n + 1, later)
+                scores = now[...]
+                peak = jnp.maximum(top[...], jnp.max(scores, axis=0, keepdims=True))
+                fade = jnp.exp2(top[...] - peak)
+                top[...] = peak
+                value = jnp.exp2(scores - peak).astype(bf16)
+                weights[...] = value
+                acc[...] = acc[...] * fade + dot(vt[k_tile], value)
+
+            keep(j, k_tile, weights, which).start()
+            peaks[j, k_tile] = top[...]
+
+            @pl.when(last)
+            def _():
+                total = acc[HD : HD + 1]
+                out_t = acc[0:HD] / total
+                lse[j] = top[...] + jnp.log2(total)
+                ot[j] = out_t
+                packed = pack_transposed(out_t)
+                for b in range(4):
+                    m = j * 4 + b
+                    stage1[m] = packed[b]
+                    send_to(place, *out_hop(m))
+
+        score(0, even)
+
+        def pair(i):
+            body(2 * i, even, odd, even_p, 0)
+            body(2 * i + 1, odd, even, odd_p, 1)
+
+        loop(STEPS // 2, pair)
+        keep(0, 0, even_p, 0).wait()
+        keep(0, 0, odd_p, 1).wait()
+
+        def finish(n):
+            sent_to(place, *packet_hop(n))
+            forward(n).wait_send()
+            sent_to(place, *out_hop(n))
+
+        loop(16, finish)
+
+    pl.run_scoped(
+        attention,
+        pltpu.VMEM((3, TILE, 128), f32),
+        pltpu.VMEM((TILES, TILE, 256), bf16),
+        pltpu.VMEM((4, TILE, 256), bf16),
+        pltpu.VMEM((TILES, HD + 16, TILE), bf16),
+        pltpu.VMEM((1, TILE), f32),
+        pltpu.VMEM((HD + 16, TILE), f32),
+        pltpu.VMEM((TILE, TILE), f32),
+        pltpu.VMEM((TILE, TILE), f32),
+        pltpu.VMEM((TILE, TILE), bf16),
+        pltpu.VMEM((TILE, TILE), bf16),
+    )
 
     def da_hop(h):
         return (
             stage1.at[h], da_in.at[place.slot], a_send.at[h], a_recv.at[place.slot], place.head_device(h),
         )
-
-    a_hop = across(6, a2.at[0:T], a2.at[T : 2 * T])
 
     def feed_forward(wo, wu, wd, b2t, gzt, x1s, ysum, hsum):
         def up_copy(j):
@@ -776,14 +764,15 @@
             up_copy(j).start()
             down_copy(j).start()
         dm2[0:T] = dy_ref[0]
+        dm_hop = across(0, dm2.at[0:T], dm2.at[T : 2 * T])
+        dm_hop.start()
         for m in range(8):
+            for h in (2 * m, 2 * m + 1):
+                arrived(o_in.at[h], c_recv.at[h])
             lo, hi = swap_halves(o_in[2 * m], o_in[2 * m + 1])
             o2[0:HT, 128 * m : 128 * m + 128] = lo
             o2[HT:T, 128 * m : 128 * m + 128] = hi
-        pl.semaphore_wait(barrier, 2 * (16 - place.self_count) + Net.GREETINGS + mid.greetings())
-        dm_hop = across(0, dm2.at[0:T], dm2.at[T : 2 * T])
         o_hop = across(1, o2.at[0:T], o2.at[T : 2 * T])
-        dm_hop.start()
         o_hop.start()
         out_copy.wait()
         x1 = x_ref[0].astype(f32) + dot(o2[0:T], wo[...])
@@ -792,9 +781,6 @@
         b2[0:T] = (x1 * scale1 * gain2_ref[...]).astype(bf16)
         b_hop = across(2, b2.at[0:T], b2.at[T : 2 * T])
         b_hop.start()
-        x = x_ref[0].astype(f32)
-        a2[0:T] = (x * lax.rsqrt(jnp.mean(x * x, axis=-1, keepdims=True) + EPS) * gain1_ref[...]).astype(bf16)
-        a_hop.start()
         dm_hop.wait_recv()
         b_hop.wait_recv()
         b2t[...] = transposed(b2[...])
@@ -852,17 +838,17 @@
         dx1 = dy_ref[0].astype(f32) + back
         hside[...] = dx1
         da = dx1.astype(bf16)
-        da_side[0, 0:T] = da[:, 0:512]
-        da_side[1, 0:T] = da[:, 512:1024]
-        side_hop = across(5, da_side.at[1 - core, 0:T], da_side.at[1 - core, T : 2 * T])
+        das[...] = da
+        side_hop = across(5, das.at[:, pl.ds(pl.multiple_of((1 - core) * 512, 512), 512)], da_side)
         side_hop.start()
         for g in range(4):
-            dattn = dot_nt(da, wo[256 * g : 256 * g + 256]).astype(bf16)
+            group = lax.rem(g + lax.rem(lax.div(place.s, 4), 4), 4)
+            dattn = dot_nt(da, wo[pl.ds(pl.multiple_of(group * 256, 256), 256)]).astype(bf16)
             for m in range(2):
                 tile = dattn[:, 128 * m : 128 * m + 128]
                 packed = swap_halves(tile[:HT], tile[HT:])
                 for e in range(2):
-                    h = 4 * g + 2 * m + e
+                    h = 4 * group + 2 * m + e
                     stage1[h] = packed[e]
                     send_to(place, *da_hop(h))
         down_units(1)
@@ -870,7 +856,9 @@
         y_ref[0] = (x1 + ysum[0:T] + yside[...]).astype(bf16)
         o_hop.wait_recv()
         side_hop.wait_recv()
-        out = dot(transposed(o2[...]), da_side[core]).astype(bf16)
+        o2t = transposed(o2[...])
+        mine = das[:, pl.ds(pl.multiple_of(core * 512, 512), 512)]
+        out = (dot(o2t[:, 0:T], mine) + dot(o2t[:, T:], da_side[...])).astype(bf16)
         for u in range(2):
             spread(outg, u, TURN[16 + u], out[:, u * 256 : u * 256 + 256])
             outs[u].start()
@@ -933,29 +921,19 @@
     def part_hop(j):
         return remote(part.at[j], landed.at[j], q_send.at[j], q_recv.at[j], place.partner)
 
-    def attention(pk, ot, seg, keys, queries, kt, gp, delta, dq, dkv):
-        pk_copy = pltpu.make_async_copy(pk_in, pk, l_sem.at[0])
-        ot_copy = pltpu.make_async_copy(ot_in, ot, l_sem.at[1])
-        pk_copy.start()
-        ot_copy.start()
-        pk_copy.wait()
-        fill_operands(place, pk, seg, keys, queries)
-        low = lax.broadcasted_iota(jnp.int32, (HT, 128), 1) < HD
-
+    def attention_back(queries, kt, gp, delta, dq, dkv, weights):
         def prepare(t):
-            kt[t] = transposed(keys[t, :, 0:128])[:HD]
+            kt[t] = transposed(load_keys(pk, t))[:HD]
             dkv[t] = jnp.zeros((TILE, 128), f32)
 
         loop(TILES, prepare)
-        ot_copy.wait()
 
         def prepare_query(j):
             for b in range(4):
                 m = j * 4 + b
+                put_unpacked(pk[place.own_block(m), T : T + HT], False, queries.at[j, b * T : (b + 1) * T])
                 arrived(da_in.at[m], a_recv.at[m])
-                packed = da_in[m].astype(f32)
-                gp[j, b * T : b * T + HT] = jnp.where(low, 0.0, pltpu.roll(packed, HD, 1)).astype(bf16)
-                gp[j, b * T + HT : b * T + T] = jnp.where(low, 0.0, packed).astype(bf16)
+                put_unpacked(da_in[m], True, gp.at[j, b * T : (b + 1) * T])
             delta[j] = jnp.sum(gp[j].astype(f32).T[HD:] * ot[j], axis=0, keepdims=True)
             dq[j] = jnp.zeros((HD, TILE), f32)
 
@@ -980,15 +958,16 @@
                 stage2[m, 0:T] = total[b * T : (b + 1) * T]
                 send_to(place, *key_hop(m))
 
-        def step(j, k_tile, diagonal):
-            rows = keys[k_tile]
-            scores = dot_nt(rows, queries[j])
-            if diagonal:
-                scores = causal(scores)
-            weights = jnp.exp2(scores - lse_ref[j])
-            slopes = (weights * (dot_nt(rows[:, 0:128], gp[j]) - delta[j])).astype(bf16)
-            weights = weights.astype(bf16)
-            dkv[k_tile] += dot(weights, gp[j]) + dot(slopes, queries[j, :, 0:128])
+        def fetch(j, k_tile, n):
+            which = lax.rem(n, 2)
+            return pltpu.make_async_copy(probs.at[j, k_tile], weights.at[which], s_sem.at[2 + which])
+
+        def step(j, k_tile, n):
+            rows = load_keys(pk, k_tile)
+            value = weights[lax.rem(n, 2)].astype(f32) * jnp.exp2(peaks[j, k_tile] - lse[j])
+            slopes = (value * (dot_nt(rows, gp[j]) - delta[j])).astype(bf16)
+            value = value.astype(bf16)
+            dkv[k_tile] += dot(value, gp[j]) + dot(slopes, queries[j])
             dq[j] += dot(kt[k_tile], slopes)
 
         def hooks(n):
@@ -999,29 +978,43 @@
                     def _(which=which):
                         hook(which)
 
-        turn = lax.div(place.head, 4)
-
         def owned(k_tile):
             return lax.rem(lax.div(k_tile + 1, 2), 2) == core
 
-        def key_tile(i, n):
-            k_tile = key_order(place, i)
+        def skipped(k_tile):
             skip = 0
             for j in range(4):
                 skip = skip + jnp.where(place.own_tile(j) < k_tile, 1, 0)
+            return skip
+
+        def query_of(at, k_tile):
+            return jnp.where(k_tile == 0, lax.rem(at + turn, 4), at)
+
+        def later(i):
+            k_tile = key_order(place, i)
+            return jnp.where(jnp.logical_and(core == 1, k_tile == 7), key_order(place, i + 1), k_tile)
+
+        first = later(0)
+        fetch(query_of(skipped(first), first), first, 0).start()
+
+        def key_tile(i, n):
+            k_tile = key_order(place, i)
+            following = later(jnp.minimum(i + 1, 7))
 
             def query_tile(at, n):
                 hooks(n)
-                j = jnp.where(k_tile == 0, lax.rem(at + turn, 4), at)
-                diagonal = place.own_tile(j) == k_tile
-
-                @pl.when(diagonal)
+                j = query_of(at, k_tile)
+                fetch(j, k_tile, n).wait()
+
+                @pl.when(at < 3)
                 def _():
-                    step(j, k_tile, True)
-
-                @pl.when(jnp.logical_not(diagonal))
+                    fetch(query_of(at + 1, k_tile), k_tile, n + 1).start()
+
+                @pl.when(jnp.logical_and(at == 3, i < 7))
                 def _():
-                    step(j, k_tile, False)
+                    fetch(query_of(skipped(following), following), following, n + 1).start()
+
+                step(j, k_tile, n)
 
                 @pl.when(k_tile == 0)
                 def _():
@@ -1033,7 +1026,7 @@
 
                 return n + 1
 
-            n = lax.fori_loop(skip, 4, query_tile, n)
+            n = lax.fori_loop(skipped(k_tile), 4, query_tile, n)
             mine = owned(k_tile)
             before = key_order(place, jnp.maximum(i - 1, 0))
 
@@ -1057,25 +1050,29 @@
             if HOOKS[which] == STEPS:
                 hook(which)
 
-    pl.run_scoped(
-        attention,
-        pltpu.VMEM((BLOCKS, PACK, 128), bf16),
-        pltpu.VMEM((4, HD, TILE), f32),
-        pltpu.VMEM((3, TILE, 128), f32),
-        pltpu.VMEM((TILES, TILE, 256), bf16),
-        pltpu.VMEM((4, TILE, 256), bf16),
-        pltpu.VMEM((TILES, HD, TILE), bf16),
-        pltpu.VMEM((4, TILE, 128), bf16),
-        pltpu.VMEM((4, 1, TILE), f32),
-        pltpu.VMEM((4, HD, TILE), f32),
-        pltpu.VMEM((TILES, TILE, 128), f32),
-    )
-
-    def last(w_scr, dn, a2t):
-        weight = pltpu.make_async_copy(w_qkv, w_scr, l_sem.at[2])
+    def back(w_scr, a2t):
+        weight = pltpu.make_async_copy(w_qkv, w_scr, l_sem.at[0])
         weight.start()
         a_hop.wait_recv()
         a2t[...] = transposed(a2[...])
+        pl.run_scoped(
+            attention_back,
+            pltpu.VMEM((4, TILE, 128), bf16),
+            pltpu.VMEM((TILES, HD, TILE), bf16),
+            pltpu.VMEM((4, TILE, 128), bf16),
+            pltpu.VMEM((4, 1, TILE), f32),
+            pltpu.VMEM((4, HD, TILE), f32),
+            pltpu.VMEM((TILES, TILE, 128), f32),
+            pltpu.VMEM((2, TILE, TILE), bf16),
+        )
+        pl.run_scoped(
+            functools.partial(last, weight, w_scr, a2t),
+            pltpu.VMEM((T, 3 * D), bf16),
+            pltpu.VMEM((6, 64, 16, 256), bf16),
+        )
+
+    def last(weight, w_scr, a2t, dn, gs3):
+        sums = [Part(net, gs3, land3, tail3, u, u, 1, u, (t_send, u), (t_recv, u)) for u in range(6)]
         for m in range(8):
             for h in (2 * m, 2 * m + 1):
                 arrived(dqkv_in.at[h, 0:T], b_recv.at[0, h])
@@ -1086,16 +1083,20 @@
             dn[HT:T, 128 * m : 128 * m + 128] = hi
             dn[:, D + 128 * m : D + 128 * m + 128] = dk
             dn[:, 2 * D + 128 * m : 2 * D + 128 * m + 128] = dv
-            at = 128 * (m % 4)
-            dhalf[m // 4, 0:HT, at : at + 128] = lo
-            dhalf[m // 4, HT:T, at : at + 128] = hi
-            dhalf[m // 4, 0:T, 512 + at : 512 + at + 128] = dk
-            dhalf[m // 4, 0:T, 1024 + at : 1024 + at + 128] = dv
-        d_hop = across(7, dhalf.at[1 - core, 0:T], dhalf.at[1 - core, T : 2 * T])
-        d_hop.start()
-        d_hop.wait_recv()
+        d_hops = []
+        for section in range(3):
+            at = pl.multiple_of(section * D + (1 - core) * 512, 512)
+            d_hops.append(
+                across(9 + section, dn.at[:, pl.ds(at, 512)], d_side.at[:, section * 512 : section * 512 + 512])
+            )
+            d_hops[section].start()
         for u in range(6):
-            spread(gs3, u, u, dot(a2t[...], dhalf[core, :, u * 256 : u * 256 + 256]).astype(bf16))
+            section, half = u // 2, u % 2
+            if half == 0:
+                d_hops[section].wait_recv()
+            at = pl.multiple_of(section * D + core * 512 + half * 256, 256)
+            grad = dot(a2t[:, 0:T], dn[:, pl.ds(at, 256)]) + dot(a2t[:, T:], d_side[:, u * 256 : u * 256 + 256])
+            spread(gs3, u, u, grad.astype(bf16))
             sums[u].start()
         weight.wait()
         x = x_ref[0].astype(f32)
@@ -1146,15 +1147,12 @@
             at = (u // 2) * D + (u % 2) * 256
             qkv_out[:, pl.ds(at + mine * 512, 256)] = fin3[u, mine]
             qkv_out[:, pl.ds(at + other * 512, 256)] = side3[u]
-        for hop in (a_hop, d_hop, aside):
+        for hop in [a_hop, aside] + d_hops:
             hop.wait_send()
-
-    pl.run_scoped(
-        last,
-        pltpu.VMEM((D, 3 * D), bf16),
-        pltpu.VMEM((T, 3 * D), bf16),
-        pltpu.VMEM((D, 2 * T), bf16),
-    )
+        for sums_of in sums:
+            sums_of.finish()
+
+    pl.run_scoped(back, pltpu.VMEM((D, 3 * D), bf16), pltpu.VMEM((D, 2 * T), bf16))
 
     def finish(n):
         sent_to(place, *da_hop(n))
@@ -1168,15 +1166,15 @@
         return carry
 
     lax.fori_loop(0, 4 - core, given, 0)
-    for sums_of in main + outs + sums + ends + ends3 + [gains]:
+    for sums_of in main + outs + ends + ends3 + [gains]:
         sums_of.finish()
 
 
-def rest_call(o_in, frames, out_grad, gain1, gain2, lse, w_out, w_up, w_down, w_qkv, pk, ot):
+def block_call(frames, segment_ids, out_grad, gain1, gain2, w_qkv, w_out, w_up, w_down):
     dma = pltpu.SemaphoreType.DMA
     return pl.pallas_call(
-        rest_kernel,
-        name="feed_forward_and_back",
+        block_kernel,
+        name="block",
         out_shape=(
             jax.ShapeDtypeStruct((1, T, D), bf16),
             jax.ShapeDtypeStruct((1, T, D), bf16),
@@ -1185,16 +1183,23 @@
             jax.ShapeDtypeStruct((8, FF), f32),
             jax.ShapeDtypeStruct((8, D), f32),
             jax.ShapeDtypeStruct((32, D), f32),
+            jax.ShapeDtypeStruct((4, TILES, TILE, TILE), bf16),
         ),
-        in_specs=[VM] * 6 + [ANY] * 6,
-        out_specs=(VM,) * 7,
+        in_specs=[VM] * 5 + [ANY] * 4,
+        out_specs=(VM,) * 7 + (ANY,),
         scratch_shapes=[
+            pltpu.VMEM((BLOCKS, PACK, 128), bf16),
+            pltpu.VMEM((16, HT, 128), bf16),
+            pltpu.VMEM((4, HD, TILE), f32),
+            pltpu.VMEM((4, 1, TILE), f32),
+            pltpu.VMEM((4, TILES, 1, TILE), f32),
             pltpu.VMEM((2 * T, D), bf16),
             pltpu.VMEM((2 * T, D), bf16),
             pltpu.VMEM((2 * T, D), bf16),
             pltpu.VMEM((T, D), f32),
             pltpu.VMEM((T, D), f32),
-            pltpu.VMEM((2, 2 * T, 512), bf16),
+            pltpu.VMEM((T, D), bf16),
+            pltpu.VMEM((T, 512), bf16),
             pltpu.VMEM((1, D), f32),
             pltpu.VMEM((16, 64, 16, 256), bf16),
             pltpu.VMEM((16, 56, 16, 256), bf16),
@@ -1207,13 +1212,12 @@
             pltpu.VMEM((4, TILE, 128), bf16),
             pltpu.VMEM((4, TILE, 128), bf16),
             pltpu.VMEM((16, GRAD, 128), bf16),
-            pltpu.VMEM((16, GRAD, 128), bf16),
+            pltpu.VMEM((16, PACK, 128), bf16),
             pltpu.VMEM((18, 2, 8, 256), f32),
             pltpu.VMEM((10, 8, 256), f32),
             pltpu.VMEM((2, 4, 2, 8, 256), f32),
             pltpu.VMEM((2 * T, D), bf16),
-            pltpu.VMEM((2, 2 * T, 1536), bf16),
-            pltpu.VMEM((6, 64, 16, 256), bf16),
+            pltpu.VMEM((T, 1536), bf16),
             pltpu.VMEM((6, 56, 16, 256), bf16),
             pltpu.VMEM((6, 8, 16, 256), bf16),
             pltpu.VMEM((2, 7, 3, 16, 256), bf16),
@@ -1221,12 +1225,13 @@
             pltpu.VMEM((3, 7, 16, 128), f32),
             pltpu.VMEM((6, 2, 8, 256), f32),
             pltpu.VMEM((6, 8, 256), f32),
-            dma((9,)), dma((3,)), dma((9,)), dma((9,)), dma((4,)), dma((4,)), dma((16,)), dma((16,)),
+            dma((9,)), dma((1,)), dma((12,)), dma((12,)), dma((4,)), dma((4,)), dma((16,)), dma((16,)),
             dma((16,)), dma((16,)), dma((2, 16)), dma((2, 16)), dma((8, 3)), dma((8, 3)), dma((6, 3)), dma((6, 3)),
             dma((4, 7)), dma((4, 7)), dma((3, 7)), dma((3, 7)), dma((6,)),
+            dma((4, 3)), dma((16,)), dma((16,)), dma((16,)), dma((16,)), dma((16,)), dma((16,)), dma((4,)),
         ],
-        compiler_params=params(1),
-    )(o_in, frames, out_grad, gain1, gain2, lse, w_out, w_up, w_down, w_qkv, pk, ot)
+        compiler_params=params(0),
+    )(frames, segment_ids, out_grad, gain1, gain2, w_qkv, w_out, w_up, w_down)
 
 
 def deliver_kernel(*refs):
@@ -1255,9 +1260,8 @@
 
 def shards(frames, segment_ids, norm1_gain, w_qkv, w_out, norm2_gain, w_up, w_down, out_grad):
     gain1, gain2 = norm1_gain[None], norm2_gain[None]
-    pk, o_in, lse, ot = forward_call(frames, segment_ids, gain1, w_qkv)
-    y, dx, qkv_sum, gain_sums, up_sum, out_sum, down_sum = rest_call(
-        o_in, frames, out_grad, gain1, gain2, lse, w_out, w_up, w_down, w_qkv, pk, ot
+    y, dx, qkv_sum, gain_sums, up_sum, out_sum, down_sum, _ = block_call(
+        frames, segment_ids, out_grad, gain1, gain2, w_qkv, w_out, w_up, w_down
     )
     y, dx, qkv_sum, out_sum, up_sum, down_sum, gain1_sum, gain2_sum = deliver(
         (y, dx, qkv_sum, out_sum, up_sum, down_sum), gain_sums

time: 186 us -> 177 us (0.952)
  Pallas kernels: 185 us -> 175 us
    pallas_call x2 -> x1, Pallas kernels: 182 us -> 173 us  [block_call(): pl.pallas_call(block_kernel, name='block', out_shape=(jax.ShapeDtypeStruc...]
where the time goes in v5:
time: 177 us; the launch traced here: 176 us
  Pallas kernels  175 us (99%)
    pallas_call x1, Pallas kernels, block_call(): pl.pallas_call(block_kernel, name='block', out_shape=(jax.ShapeDtypeStruc...  173 us

profile of v5, /device:TPU:1, one launch (start us, length us, event | category | flops | bytes accessed | tf_op | source)
XLA Modules:
  0.0 176.3 jit_solution(7519075493500377445)
XLA Ops:
  0.6 173.1 %block.1 = (bf16[1,192,1024]{2,1,0:T(8,128)(2,1)}, bf16[1,192,1024]{2,1,0:T(8,128)(2,1)}, f32[8,3072]{1,0:T(8,128)}, f32[8,128]{1,0:T(8,128)}, f32[8,4096]{1,0:T...) custom-call(bf16[1,192,1024]{2,1,0:T(8,128)(2,1)} %x_ref.1, s32[1,192]{1,0:T(1,128)} %seg_ref.1, ...), custom_call_target="tpu_custom_call" | custom-call | tf_op jit(solution)/shard_map/block/pallas_call | solution.py:1175
  173.8 2.3 %deliver.1 = (bf16[1,192,1024]{2,1,0:T(8,128)(2,1)}, bf16[1,192,1024]{2,1,0:T(8,128)(2,1)}, f32[8,3072]{1,0:T(8,128)}, f32[8,1024]{1,0:T(8,128)}, f32[8,4096]{1,...) custom-call(bf16[1,192,1024]{2,1,0:T(8,128)(2,1)} %get-tuple-element.23.refs_0_, ...), custom_call_target="tpu_custom_call" | custom-call | tf_op jit(solution)/shard_map/deliver/pallas_call | solution.py:1251

commit v6 on v5

--- a/solution.py
+++ b/solution.py
@@ -158,30 +158,17 @@
     )
 
 
-def fill_segments(pk_ref, seg):
-    first = seg_column(pk_ref, 0)
-    last = seg_column(pk_ref, BLOCKS - 1)
-    common = jnp.broadcast_to(first[T - 1 : T], (TILE, 128))
-    seg[0] = common
-    seg[1] = common
-    seg[2] = common
-    seg[0, 0:T] = first
-    seg[2, TILE - T : TILE] = last
-
-
-def seg_kind(tile):
-    return jnp.where(tile == 0, 0, jnp.where(tile == TILES - 1, 2, 1))
-
-
-def key_marks(seg, tile):
-    number = lax.broadcasted_iota(jnp.int32, (TILE, 128), 1).astype(f32)
-    return jnp.where(seg[seg_kind(tile)] == number, 1.0, 0.0).astype(bf16)
-
-
-def query_marks(seg, tile):
-    lane = lax.broadcasted_iota(jnp.int32, (TILE, 128), 1)
-    other = jnp.logical_and(lane < 8, seg[seg_kind(tile)] != lane.astype(f32))
-    return jnp.where(other, NEG, 0.0).astype(bf16)
+MIDDLE = 4
+
+
+def put_marks(pk_ref, tile, put):
+    lane = lax.broadcasted_iota(jnp.int32, (TILE, 128), 1).astype(f32)
+    put(slice(0, TILE), lane, jnp.full((TILE, 128), MIDDLE, f32))
+    for special, block, rows in ((0, 0, slice(0, T)), (TILES - 1, BLOCKS - 1, slice(TILE - T, TILE))):
+
+        @pl.when(tile == special)
+        def _(block=block, rows=rows):
+            put(rows, lane[:T], seg_column(pk_ref, block) + MIDDLE)
 
 
 def put_unpacked(packed, high, target):
@@ -199,24 +186,27 @@
 STEPS = 18
 
 
+OFF = STEPS - 4
+
+
 def walk(place, n):
     turn = lax.div(place.head, 4)
-    j, start, end = lax.rem(turn, 4), 0, 0
-    end = place.own_tile(j) + 1
+    j, start = turn, 0
+    end = place.own_tile(j)
     for k in range(1, 4):
         past = n >= end
         following = lax.rem(turn + k, 4)
         j = jnp.where(past, following, j)
         start = jnp.where(past, end, start)
-        end = jnp.where(past, end + place.own_tile(following) + 1, end)
-    at = n - start
-    k_tile = jnp.where(at == 0, place.own_tile(j), at - 1)
-    return j, k_tile, at == 0, n + 1 == end
+        end = jnp.where(past, end + place.own_tile(following), end)
+    return j, n - start, n + 1 == end
 
 
 def key_order(place, i):
     turn = lax.div(place.head, 4)
-    return jnp.where(i == 7, 0, 7 - lax.rem(i + 2 * turn, 7))
+    k_tile = 7 - lax.rem(i + 2 * turn, 7)
+    k_tile = jnp.where(jnp.logical_and(place.core == 1, k_tile == 1), 0, k_tile)
+    return jnp.where(i == 7, place.core, k_tile)
 
 
 def causal(scores):
@@ -246,14 +236,15 @@
     return [FIRST(x), FIRST(y), FIRST(z), SECOND(x), SECOND(y), SECOND(z)]
 
 
-ORDER = [[(p + k) % 3 + 3 * (p // 3) for k in range(3)] + [k + 3 * (1 - p // 3) for k in range(3)] for p in range(6)]
-
-
-def position(part, y_lo, x, z, y_hi):
+SHORT = [[(p + k) % 3 + 3 * (p // 3) for k in range(3)] + [k + 3 * (1 - p // 3) for k in range(3)] for p in range(6)]
+LONG = [[(p + k) % 3 + 3 * ((p // 3 + k // 3) % 2) for k in range(6)] for p in range(6)]
+
+
+def position(order, y_lo, x, z, y_hi):
     bits = chip_bits(x, y_hi * 2 + y_lo, z)
     at = 0
-    for k in range(6):
-        at = at * 2 + bits[ORDER[part][k]]
+    for dim in order:
+        at = at * 2 + bits[dim]
     return at
 
 
@@ -285,13 +276,13 @@
 
 
 class Part:
-    def __init__(self, net, acc, land, tail, at, tail_at, count, part, send, recv, pieces=()):
-        self.net, self.acc, self.land, self.tail, self.part, self.pieces = net, acc, land, tail, part, pieces
-        self.units, self.tail_units = pl.ds(at, count), pl.ds(tail_at, count)
-        self.count, self.send, self.recv = count, send, recv
+    def __init__(self, net, acc, land, at, count, order, send, recv, pieces=(), tail=None):
+        self.net, self.acc, self.land, self.order, self.pieces, self.tail = net, acc, land, order, pieces, tail
+        self.units = pl.ds(at, count)
+        self.send, self.recv = send, recv
 
     def bit(self, stage):
-        return self.net.bits[ORDER[self.part][stage]]
+        return self.net.bits[self.order[stage]]
 
     def base(self, stage):
         at = 0
@@ -310,7 +301,7 @@
             self.land.at[self.units, pl.ds(self.landing(stage), half)],
             self.send[0].at[self.send[1], stage],
             self.recv[0].at[self.recv[1], stage],
-            self.net.neighbour(ORDER[self.part][stage]),
+            self.net.neighbour(self.order[stage]),
         )
 
     def start(self):
@@ -345,10 +336,15 @@
     def settle(self):
         self.hop(2).wait_recv()
         for at in range(0, 8, 4):
-            self.tail[self.tail_units, at : at + 4] = self.total(self.base(2) + at, self.landing(2) + at, 4)
+            self.tail[self.units, at : at + 4] = self.total(self.base(2) + at, self.landing(2) + at, 4)
+
+    def last(self):
+        self.hop(5).wait_recv()
+        mine = self.acc[self.units, pl.ds(self.base(5), 1)].astype(f32)
+        return (mine + self.land[self.units, pl.ds(self.landing(5), 1)].astype(f32))[:, 0]
 
     def finish(self):
-        for stage in range(3):
+        for stage in range(6 if self.tail is None else 3):
             for hop in self.hops(stage):
                 hop.wait_send()
 
@@ -512,24 +508,24 @@
 ]
 
 
-def spread(target, unit_slot, turn, block):
+def spread(target, unit_slot, order, block):
     for chip in range(64):
         y_lo, x, z, y_hi = chip // 32, chip // 8 % 4, chip // 2 % 4, chip % 2
-        target[unit_slot, position(turn, y_lo, x, z, y_hi)] = block[chip * 16 : chip * 16 + 16]
+        target[unit_slot, position(order, y_lo, x, z, y_hi)] = block[chip * 16 : chip * 16 + 16]
 
 
 ROOT = math.sqrt(2.0 / math.pi)
 CUBE = 0.044715
 
 
-HOOKS = (1, 7, 18, 19, 20, 22)
+HOOKS = (1, 5, 11, 18, 19, 20, 21, 22)
 
 
 def block_kernel(
     x_ref, seg_ref, dy_ref, gain1_ref, gain2_ref, w_qkv, w_out, w_up, w_down,
     y_ref, dx_ref, qkv_out, gain_out, up_out, out_out, down_out, probs,
-    pk, o_in, ot, lse, peaks, o2, b2, dm2, yside, hside, das, da_side, gain2_grad,
-    gs, land, outg, land2, tail, tail_land, da_in, stage1,
+    pk, kt, o_in, ot, lse, peaks, o2, b2, dm2, yside, hside, das, da_side, gain2_grad,
+    gs, land, outg, land2, da_in, stage1,
     part, landed, dqkv_in, stage2, fin, side, down, a2, d_side, land3, tail3, tail_land3, gain_value, gain_land,
     fin3, side3,
     w_sem, l_sem, p_send, p_recv, q_send, q_recv, h_send, h_recv, a_send, a_recv, b_send, b_recv,
@@ -551,22 +547,19 @@
             h_send.at[unit], h_recv.at[unit], net.neighbour(TURN[unit]),
         )
 
-    tails = [tail.at[0:9], tail.at[9:18]]
     main = [
         Part(
-            net, gs, land, tail, STARTS[p], STARTS[p], COUNTS[p], p, (n_send, p), (n_recv, p),
+            net, gs, land, STARTS[p], COUNTS[p], LONG[p], (n_send, p), (n_recv, p),
             [first_hop(p + 6 * k) for k in range(COUNTS[p])],
         )
         for p in range(6)
     ]
     outs = [
-        Part(net, outg, land2, tail, u, 16 + u, 1, TURN[16 + u], (n_send, 6 + u), (n_recv, 6 + u))
-        for u in range(2)
+        Part(net, outg, land2, u, 1, LONG[TURN[16 + u]], (n_send, 6 + u), (n_recv, 6 + u)) for u in range(2)
     ]
-    ends = [Exchange(net, 1 - g, tails[g], tail_land.at[g], e_send.at[g], e_recv.at[g]) for g in range(2)]
     mid = MidSums(place, fin, side, down, m_sem, up_out, out_out, down_out)
     ends3 = [
-        Exchange(net, 1 - g, tail3.at[3 * g : 3 * g + 3], tail_land3.at[g], e_send.at[2 + g], e_recv.at[2 + g])
+        Exchange(net, 1 - g, tail3.at[3 * g : 3 * g + 3], tail_land3.at[g], e_send.at[g], e_recv.at[g])
         for g in range(2)
     ]
     gains = Shared(net, place, gain_value, gain_land, g_send, g_recv)
@@ -577,6 +570,7 @@
     net.greet(barrier)
     mid.greet(barrier)
     a_hop = across(6, a2.at[0:T], a2.at[T : 2 * T])
+    dm_hop = across(0, dm2.at[0:T], dm2.at[T : 2 * T])
 
     def packet_hop(h):
         return (stage2.at[h], pk.at[place.s], x_send.at[h], x_recv.at[place.slot], place.head_device(h))
@@ -592,7 +586,9 @@
         x = x_ref[0].astype(f32)
         a = (x * lax.rsqrt(jnp.mean(x * x, axis=-1, keepdims=True) + EPS) * gain1_ref[...]).astype(bf16)
         a2[0:T] = a
+        dm2[0:T] = dy_ref[0]
         numbers = seg_ref[...].astype(f32)
+        numbers = numbers - jnp.where(place.s == BLOCKS - 1, numbers[:, 0:1], numbers[:, T - 1 : T])
         row = lax.broadcasted_iota(jnp.int32, (16, 128), 0)
         rest = jnp.concatenate([numbers[:, 128:T], jnp.zeros((1, 256 - T), f32)], axis=1)
         seg_tile = jnp.where(row == 0, numbers[:, :128], jnp.where(row == 1, rest, 0.0)).astype(bf16)
@@ -615,13 +611,14 @@
                     stage2[h + e, T + HT : PACK] = seg_tile
                     send_to(place, *packet_hop(h + e))
         a_hop.start()
+        dm_hop.start()
 
     pl.run_scoped(qkv, pltpu.VMEM((4, 3, D, 256), bf16))
 
     def out_hop(m):
         return (stage1.at[m], o_in.at[place.head], c_send.at[m], c_recv.at[place.head], place.block_device(m))
 
-    def attention(seg, keys, queries, vt, top, acc, even, odd, even_p, odd_p):
+    def attention(keys, queries, vt, top, acc, even, odd, even_p, odd_p):
         one = jnp.where(lax.broadcasted_iota(jnp.int32, (16, TILE), 0) == 0, 1.0, 0.0).astype(bf16)
 
         def forward(n):
@@ -631,20 +628,76 @@
         def key_tile(t):
             rows = load_keys(pk, t)
             keys[t, :, 0:128] = rows
-            vt[t, 0:HD] = transposed(rows)[HD:]
+
+            def put(rows, lane, number):
+                keys[t, rows, 128:256] = jnp.where(lane == number, 1.0, 0.0).astype(bf16)
+
+            put_marks(pk, t, put)
+            turned = transposed(rows)
+            kt[t] = turned[:HD]
+            vt[t, 0:HD] = turned[HD:]
             vt[t, HD : HD + 16] = one
 
-        def own(j):
+        def query_tile(j):
+            t = place.own_tile(j)
+            for b in range(4):
+                put_unpacked(pk[t * 4 + b, T : T + HT], False, queries.at[j, b * T : (b + 1) * T, 0:128])
+
+            def put(rows, lane, number):
+                other = jnp.logical_and(lane < 2 * MIDDLE + 1, lane != number)
+                queries[j, rows, 128:256] = jnp.where(other, NEG, 0.0).astype(bf16)
+
+            put_marks(pk, t, put)
+
+        def keep(j, k_tile, weights, which):
+            for half in (slice(0, TILE // 2), slice(TILE // 2, TILE)):
+                pltpu.make_async_copy(weights.at[half], probs.at[j, k_tile, half], s_sem.at[which]).start()
+
+        def kept(weights, which):
+            pltpu.make_async_copy(weights, probs.at[0, 0], s_sem.at[which]).wait()
+
+        def finish_tile(j):
+            total = acc[j, HD : HD + 1]
+            out_t = acc[j, 0:HD] / total
+            lse[j] = top[j] + jnp.log2(total)
+            ot[j] = out_t
+            packed = pack_transposed(out_t)
+            for b in range(4):
+                m = j * 4 + b
+                stage1[m] = packed[b]
+                send_to(place, *out_hop(m))
+
+        def diagonal(j, weights, which, again):
             for b in range(4):
                 n = j * 4 + b
                 arrived(pk.at[place.own_block(n)], x_recv.at[n])
                 forward(n).start()
             t = place.own_tile(j)
             key_tile(t)
-            for b in range(4):
-                put_unpacked(pk[t * 4 + b, T : T + HT], False, queries.at[j, b * T : (b + 1) * T, 0:128])
-
-        loop(4, own)
+            query_tile(j)
+            scores = causal(dot_nt(keys[t], queries[j]))
+            peak = jnp.max(scores, axis=0, keepdims=True)
+            top[j] = peak
+            peaks[j, t] = peak
+            value = jnp.exp2(scores - peak).astype(bf16)
+
+            @pl.when(again)
+            def _():
+                kept(weights, which)
+
+            weights[...] = value
+            keep(j, t, weights, which)
+            acc[j] = dot(vt[t], value)
+
+        def diagonals(i):
+            diagonal(2 * i, even_p, 0, i > 0)
+            diagonal(2 * i + 1, odd_p, 1, i > 0)
+
+        loop(2, diagonals)
+
+        @pl.when(core == 0)
+        def _():
+            finish_tile(0)
 
         def others(j):
             for b in range(4):
@@ -652,66 +705,28 @@
             key_tile(place.own_tile(j, 1 - core))
 
         loop(4, others)
-        fill_segments(pk, seg)
-
-        def key_mark(t):
-            keys[t, :, 128:256] = key_marks(seg, t)
-
-        def query_mark(j):
-            queries[j, :, 128:256] = query_marks(seg, place.own_tile(j))
-
-        loop(TILES, key_mark)
-        loop(4, query_mark)
 
         def score(n, scores):
-            j, k_tile, _, _ = walk(place, jnp.minimum(n, STEPS - 1))
+            j, k_tile, _ = walk(place, jnp.minimum(n, OFF - 1))
             scores[...] = dot_nt(keys[k_tile], queries[j])
 
-        def keep(j, k_tile, weights, which):
-            return pltpu.make_async_copy(weights, probs.at[j, k_tile], s_sem.at[which])
-
         def body(n, now, later, weights, which):
-            j, k_tile, first, last = walk(place, n)
-
-            @pl.when(n >= 2)
-            def _():
-                keep(j, k_tile, weights, which).wait()
-
-            @pl.when(first)
-            def _():
-                score(n + 1, later)
-                scores = causal(now[...])
-                peak = jnp.max(scores, axis=0, keepdims=True)
-                top[...] = peak
-                value = jnp.exp2(scores - peak).astype(bf16)
-                weights[...] = value
-                acc[...] = dot(vt[k_tile], value)
-
-            @pl.when(jnp.logical_not(first))
-            def _():
-                score(n + 1, later)
-                scores = now[...]
-                peak = jnp.maximum(top[...], jnp.max(scores, axis=0, keepdims=True))
-                fade = jnp.exp2(top[...] - peak)
-                top[...] = peak
-                value = jnp.exp2(scores - peak).astype(bf16)
-                weights[...] = value
-                acc[...] = acc[...] * fade + dot(vt[k_tile], value)
-
-            keep(j, k_tile, weights, which).start()
-            peaks[j, k_tile] = top[...]
+            j, k_tile, last = walk(place, n)
+            kept(weights, which)
+            score(n + 1, later)
+            scores = now[...]
+            peak = jnp.maximum(top[j], jnp.max(scores, axis=0, keepdims=True))
+            fade = jnp.exp2(top[j] - peak)
+            top[j] = peak
+            peaks[j, k_tile] = peak
+            value = jnp.exp2(scores - peak).astype(bf16)
+            weights[...] = value
+            acc[j] = acc[j] * fade + dot(vt[k_tile], value)
+            keep(j, k_tile, weights, which)
 
             @pl.when(last)
             def _():
-                total = acc[HD : HD + 1]
-                out_t = acc[0:HD] / total
-                lse[j] = top[...] + jnp.log2(total)
-                ot[j] = out_t
-                packed = pack_transposed(out_t)
-                for b in range(4):
-                    m = j * 4 + b
-                    stage1[m] = packed[b]
-                    send_to(place, *out_hop(m))
+                finish_tile(j)
 
         score(0, even)
 
@@ -719,9 +734,9 @@
             body(2 * i, even, odd, even_p, 0)
             body(2 * i + 1, odd, even, odd_p, 1)
 
-        loop(STEPS // 2, pair)
-        keep(0, 0, even_p, 0).wait()
-        keep(0, 0, odd_p, 1).wait()
+        loop(OFF // 2, pair)
+        kept(even_p, 0)
+        kept(odd_p, 1)
 
         def finish(n):
             sent_to(place, *packet_hop(n))
@@ -732,12 +747,11 @@
 
     pl.run_scoped(
         attention,
-        pltpu.VMEM((3, TILE, 128), f32),
         pltpu.VMEM((TILES, TILE, 256), bf16),
         pltpu.VMEM((4, TILE, 256), bf16),
         pltpu.VMEM((TILES, HD + 16, TILE), bf16),
-        pltpu.VMEM((1, TILE), f32),
-        pltpu.VMEM((HD + 16, TILE), f32),
+        pltpu.VMEM((4, 1, TILE), f32),
+        pltpu.VMEM((4, HD + 16, TILE), f32),
         pltpu.VMEM((TILE, TILE), f32),
         pltpu.VMEM((TILE, TILE), f32),
         pltpu.VMEM((TILE, TILE), bf16),
@@ -749,7 +763,7 @@
             stage1.at[h], da_in.at[place.slot], a_send.at[h], a_recv.at[place.slot], place.head_device(h),
         )
 
-    def feed_forward(wo, wu, wd, b2t, gzt, x1s, ysum, hsum):
+    def feed_forward(wo, wu, wd, b2t, gzt, x1s, ysum, hsum, dgz):
         def up_copy(j):
             at = pl.multiple_of(core * 2048 + j * 512, 512)
             return pltpu.make_async_copy(w_up.at[:, pl.ds(at, 512)], wu.at[j], w_sem.at[1 + j])
@@ -759,13 +773,15 @@
             return pltpu.make_async_copy(w_down.at[pl.ds(at, 512)], wd.at[j], w_sem.at[5 + j])
 
         out_copy = pltpu.make_async_copy(w_out, wo, w_sem.at[0])
+        for j in range(4):
+            down_copy(j).start()
         out_copy.start()
         for j in range(4):
             up_copy(j).start()
-            down_copy(j).start()
-        dm2[0:T] = dy_ref[0]
-        dm_hop = across(0, dm2.at[0:T], dm2.at[T : 2 * T])
-        dm_hop.start()
+        dm_hop.wait_recv()
+        for j in range(4):
+            down_copy(j).wait()
+            dgz[j] = dot_nt(dm2[...], wd[j]).astype(bf16)
         for m in range(8):
             for h in (2 * m, 2 * m + 1):
                 arrived(o_in.at[h], c_recv.at[h])
@@ -781,20 +797,18 @@
         b2[0:T] = (x1 * scale1 * gain2_ref[...]).astype(bf16)
         b_hop = across(2, b2.at[0:T], b2.at[T : 2 * T])
         b_hop.start()
-        dm_hop.wait_recv()
         b_hop.wait_recv()
         b2t[...] = transposed(b2[...])
 
         for j in range(4):
             up_copy(j).wait()
-            down_copy(j).wait()
             z = dot(b2[...], wu[j])
             zz = z * z
             th = jnp.tanh(ROOT * z * (1.0 + CUBE * zz))
             half = 0.5 * (1.0 + th)
             gz = (z * half).astype(bf16)
             slope = half + 0.5 * z * (1.0 - th * th) * (ROOT * (1.0 + 3.0 * CUBE * zz))
-            dz = (dot_nt(dm2[...], wd[j]) * slope).astype(bf16)
+            dz = (dgz[j].astype(f32) * slope).astype(bf16)
             gzt[j * 512 : (j + 1) * 512] = transposed(gz)
             yj = dot(gz, wd[j])
             hj = dot_nt(dz, wu[j])
@@ -807,7 +821,7 @@
             up = dot(b2t[...], dz).astype(bf16)
             for u in range(2):
                 unit = 2 * j + u
-                spread(gs, SLOT[unit], TURN[unit], up[:, u * 256 : u * 256 + 256])
+                spread(gs, SLOT[unit], LONG[TURN[unit]], up[:, u * 256 : u * 256 + 256])
                 first_hop(unit).start()
 
         y_hop = across(3, ysum.at[T : 2 * T], yside)
@@ -822,7 +836,7 @@
                 for owner in range(32):
                     for group in range(4):
                         unit = 8 + u * 4 + group
-                        place_at = position(TURN[unit], y_lo, owner // 8, owner // 2 % 4, owner % 2)
+                        place_at = position(LONG[TURN[unit]], y_lo, owner // 8, owner // 2 % 4, owner % 2)
                         gs[SLOT[unit], place_at] = grad[owner * 64 + group * 16 : owner * 64 + group * 16 + 16]
             for group in range(4):
                 first_hop(8 + u * 4 + group).start()
@@ -860,7 +874,7 @@
         mine = das[:, pl.ds(pl.multiple_of(core * 512, 512), 512)]
         out = (dot(o2t[:, 0:T], mine) + dot(o2t[:, T:], da_side[...])).astype(bf16)
         for u in range(2):
-            spread(outg, u, TURN[16 + u], out[:, u * 256 : u * 256 + 256])
+            spread(outg, u, LONG[TURN[16 + u]], out[:, u * 256 : u * 256 + 256])
             outs[u].start()
         for hop in (dm_hop, o_hop, b_hop, y_hop, h_hop, side_hop):
             hop.wait_send()
@@ -875,36 +889,34 @@
         pltpu.VMEM((T, D), f32),
         pltpu.VMEM((2 * T, D), f32),
         pltpu.VMEM((2 * T, D), f32),
+        pltpu.VMEM((4, 2 * T, 512), bf16),
     )
 
     def hook(which):
-        if which < 2:
+        if which == 0:
             for sums_of in main:
-                sums_of.advance(which)
-            if which == 1:
-                for sums_of in outs:
-                    sums_of.advance(0)
-        elif which == 2:
-            for sums_of in main:
-                sums_of.settle()
-            ends[0].start()
+                sums_of.advance(0)
+        elif which == 1:
             for sums_of in outs:
-                sums_of.advance(1)
-        elif which == 3:
-            for sums_of in outs:
-                sums_of.settle()
-            ends[1].start()
-        elif which == 4:
-            for end in ends:
-                end.wait()
-            for unit in range(16):
-                group = SLOT[unit] // 9
-                mid.store(unit, ends[group].result(SLOT[unit] - 9 * group))
-            for u in range(2):
-                mid.store(16 + u, ends[1].result(7 + u))
+                sums_of.advance(0)
+        elif which < 6:
+            for sums_of in main + outs:
+                sums_of.advance(which - 1)
+        elif which == 6:
+            for p, sums_of in enumerate(main):
+                total = sums_of.last()
+                for k in range(COUNTS[p]):
+                    mid.store(p + 6 * k, total[k])
+            for u, sums_of in enumerate(outs):
+                mid.store(16 + u, sums_of.last()[0])
             mid.start()
         else:
             mid.finish()
+
+    def hooks_at(slot):
+        for which in range(8):
+            if HOOKS[which] == slot:
+                hook(which)
 
     def key_hop(m):
         return (
@@ -921,9 +933,10 @@
     def part_hop(j):
         return remote(part.at[j], landed.at[j], q_send.at[j], q_recv.at[j], place.partner)
 
-    def attention_back(queries, kt, gp, delta, dq, dkv, weights):
+    def attention_back(queries, gp, delta, dq, dkv, weights):
+        hooks_at(-1)
+
         def prepare(t):
-            kt[t] = transposed(load_keys(pk, t))[:HD]
             dkv[t] = jnp.zeros((TILE, 128), f32)
 
         loop(TILES, prepare)
@@ -960,19 +973,31 @@
 
         def fetch(j, k_tile, n):
             which = lax.rem(n, 2)
-            return pltpu.make_async_copy(probs.at[j, k_tile], weights.at[which], s_sem.at[2 + which])
-
-        def step(j, k_tile, n):
-            rows = load_keys(pk, k_tile)
-            value = weights[lax.rem(n, 2)].astype(f32) * jnp.exp2(peaks[j, k_tile] - lse[j])
-            slopes = (value * (dot_nt(rows, gp[j]) - delta[j])).astype(bf16)
-            value = value.astype(bf16)
-            dkv[k_tile] += dot(value, gp[j]) + dot(slopes, queries[j])
-            dq[j] += dot(kt[k_tile], slopes)
+            for half in (slice(0, TILE // 2), slice(TILE // 2, TILE)):
+                pltpu.make_async_copy(
+                    probs.at[j, k_tile, half], weights.at[which, half], s_sem.at[2 + which]
+                ).start()
+
+        def fetched(n):
+            which = lax.rem(n, 2)
+            pltpu.make_async_copy(probs.at[0, 0], weights.at[which], s_sem.at[2 + which]).wait()
+
+        def step(j, k_tile, n, pieces):
+            size = TILE // len(pieces)
+            which = lax.rem(n, 2)
+            shift = jnp.exp2(peaks[j, k_tile] - lse[j])
+            for at, begin in pieces:
+                ks, qs = slice(at, at + size), slice(begin, TILE)
+                value = weights[which, ks, qs].astype(f32) * shift[:, qs]
+                rows = load_keys(pk, k_tile)[ks]
+                slopes = (value * (dot_nt(rows, gp[j, qs]) - delta[j][:, qs])).astype(bf16)
+                value = value.astype(bf16)
+                dkv[k_tile, ks] += dot(value, gp[j, qs]) + dot(slopes, queries[j, qs])
+                dq[j, :, qs] += dot(kt[k_tile][:, ks], slopes)
 
         def hooks(n):
-            for which in range(6):
-                if HOOKS[which] < STEPS:
+            for which in range(8):
+                if 0 <= HOOKS[which] < STEPS:
 
                     @pl.when(n == HOOKS[which])
                     def _(which=which):
@@ -987,36 +1012,44 @@
                 skip = skip + jnp.where(place.own_tile(j) < k_tile, 1, 0)
             return skip
 
-        def query_of(at, k_tile):
-            return jnp.where(k_tile == 0, lax.rem(at + turn, 4), at)
+        def query_of(at, i):
+            return jnp.where(i == 7, lax.rem(at + turn, 4), at)
 
         def later(i):
+            empty = jnp.logical_and(core == 1, key_order(place, i) == 7)
+            i = jnp.where(empty, i + 1, i)
             k_tile = key_order(place, i)
-            return jnp.where(jnp.logical_and(core == 1, k_tile == 7), key_order(place, i + 1), k_tile)
-
-        first = later(0)
-        fetch(query_of(skipped(first), first), first, 0).start()
+            return query_of(skipped(k_tile), i), k_tile
+
+        fetch(*later(0), 0)
 
         def key_tile(i, n):
             k_tile = key_order(place, i)
-            following = later(jnp.minimum(i + 1, 7))
 
             def query_tile(at, n):
                 hooks(n)
-                j = query_of(at, k_tile)
-                fetch(j, k_tile, n).wait()
+                j = query_of(at, i)
+                fetched(n)
 
                 @pl.when(at < 3)
                 def _():
-                    fetch(query_of(at + 1, k_tile), k_tile, n + 1).start()
+                    fetch(query_of(at + 1, i), k_tile, n + 1)
 
                 @pl.when(jnp.logical_and(at == 3, i < 7))
                 def _():
-                    fetch(query_of(skipped(following), following), following, n + 1).start()
-
-                step(j, k_tile, n)
-
-                @pl.when(k_tile == 0)
+                    fetch(*later(jnp.minimum(i + 1, 7)), n + 1)
+
+                diagonal = place.own_tile(j) == k_tile
+
+                @pl.when(diagonal)
+                def _():
+                    step(j, k_tile, n, [(at, at) for at in range(0, TILE, 256)])
+
+                @pl.when(jnp.logical_not(diagonal))
+                def _():
+                    step(j, k_tile, n, [(0, 0)])
+
+                @pl.when(i == 7)
                 def _():
                     packed = pack_transposed(dq[j] * SCALE)
                     for b in range(4):
@@ -1041,14 +1074,9 @@
             return n
 
         lax.fori_loop(0, TILES, key_tile, 0)
-
-        @pl.when(core == 0)
-        def _():
-            take(0)
-
-        for which in range(6):
-            if HOOKS[which] == STEPS:
-                hook(which)
+        take(0)
+
+        hooks_at(STEPS)
 
     def back(w_scr, a2t):
         weight = pltpu.make_async_copy(w_qkv, w_scr, l_sem.at[0])
@@ -1058,7 +1086,6 @@
         pl.run_scoped(
             attention_back,
             pltpu.VMEM((4, TILE, 128), bf16),
-            pltpu.VMEM((TILES, HD, TILE), bf16),
             pltpu.VMEM((4, TILE, 128), bf16),
             pltpu.VMEM((4, 1, TILE), f32),
             pltpu.VMEM((4, HD, TILE), f32),
@@ -1072,7 +1099,7 @@
         )
 
     def last(weight, w_scr, a2t, dn, gs3):
-        sums = [Part(net, gs3, land3, tail3, u, u, 1, u, (t_send, u), (t_recv, u)) for u in range(6)]
+        sums = [Part(net, gs3, land3, u, 1, SHORT[u], (t_send, u), (t_recv, u), (), tail3) for u in range(6)]
         for m in range(8):
             for h in (2 * m, 2 * m + 1):
                 arrived(dqkv_in.at[h, 0:T], b_recv.at[0, h])
@@ -1096,7 +1123,7 @@
                 d_hops[section].wait_recv()
             at = pl.multiple_of(section * D + core * 512 + half * 256, 256)
             grad = dot(a2t[:, 0:T], dn[:, pl.ds(at, 256)]) + dot(a2t[:, T:], d_side[:, u * 256 : u * 256 + 256])
-            spread(gs3, u, u, grad.astype(bf16))
+            spread(gs3, u, SHORT[u], grad.astype(bf16))
             sums[u].start()
         weight.wait()
         x = x_ref[0].astype(f32)
@@ -1116,26 +1143,20 @@
                 sums_of.advance(stage)
             gains.take(stage)
             gains.start(stage + 1)
-            for which in range(6):
-                if HOOKS[which] == STEPS + 1 + stage:
-                    hook(which)
+            hooks_at(STEPS + 1 + stage)
         for g in range(2):
             for sums_of in sums[3 * g : 3 * g + 3]:
                 sums_of.settle()
             ends3[g].start()
         gains.take(2)
-        for which in range(6):
-            if HOOKS[which] == STEPS + 3:
-                hook(which)
+        hooks_at(STEPS + 3)
         for g in range(2):
             ends3[g].wait()
             for u in range(3):
                 fin3[3 * g + u] = ends3[g].result(u).reshape(2, 8, 256)
         aside = across(8, fin3.at[:, 1 - core], side3)
         aside.start()
-        for which in range(6):
-            if HOOKS[which] == STEPS + 4:
-                hook(which)
+        hooks_at(STEPS + 4)
         shard = place.s * 4 + place.r
         turn = lax.rem(128 - lax.rem(shard, 16) * 8, 128)
         for k in range(2):
@@ -1166,7 +1187,7 @@
         return carry
 
     lax.fori_loop(0, 4 - core, given, 0)
-    for sums_of in main + outs + ends + ends3 + [gains]:
+    for sums_of in main + outs + ends3 + [gains]:
         sums_of.finish()
 
 
@@ -1189,6 +1210,7 @@
         out_specs=(VM,) * 7 + (ANY,),
         scratch_shapes=[
             pltpu.VMEM((BLOCKS, PACK, 128), bf16),
+            pltpu.VMEM((TILES, HD, TILE), bf16),
             pltpu.VMEM((16, HT, 128), bf16),
             pltpu.VMEM((4, HD, TILE), f32),
             pltpu.VMEM((4, 1, TILE), f32),
@@ -1202,11 +1224,9 @@
             pltpu.VMEM((T, 512), bf16),
             pltpu.VMEM((1, D), f32),
             pltpu.VMEM((16, 64, 16, 256), bf16),
-            pltpu.VMEM((16, 56, 16, 256), bf16),
+            pltpu.VMEM((16, 63, 16, 256), bf16),
             pltpu.VMEM((2, 64, 16, 256), bf16),
-            pltpu.VMEM((2, 56, 16, 256), bf16),
-            pltpu.VMEM((18, 8, 16, 256), bf16),
-            pltpu.VMEM((2, 7, 9, 16, 256), bf16),
+            pltpu.VMEM((2, 63, 16, 256), bf16),
             pltpu.VMEM((16, HT, 128), bf16),
             pltpu.VMEM((16, HT, 128), bf16),
             pltpu.VMEM((4, TILE, 128), bf16),
@@ -1226,8 +1246,8 @@
             pltpu.VMEM((6, 2, 8, 256), f32),
             pltpu.VMEM((6, 8, 256), f32),
             dma((9,)), dma((1,)), dma((12,)), dma((12,)), dma((4,)), dma((4,)), dma((16,)), dma((16,)),
-            dma((16,)), dma((16,)), dma((2, 16)), dma((2, 16)), dma((8, 3)), dma((8, 3)), dma((6, 3)), dma((6, 3)),
-            dma((4, 7)), dma((4, 7)), dma((3, 7)), dma((3, 7)), dma((6,)),
+            dma((16,)), dma((16,)), dma((2, 16)), dma((2, 16)), dma((8, 6)), dma((8, 6)), dma((6, 3)), dma((6, 3)),
+            dma((2, 7)), dma((2, 7)), dma((3, 7)), dma((3, 7)), dma((6,)),
             dma((4, 3)), dma((16,)), dma((16,)), dma((16,)), dma((16,)), dma((16,)), dma((16,)), dma((4,)),
         ],
         compiler_params=params(0),

time: 177 us -> 173 us (0.977)
  Pallas kernels: 175 us -> 172 us
    pallas_call x1, Pallas kernels: 173 us -> 170 us  [block_call(): pl.pallas_call(block_kernel, name='block', out_shape=(jax.ShapeDtypeStruc...]
where the time goes in v6:
time: 173 us
  Pallas kernels  172 us (99%)
    pallas_call x1, Pallas kernels, block_call(): pl.pallas_call(block_kernel, name='block', out_shape=(jax.ShapeDtypeStruc...  170 us

profile of v6, /device:TPU:1, one launch (start us, length us, event | category | flops | bytes accessed | tf_op | source)
XLA Modules:
  0.0 172.7 jit_solution(8869574150948697845)
XLA Ops:
  0.6 169.5 %block.1 = (bf16[1,192,1024]{2,1,0:T(8,128)(2,1)}, bf16[1,192,1024]{2,1,0:T(8,128)(2,1)}, f32[8,3072]{1,0:T(8,128)}, f32[8,128]{1,0:T(8,128)}, f32[8,4096]{1,0:T...) custom-call(bf16[1,192,1024]{2,1,0:T(8,128)(2,1)} %x_ref.1, s32[1,192]{1,0:T(1,128)} %seg_ref.1, ...), custom_call_target="tpu_custom_call" | custom-call | tf_op jit(solution)/shard_map/block/pallas_call | solution.py:1196
  170.2 2.3 %deliver.1 = (bf16[1,192,1024]{2,1,0:T(8,128)(2,1)}, bf16[1,192,1024]{2,1,0:T(8,128)(2,1)}, f32[8,3072]{1,0:T(8,128)}, f32[8,1024]{1,0:T(8,128)}, f32[8,4096]{1,...) custom-call(bf16[1,192,1024]{2,1,0:T(8,128)(2,1)} %get-tuple-element.23.refs_0_, ...), custom_call_target="tpu_custom_call" | custom-call | tf_op jit(solution)/shard_map/deliver/pallas_call | solution.py:1271

commit v7 on v6

--- a/solution.py
+++ b/solution.py
@@ -21,8 +21,7 @@
 BLOCKS = 32
 TILE = 768
 TILES = 8
-PACK = 304
-GRAD = 288
+PACK = 288
 EPS = 1e-05
 NEG = -1e30
 LOG2E = math.log2(math.e)
@@ -147,8 +146,8 @@
     )
 
 
-def seg_column(pk_ref, block):
-    tile = pk_ref[block, T + HT : PACK].astype(f32)
+def seg_column(tile):
+    tile = tile.astype(f32)
     return jnp.concatenate(
         [
             jnp.broadcast_to(tile[0:1], (128, 128)).T,
@@ -161,14 +160,14 @@
 MIDDLE = 4
 
 
-def put_marks(pk_ref, tile, put):
+def put_marks(segs, tile, put):
     lane = lax.broadcasted_iota(jnp.int32, (TILE, 128), 1).astype(f32)
     put(slice(0, TILE), lane, jnp.full((TILE, 128), MIDDLE, f32))
-    for special, block, rows in ((0, 0, slice(0, T)), (TILES - 1, BLOCKS - 1, slice(TILE - T, TILE))):
+    for which, special, rows in ((0, 0, slice(0, T)), (1, TILES - 1, slice(TILE - T, TILE))):
 
         @pl.when(tile == special)
-        def _(block=block, rows=rows):
-            put(rows, lane[:T], seg_column(pk_ref, block) + MIDDLE)
+        def _(which=which, rows=rows):
+            put(rows, lane[:T], seg_column(segs[which]) + MIDDLE)
 
 
 def put_unpacked(packed, high, target):
@@ -184,6 +183,7 @@
 
 
 STEPS = 18
+AHEAD = 4
 
 
 OFF = STEPS - 4
@@ -524,13 +524,13 @@
 def block_kernel(
     x_ref, seg_ref, dy_ref, gain1_ref, gain2_ref, w_qkv, w_out, w_up, w_down,
     y_ref, dx_ref, qkv_out, gain_out, up_out, out_out, down_out, probs,
-    pk, kt, o_in, ot, lse, peaks, o2, b2, dm2, yside, hside, das, da_side, gain2_grad,
+    pk, segs, seg_tile, kt, o_in, ot, lse, peaks, o2, b2, dm2, yside, hside, das, da_side, gain2_grad,
     gs, land, outg, land2, da_in, stage1,
     part, landed, dqkv_in, stage2, fin, side, down, a2, d_side, land3, tail3, tail_land3, gain_value, gain_land,
     fin3, side3,
     w_sem, l_sem, p_send, p_recv, q_send, q_recv, h_send, h_recv, a_send, a_recv, b_send, b_recv,
     n_send, n_recv, t_send, t_recv, e_send, e_recv, g_send, g_recv, m_sem,
-    k_sem, x_send, x_recv, f_send, f_recv, c_send, c_recv, s_sem,
+    k_sem, x_send, x_recv, f_send, f_recv, c_send, c_recv, s_sem, y_send, y_recv,
 ):
     place = Place()
     core = place.core
@@ -572,6 +572,12 @@
     a_hop = across(6, a2.at[0:T], a2.at[T : 2 * T])
     dm_hop = across(0, dm2.at[0:T], dm2.at[T : 2 * T])
 
+    edge = jnp.logical_or(place.s == 0, place.s == BLOCKS - 1)
+    which_edge = lax.div(place.s, BLOCKS - 1)
+
+    def seg_hop(h):
+        return (seg_tile, segs.at[which_edge], y_send.at[h], y_recv.at[which_edge], place.head_device(h))
+
     def packet_hop(h):
         return (stage2.at[h], pk.at[place.s], x_send.at[h], x_recv.at[place.slot], place.head_device(h))
 
@@ -591,14 +597,20 @@
         numbers = numbers - jnp.where(place.s == BLOCKS - 1, numbers[:, 0:1], numbers[:, T - 1 : T])
         row = lax.broadcasted_iota(jnp.int32, (16, 128), 0)
         rest = jnp.concatenate([numbers[:, 128:T], jnp.zeros((1, 256 - T), f32)], axis=1)
-        seg_tile = jnp.where(row == 0, numbers[:, :128], jnp.where(row == 1, rest, 0.0)).astype(bf16)
-        pl.semaphore_wait(barrier, 2 * (16 - place.self_count) + Net.GREETINGS + mid.greetings())
+        seg_tile[...] = jnp.where(row == 0, numbers[:, :128], jnp.where(row == 1, rest, 0.0)).astype(bf16)
         for g in range(4):
             for section in range(3):
                 weight(g, section).wait()
             q = dot(a, w_scr[g, 0]) * (SCALE * LOG2E)
             k = dot(a, w_scr[g, 1])
             v = dot(a, w_scr[g, 2])
+            if g == 0:
+                pl.semaphore_wait(barrier, 2 * (16 - place.self_count) + Net.GREETINGS + mid.greetings())
+
+                @pl.when(edge)
+                def _():
+                    loop(16, lambda h: send_to(place, *seg_hop(h)))
+
             for m in range(2):
                 lanes = slice(128 * m, 128 * m + 128)
                 h = 4 * lax.rem(g + turn, 4) + 2 * m
@@ -607,8 +619,7 @@
                 qp = swap_halves(qq[:HT], qq[HT:])
                 for e in range(2):
                     stage2[h + e, 0:T] = kv[e]
-                    stage2[h + e, T : T + HT] = qp[e]
-                    stage2[h + e, T + HT : PACK] = seg_tile
+                    stage2[h + e, T:PACK] = qp[e]
                     send_to(place, *packet_hop(h + e))
         a_hop.start()
         dm_hop.start()
@@ -623,7 +634,10 @@
 
         def forward(n):
             i = place.own_block(n)
-            return remote(pk.at[i], pk.at[i], f_send.at[n], f_recv.at[n], place.partner)
+            return remote(pk.at[i, 0:T], pk.at[i, 0:T], f_send.at[n], f_recv.at[n], place.partner)
+
+        def seg_forward(k):
+            return remote(segs.at[k], segs.at[k], f_send.at[16 + k], f_recv.at[16 + k], place.partner)
 
         def key_tile(t):
             rows = load_keys(pk, t)
@@ -632,7 +646,7 @@
             def put(rows, lane, number):
                 keys[t, rows, 128:256] = jnp.where(lane == number, 1.0, 0.0).astype(bf16)
 
-            put_marks(pk, t, put)
+            put_marks(segs, t, put)
             turned = transposed(rows)
             kt[t] = turned[:HD]
             vt[t, 0:HD] = turned[HD:]
@@ -647,7 +661,7 @@
                 other = jnp.logical_and(lane < 2 * MIDDLE + 1, lane != number)
                 queries[j, rows, 128:256] = jnp.where(other, NEG, 0.0).astype(bf16)
 
-            put_marks(pk, t, put)
+            put_marks(segs, t, put)
 
         def keep(j, k_tile, weights, which):
             for half in (slice(0, TILE // 2), slice(TILE // 2, TILE)):
@@ -673,6 +687,13 @@
                 arrived(pk.at[place.own_block(n)], x_recv.at[n])
                 forward(n).start()
             t = place.own_tile(j)
+            for k, special in ((0, 0), (1, TILES - 1)):
+
+                @pl.when(t == special)
+                def _(k=k):
+                    arrived(segs.at[k], y_recv.at[k])
+                    seg_forward(k).start()
+
             key_tile(t)
             query_tile(j)
             scores = causal(dot_nt(keys[t], queries[j]))
@@ -702,6 +723,13 @@
         def others(j):
             for b in range(4):
                 forward(j * 4 + b).wait_recv()
+            other = place.own_tile(j, 1 - core)
+            for k, special in ((0, 0), (1, TILES - 1)):
+
+                @pl.when(other == special)
+                def _(k=k):
+                    seg_forward(k).wait_recv()
+
             key_tile(place.own_tile(j, 1 - core))
 
         loop(4, others)
@@ -738,10 +766,20 @@
         kept(even_p, 0)
         kept(odd_p, 1)
 
+        @pl.when(core == 0)
+        def _():
+            for k in range(2):
+                seg_forward(k).wait_send()
+
+
         def finish(n):
             sent_to(place, *packet_hop(n))
+
+            @pl.when(edge)
+            def _():
+                sent_to(place, *seg_hop(n))
+
             forward(n).wait_send()
-            sent_to(place, *out_hop(n))
 
         loop(16, finish)
 
@@ -855,6 +893,7 @@
         das[...] = da
         side_hop = across(5, das.at[:, pl.ds(pl.multiple_of((1 - core) * 512, 512), 512)], da_side)
         side_hop.start()
+        loop(16, lambda n: sent_to(place, *out_hop(n)))
         for g in range(4):
             group = lax.rem(g + lax.rem(lax.div(place.s, 4), 4), 4)
             dattn = dot_nt(da, wo[pl.ds(pl.multiple_of(group * 256, 256), 256)]).astype(bf16)
@@ -926,7 +965,7 @@
 
     def query_hop(m):
         return (
-            stage2.at[m, T:GRAD], dqkv_in.at[place.head, T:GRAD], b_send.at[1, m], b_recv.at[1, place.head],
+            stage2.at[m, T:PACK], dqkv_in.at[place.head, T:PACK], b_send.at[1, m], b_recv.at[1, place.head],
             place.block_device(m),
         )
 
@@ -971,20 +1010,21 @@
                 stage2[m, 0:T] = total[b * T : (b + 1) * T]
                 send_to(place, *key_hop(m))
 
-        def fetch(j, k_tile, n):
-            which = lax.rem(n, 2)
+        def fetch(i, at, n):
+            which = lax.rem(n, AHEAD)
+            j, k_tile = query_of(at, i), key_order(place, i)
             for half in (slice(0, TILE // 2), slice(TILE // 2, TILE)):
                 pltpu.make_async_copy(
                     probs.at[j, k_tile, half], weights.at[which, half], s_sem.at[2 + which]
                 ).start()
 
         def fetched(n):
-            which = lax.rem(n, 2)
+            which = lax.rem(n, AHEAD)
             pltpu.make_async_copy(probs.at[0, 0], weights.at[which], s_sem.at[2 + which]).wait()
 
         def step(j, k_tile, n, pieces):
             size = TILE // len(pieces)
-            which = lax.rem(n, 2)
+            which = lax.rem(n, AHEAD)
             shift = jnp.exp2(peaks[j, k_tile] - lse[j])
             for at, begin in pieces:
                 ks, qs = slice(at, at + size), slice(begin, TILE)
@@ -1015,29 +1055,31 @@
         def query_of(at, i):
             return jnp.where(i == 7, lax.rem(at + turn, 4), at)
 
-        def later(i):
-            empty = jnp.logical_and(core == 1, key_order(place, i) == 7)
-            i = jnp.where(empty, i + 1, i)
+        def first_of(i):
+            i = jnp.where(jnp.logical_and(core == 1, key_order(place, i) == 7), i + 1, i)
+            return i, skipped(key_order(place, i))
+
+        def following(i, at):
+            next_i, next_at = first_of(jnp.minimum(i + 1, 7))
+            return jnp.where(at < 3, i, next_i), jnp.where(at < 3, at + 1, next_at)
+
+        ahead = first_of(0)
+        for n in range(AHEAD - 1):
+            fetch(*ahead, n)
+            ahead = following(*ahead)
+
+        def key_tile(i, carry):
             k_tile = key_order(place, i)
-            return query_of(skipped(k_tile), i), k_tile
-
-        fetch(*later(0), 0)
-
-        def key_tile(i, n):
-            k_tile = key_order(place, i)
-
-            def query_tile(at, n):
+
+            def query_tile(at, carry):
+                n, ahead = carry[0], carry[1:]
                 hooks(n)
                 j = query_of(at, i)
                 fetched(n)
 
-                @pl.when(at < 3)
+                @pl.when(n + AHEAD - 1 < STEPS)
                 def _():
-                    fetch(query_of(at + 1, i), k_tile, n + 1)
-
-                @pl.when(jnp.logical_and(at == 3, i < 7))
-                def _():
-                    fetch(*later(jnp.minimum(i + 1, 7)), n + 1)
+                    fetch(*ahead, n + AHEAD - 1)
 
                 diagonal = place.own_tile(j) == k_tile
 
@@ -1054,12 +1096,12 @@
                     packed = pack_transposed(dq[j] * SCALE)
                     for b in range(4):
                         m = j * 4 + b
-                        stage2[m, T:GRAD] = packed[b]
+                        stage2[m, T:PACK] = packed[b]
                         send_to(place, *query_hop(m))
 
-                return n + 1
-
-            n = lax.fori_loop(skipped(k_tile), 4, query_tile, n)
+                return (n + 1,) + following(*ahead)
+
+            carry = lax.fori_loop(skipped(k_tile), 4, query_tile, carry)
             mine = owned(k_tile)
             before = key_order(place, jnp.maximum(i - 1, 0))
 
@@ -1071,9 +1113,9 @@
             def _():
                 take(lax.div(before, 2))
 
-            return n
-
-        lax.fori_loop(0, TILES, key_tile, 0)
+            return carry
+
+        lax.fori_loop(0, TILES, key_tile, (0,) + ahead)
         take(0)
 
         hooks_at(STEPS)
@@ -1090,7 +1132,7 @@
             pltpu.VMEM((4, 1, TILE), f32),
             pltpu.VMEM((4, HD, TILE), f32),
             pltpu.VMEM((TILES, TILE, 128), f32),
-            pltpu.VMEM((2, TILE, TILE), bf16),
+            pltpu.VMEM((AHEAD, TILE, TILE), bf16),
         )
         pl.run_scoped(
             functools.partial(last, weight, w_scr, a2t),
@@ -1103,8 +1145,8 @@
         for m in range(8):
             for h in (2 * m, 2 * m + 1):
                 arrived(dqkv_in.at[h, 0:T], b_recv.at[0, h])
-                arrived(dqkv_in.at[h, T:GRAD], b_recv.at[1, h])
-            lo, hi = swap_halves(dqkv_in[2 * m, T:GRAD], dqkv_in[2 * m + 1, T:GRAD])
+                arrived(dqkv_in.at[h, T:PACK], b_recv.at[1, h])
+            lo, hi = swap_halves(dqkv_in[2 * m, T:PACK], dqkv_in[2 * m + 1, T:PACK])
             dk, dv = swap_halves(dqkv_in[2 * m, 0:T], dqkv_in[2 * m + 1, 0:T])
             dn[0:HT, 128 * m : 128 * m + 128] = lo
             dn[HT:T, 128 * m : 128 * m + 128] = hi
@@ -1210,6 +1252,8 @@
         out_specs=(VM,) * 7 + (ANY,),
         scratch_shapes=[
             pltpu.VMEM((BLOCKS, PACK, 128), bf16),
+            pltpu.VMEM((2, 16, 128), bf16),
+            pltpu.VMEM((16, 128), bf16),
             pltpu.VMEM((TILES, HD, TILE), bf16),
             pltpu.VMEM((16, HT, 128), bf16),
             pltpu.VMEM((4, HD, TILE), f32),
@@ -1231,7 +1275,7 @@
             pltpu.VMEM((16, HT, 128), bf16),
             pltpu.VMEM((4, TILE, 128), bf16),
             pltpu.VMEM((4, TILE, 128), bf16),
-            pltpu.VMEM((16, GRAD, 128), bf16),
+            pltpu.VMEM((16, PACK, 128), bf16),
             pltpu.VMEM((16, PACK, 128), bf16),
             pltpu.VMEM((18, 2, 8, 256), f32),
             pltpu.VMEM((10, 8, 256), f32),
@@ -1248,7 +1292,8 @@
             dma((9,)), dma((1,)), dma((12,)), dma((12,)), dma((4,)), dma((4,)), dma((16,)), dma((16,)),
             dma((16,)), dma((16,)), dma((2, 16)), dma((2, 16)), dma((8, 6)), dma((8, 6)), dma((6, 3)), dma((6, 3)),
             dma((2, 7)), dma((2, 7)), dma((3, 7)), dma((3, 7)), dma((6,)),
-            dma((4, 3)), dma((16,)), dma((16,)), dma((16,)), dma((16,)), dma((16,)), dma((16,)), dma((4,)),
+            dma((4, 3)), dma((16,)), dma((16,)), dma((18,)), dma((18,)), dma((16,)), dma((16,)), dma((2 + AHEAD,)),
+            dma((16,)), dma((2,)),
         ],
         compiler_params=params(0),
     )(frames, segment_ids, out_grad, gain1, gain2, w_qkv, w_out, w_up, w_down)

time: 173 us -> 169 us (0.977)
  Pallas kernels: 172 us -> 167 us
    pallas_call x1, Pallas kernels: 170 us -> 165 us  [block_call(): pl.pallas_call(block_kernel, name='block', out_shape=(jax.ShapeDtypeStruc...]
where the time goes in v7:
time: 169 us; the launch traced here: 168 us
  Pallas kernels  167 us (99%)
    pallas_call x1, Pallas kernels, block_call(): pl.pallas_call(block_kernel, name='block', out_shape=(jax.ShapeDtypeStruc...  165 us

profile of v7, /device:TPU:1, one launch (start us, length us, event | category | flops | bytes accessed | tf_op | source)
XLA Modules:
  0.0 168.3 jit_solution(7463004573170421841)
XLA Ops:
  0.6 165.1 %block.1 = (bf16[1,192,1024]{2,1,0:T(8,128)(2,1)}, bf16[1,192,1024]{2,1,0:T(8,128)(2,1)}, f32[8,3072]{1,0:T(8,128)}, f32[8,128]{1,0:T(8,128)}, f32[8,4096]{1,0:T...) custom-call(bf16[1,192,1024]{2,1,0:T(8,128)(2,1)} %x_ref.1, s32[1,192]{1,0:T(1,128)} %seg_ref.1, ...), custom_call_target="tpu_custom_call" | custom-call | tf_op jit(solution)/shard_map/block/pallas_call | solution.py:1238
  165.7 2.3 %deliver.1 = (bf16[1,192,1024]{2,1,0:T(8,128)(2,1)}, bf16[1,192,1024]{2,1,0:T(8,128)(2,1)}, f32[8,3072]{1,0:T(8,128)}, f32[8,1024]{1,0:T(8,128)}, f32[8,4096]{1,...) custom-call(bf16[1,192,1024]{2,1,0:T(8,128)(2,1)} %get-tuple-element.23.refs_0_, ...), custom_call_target="tpu_custom_call" | custom-call | tf_op jit(solution)/shard_map/deliver/pallas_call | solution.py:1316

commit v8 on v7

--- a/solution.py
+++ b/solution.py
@@ -1142,23 +1142,25 @@
 
     def last(weight, w_scr, a2t, dn, gs3):
         sums = [Part(net, gs3, land3, u, 1, SHORT[u], (t_send, u), (t_recv, u), (), tail3) for u in range(6)]
-        for m in range(8):
+        d_hops = []
+        for k in range(8):
+            m = k % 4 + 4 * (1 - core if k < 4 else core)
             for h in (2 * m, 2 * m + 1):
                 arrived(dqkv_in.at[h, 0:T], b_recv.at[0, h])
                 arrived(dqkv_in.at[h, T:PACK], b_recv.at[1, h])
             lo, hi = swap_halves(dqkv_in[2 * m, T:PACK], dqkv_in[2 * m + 1, T:PACK])
             dk, dv = swap_halves(dqkv_in[2 * m, 0:T], dqkv_in[2 * m + 1, 0:T])
-            dn[0:HT, 128 * m : 128 * m + 128] = lo
-            dn[HT:T, 128 * m : 128 * m + 128] = hi
-            dn[:, D + 128 * m : D + 128 * m + 128] = dk
-            dn[:, 2 * D + 128 * m : 2 * D + 128 * m + 128] = dv
-        d_hops = []
-        for section in range(3):
-            at = pl.multiple_of(section * D + (1 - core) * 512, 512)
-            d_hops.append(
-                across(9 + section, dn.at[:, pl.ds(at, 512)], d_side.at[:, section * 512 : section * 512 + 512])
-            )
-            d_hops[section].start()
+            dn[0:HT, pl.ds(pl.multiple_of(128 * m, 128), 128)] = lo
+            dn[HT:T, pl.ds(pl.multiple_of(128 * m, 128), 128)] = hi
+            dn[:, pl.ds(pl.multiple_of(D + 128 * m, 128), 128)] = dk
+            dn[:, pl.ds(pl.multiple_of(2 * D + 128 * m, 128), 128)] = dv
+            if k == 3:
+                for section in range(3):
+                    at = pl.multiple_of(section * D + (1 - core) * 512, 512)
+                    d_hops.append(
+                        across(9 + section, dn.at[:, pl.ds(at, 512)], d_side.at[:, section * 512 : section * 512 + 512])
+                    )
+                    d_hops[section].start()
         for u in range(6):
             section, half = u // 2, u % 2
             if half == 0:

time: 169 us -> 169 us (level)
  no operation moved by 1% of the time
where the time goes in v8:
time: 169 us; the launch traced here: 168 us
  Pallas kernels  167 us (99%)
    pallas_call x1, Pallas kernels, block_call(): pl.pallas_call(block_kernel, name='block', out_shape=(jax.ShapeDtypeStruc...  165 us

profile of v8, /device:TPU:1, one launch (start us, length us, event | category | flops | bytes accessed | tf_op | source)
XLA Modules:
  0.0 168.1 jit_solution(14306906279765758708)
XLA Ops:
  0.6 164.9 %block.1 = (bf16[1,192,1024]{2,1,0:T(8,128)(2,1)}, bf16[1,192,1024]{2,1,0:T(8,128)(2,1)}, f32[8,3072]{1,0:T(8,128)}, f32[8,128]{1,0:T(8,128)}, f32[8,4096]{1,0:T...) custom-call(bf16[1,192,1024]{2,1,0:T(8,128)(2,1)} %x_ref.1, s32[1,192]{1,0:T(1,128)} %seg_ref.1, ...), custom_call_target="tpu_custom_call" | custom-call | tf_op jit(solution)/shard_map/block/pallas_call | solution.py:1240
  165.5 2.3 %deliver.1 = (bf16[1,192,1024]{2,1,0:T(8,128)(2,1)}, bf16[1,192,1024]{2,1,0:T(8,128)(2,1)}, f32[8,3072]{1,0:T(8,128)}, f32[8,1024]{1,0:T(8,128)}, f32[8,4096]{1,...) custom-call(bf16[1,192,1024]{2,1,0:T(8,128)(2,1)} %get-tuple-element.23.refs_0_, ...), custom_call_target="tpu_custom_call" | custom-call | tf_op jit(solution)/shard_map/deliver/pallas_call | solution.py:1318
